TPU v7x, 128 devices: a whole 4x4x4 slice. The times are simulated.
128 devices in a mesh: gx: 16 (over x, y), gy: 8 (over z, core).
Axes of the slice: x: 4, y: 4, z: 4, core: 2. Of those that a mesh axis runs over, the one named last changes fastest.
Arguments:
- fine_nodes: bfloat16 [64, 16, 128, 512], P('gx', 'gy'), may hold values from -6 to 6
- edge_states: bfloat16 [16, 8, 64, 128, 512], P('gx', 'gy'), may hold values from -6 to 6
- middle_nodes: bfloat16 [16, 8, 128, 512], P('gx', 'gy'), may hold values from -6 to 6
- coarse_nodes: bfloat16 [1024, 512], P(('gx', 'gy')), may hold values from -6 to 6
- edge_sources: int32 [16, 8, 64, 128], P('gx', 'gy'), may hold values from 0 to 3071, as said below
- target_blocks: int32 [16, 8, 64], P('gx', 'gy'), may hold values from 0 to 7
- target_nodes: int32 [16, 8, 64, 128], P('gx', 'gy'), may hold values from 0 to 127
- live_blocks: int32 [16, 8], P('gx', 'gy'), may hold values from 32 to 64, as said below
- fine_parent: int32 [64, 16, 128], P('gx', 'gy'), may hold values from 0 to 127
- fine_weight: float32 [64, 16, 128], P('gx', 'gy'), may hold values from 0.2 to 0.6
- middle_parent: int32 [16, 8, 128], P('gx', 'gy'), may hold values from 0 to 1023, as said below
- middle_weight: float32 [16, 8, 128], P('gx', 'gy'), may hold values from 0.1 to 0.3
- edge_in: bfloat16 [3, 512, 512], replicated, may hold values from -0.15625 to 0.15625
- edge_bias: float32 [512], replicated, may hold values from -3 to 3
- edge_out: bfloat16 [512, 512], replicated, may hold values from -0.25 to 0.25
- edge_bias_two: float32 [512], replicated, may hold values from -3 to 3
- edge_gain: float32 [512], replicated, may hold values from 0.1 to 1.9
- node_in: bfloat16 [2, 512, 512], replicated, may hold values from -0.1875 to 0.1875
- node_bias: float32 [512], replicated, may hold values from -3 to 3
- node_out: bfloat16 [512, 512], replicated, may hold values from -0.25 to 0.25
- node_bias_two: float32 [512], replicated, may hold values from -3 to 3
- node_gain: float32 [512], replicated, may hold values from 0.1 to 1.9
- coarse_in: bfloat16 [2, 512, 512], replicated, may hold values from -0.1875 to 0.1875
- coarse_bias: float32 [512], replicated, may hold values from -3 to 3
- coarse_out: bfloat16 [512, 512], replicated, may hold values from -0.25 to 0.25
- coarse_bias_two: float32 [512], replicated, may hold values from -3 to 3
- coarse_gain: float32 [512], replicated, may hold values from 0.1 to 1.9
Outputs:
- fine_result: bfloat16 [64, 16, 128, 512], P('gx', 'gy')
- edge_result: bfloat16 [16, 8, 64, 128, 512], P('gx', 'gy')
- middle_result: bfloat16 [16, 8, 128, 512], P('gx', 'gy')
- coarse_result: bfloat16 [1024, 512], P(('gx', 'gy'))
Inputs may be any that keep to these rules, and one draw needn't show every extreme that they name: `edge_sources`: sources lie in the device's own blocks or in the blocks touching them (diagonals too), never outside the grid. `live_blocks`: some device has all 64 slots live in every draw. `middle_parent`: coarse node c is owned by device c // 8 in the order of gx+gy. Of the 128 middle nodes of one device, exactly 1 have their parent among the coarse nodes of each owner.
All inputs are finite; a program needn't handle non-finite values.
Results may differ from a plain program's by a relative error of at most 0.0075.
Values may be sent and summed in bfloat16 or wider, within the bound.
No kernel may reach another device: no remote copies, remote signals or barrier semaphores. Data moves between devices by JAX's collectives and lax.ppermute only.
A program may use at most 192 MiB of HBM per device.

v0:
```python
import jax
import jax.numpy as jnp
from jax import lax
from jax.sharding import PartitionSpec as P

epsilon = 1e-05


def extended(array, sides, width):
    for axis, dim in sides:
        count, length = (lax.axis_size(axis), array.shape[dim])
        up = [(i, (i + 1) % count) for i in range(count - 1)]
        down = [(j, i) for i, j in up]
        last = lax.slice_in_dim(array, length - width, length, axis=dim)
        first = lax.slice_in_dim(array, 0, width, axis=dim)
        before = lax.ppermute(last, axis, up)
        after = lax.ppermute(first, axis, down)
        array = jnp.concatenate([before, array, after], axis=dim)
    return array


def layer_norm(values, gain_vec):
    centred = values - jnp.mean(values, axis=-1, keepdims=True)
    spread = jnp.mean(centred * centred, axis=-1, keepdims=True)
    return centred * lax.rsqrt(spread + epsilon) * gain_vec


def two_layer(pre_act, bias_one, second_weight, bias_two, gain_vec):
    hidden = jax.nn.silu(pre_act + bias_one).astype(jnp.bfloat16)
    output = jnp.dot(hidden, second_weight, preferred_element_type=jnp.float32) + bias_two
    return layer_norm(output, gain_vec)


def edge_messages(edge_rows, sources, targets, active_block_mask, padded, own_rows, edge_params):
    first_w, bias_one, second_weight, bias_two, gain_vec = edge_params
    latent = edge_rows.shape[-1]
    flat_edges = edge_rows.reshape(-1, latent)
    from_source = jnp.take(padded, sources.reshape(-1), axis=0)
    from_target = jnp.take(own_rows, targets.reshape(-1), axis=0)
    pre_act = jnp.dot(flat_edges, first_w[0], preferred_element_type=jnp.float32)
    pre_act = pre_act + jnp.dot(from_source, first_w[1], preferred_element_type=jnp.float32)
    pre_act = pre_act + jnp.dot(from_target, first_w[2], preferred_element_type=jnp.float32)
    message = two_layer(pre_act, bias_one, second_weight, bias_two, gain_vec).astype(jnp.bfloat16)
    keep_rows = active_block_mask.reshape(-1, 1)
    message = jnp.where(keep_rows, message, jnp.zeros_like(message))
    edge_latent_updated = jnp.where(
        keep_rows,
        (flat_edges.astype(jnp.float32) + message.astype(jnp.float32)).astype(jnp.bfloat16),
        flat_edges,
    )
    return (message.reshape(edge_rows.shape), edge_latent_updated.reshape(edge_rows.shape))


def body(
    fine_nodes,
    edge_states,
    middle_nodes,
    coarse_nodes,
    edge_sources,
    target_blocks,
    target_nodes,
    live_blocks,
    fine_parent,
    fine_weight,
    middle_parent,
    middle_weight,
    edge_in,
    edge_bias,
    edge_out,
    edge_bias_two,
    edge_gain,
    node_in,
    node_bias,
    node_out,
    node_bias_two,
    node_gain,
    coarse_in,
    coarse_bias,
    coarse_out,
    coarse_bias_two,
    coarse_gain,
):
    rows_x, rows_y, block_size, latent = fine_nodes.shape
    own_count = rows_x * rows_y * block_size
    own_rows = fine_nodes.reshape(own_count, latent)
    padded = extended(fine_nodes, (("gx", 0), ("gy", 1)), 1).reshape(-1, latent)
    edge_rows = edge_states[0, 0]
    edge_blocks = edge_rows.shape[0]
    sources = edge_sources[0, 0]
    block_target = target_blocks[0, 0]
    node_target = target_nodes[0, 0]
    targets = block_target[:, None] * block_size + node_target
    live_count = live_blocks[0, 0]
    block_alive = lax.iota(jnp.int32, edge_blocks) < live_count
    active_block_mask = jnp.broadcast_to(block_alive[:, None], (edge_blocks, block_size))
    edge_params = (edge_in, edge_bias, edge_out, edge_bias_two, edge_gain)
    edge_message_rows, edge_latent_updated = edge_messages(
        edge_rows, sources, targets, active_block_mask, padded, own_rows, edge_params
    )
    target_indicator = (
        node_target[:, None, :] == lax.iota(jnp.int32, block_size)[None, :, None]
    ).astype(jnp.bfloat16)
    per_block = jnp.einsum(
        "uot,utx->uox", target_indicator, edge_message_rows, preferred_element_type=jnp.float32
    )
    block_select = (lax.iota(jnp.int32, rows_x * rows_y)[:, None] == block_target[None, :]).astype(
        jnp.float32
    )
    block_sums = jnp.dot(
        block_select,
        per_block.reshape(edge_blocks, block_size * latent),
        precision=lax.Precision.HIGHEST,
        preferred_element_type=jnp.float32,
    )
    aggregate = block_sums.reshape(own_count, latent).astype(jnp.bfloat16)
    node_pre = jnp.dot(own_rows, node_in[0], preferred_element_type=jnp.float32)
    node_pre = node_pre + jnp.dot(aggregate, node_in[1], preferred_element_type=jnp.float32)
    fine_mid = own_rows.astype(jnp.float32) + two_layer(
        node_pre, node_bias, node_out, node_bias_two, node_gain
    )
    parents_local = fine_parent.reshape(own_count)
    weights_local = fine_weight.reshape(own_count)
    middle_rows = middle_nodes[0, 0]
    middle_count = middle_rows.shape[0]
    restrict = (lax.iota(jnp.int32, middle_count)[:, None] == parents_local[None, :]).astype(
        jnp.float32
    ) * weights_local[None, :]
    restricted_mid = jnp.dot(
        restrict,
        own_rows.astype(jnp.float32),
        precision=lax.Precision.HIGHEST,
        preferred_element_type=jnp.float32,
    )
    middle_mid = (middle_rows.astype(jnp.float32) + restricted_mid).astype(jnp.bfloat16)
    mid_parents = middle_parent[0, 0]
    mid_weights = middle_weight[0, 0]
    middle_wide = middle_mid.astype(jnp.float32)
    coarse_own = coarse_nodes.shape[0]
    coarse_ids = lax.iota(jnp.int32, lax.axis_size(("gx", "gy")) * coarse_own)
    select = (coarse_ids[:, None] == mid_parents[None, :]).astype(jnp.float32) * mid_weights[
        None, :
    ]
    summed = lax.psum_scatter(
        jnp.dot(
            select, middle_wide, precision=lax.Precision.HIGHEST, preferred_element_type=jnp.float32
        ),
        ("gx", "gy"),
        scatter_dimension=0,
        tiled=True,
    )
    coarse_summed = summed.astype(jnp.bfloat16)
    coarse_pre = jnp.dot(coarse_nodes, coarse_in[0], preferred_element_type=jnp.float32)
    coarse_pre = coarse_pre + jnp.dot(
        coarse_summed, coarse_in[1], preferred_element_type=jnp.float32
    )
    coarse_result = (
        coarse_nodes.astype(jnp.float32)
        + two_layer(coarse_pre, coarse_bias, coarse_out, coarse_bias_two, coarse_gain)
    ).astype(jnp.bfloat16)
    everyone = lax.all_gather(coarse_result, ("gx", "gy"), axis=0, tiled=True)
    from_coarse = jnp.take(everyone, mid_parents, axis=0).astype(jnp.float32)
    middle_result = (middle_wide + mid_weights[:, None] * from_coarse).astype(jnp.bfloat16)
    from_middle = jnp.take(middle_result, parents_local, axis=0).astype(jnp.float32)
    fine_result = (fine_mid + weights_local[:, None] * from_middle).astype(jnp.bfloat16)
    return (
        fine_result.reshape(fine_nodes.shape),
        edge_latent_updated.reshape(edge_states.shape),
        middle_result.reshape(middle_nodes.shape),
        coarse_result,
    )


def solution(mesh):
    placed = (
        P("gx", "gy", None, None),
        P("gx", "gy", None, None, None),
        P("gx", "gy", None, None),
        P(("gx", "gy"), None),
        P("gx", "gy", None, None),
        P("gx", "gy", None),
        P("gx", "gy", None, None),
        P("gx", "gy"),
        P("gx", "gy", None),
        P("gx", "gy", None),
        P("gx", "gy", None),
        P("gx", "gy", None),
        P(),
        P(),
        P(),
        P(),
        P(),
        P(),
        P(),
        P(),
        P(),
        P(),
        P(),
        P(),
        P(),
        P(),
        P(),
    )
    return jax.shard_map(
        body,
        mesh=mesh,
        in_specs=placed,
        out_specs=(
            P("gx", "gy", None, None),
            P("gx", "gy", None, None, None),
            P("gx", "gy", None, None),
            P(("gx", "gy"), None),
        ),
        check_vma=False,
    )
```

profile of v0, /device:TPU:1, one launch (start us, length us, event | category | flops | bytes accessed | tf_op | source)
XLA Modules:
  0.0 741.2 jit_solution(18050050498206750060)
XLA Ops:
  7.2 1.8 fusion.70
  9.1 4.8 collective-permute-start
  13.8 1.3 collective-permute-start.1
  15.1 1.9 fusion.16
  17.0 3.1 fusion.33
  20.1 1.3 compare_and_fusion.2
  27.4 13.8 %fusion.28 = f32[8192,512]{1,0:T(8,128)} fusion(bf16[8192,512]{1,0:T(8,128)(2,1)} %bitcast.103, bf16[3,512,512]{2,1,0:T(8,128)(2,1)} %param.39), kind=kOutput, calls=%fused_computation.42 | convolution fusion | flops 4294967296 | bytes 25690112 | tf_op jit(solution)/shard_map/dot_general | solution.py:40
  42.9 1.3 fusion.69
  44.2 4.4 collective-permute-start.2
  48.6 2.1 collective-permute-start.3
  51.3 33.7 %gather_fusion.1 = bf16[8192,512]{1,0:T(8,128)(2,1)} fusion(bf16[1024,512]{1,0:T(8,128)(2,1)S(1)} %bitcast.96, s32[8192]{0:T(1024)S(1)} %broadcast_clamp_fusion), kind=kCustom, calls=%fused_computation.1 | custom fusion | bytes 16809984 | tf_op jit(solution)/shard_map/jit(_take)/gather | solution.py:39
  85.0 1.2 fusion.21
  86.2 3.1 fusion.30
  89.3 3.4 pad_maximum_fusion
  92.6 36.4 %gather_fusion = bf16[8192,512]{1,0:T(8,128)(2,1)} fusion(bf16[3072,512]{1,0:T(8,128)(2,1)} %bitcast.98, s32[8192]{0:T(1024)S(1)} %broadcast_clamp_fusion.1), kind=kCustom, calls=%fused_computation | custom fusion | bytes 16809984 | tf_op jit(solution)/shard_map/jit(_take)/gather | solution.py:38
  129.0 10.4 %fusion.3 = f32[8192,512]{1,0:T(8,128)} fusion(bf16[8192,512]{1,0:T(8,128)(2,1)} %gather_fusion, pred[8192]{0:T(1024)(128)(4,1)S(1)} %compare_and_fusion.1, bf16[3,512,512]{2,1,0:T(8,128)(2,1)S(1)} %copy-done.10), kind=kOutput, calls=%fused_computation.13 | convolution fusion | flops 4299161600 | bytes 25698304 | tf_op jit(solution)/shard_map/dot_general | solution.py:41
  139.4 22.2 %add_reduce_fusion = (f32[8192]{0:T(1024)S(1)}, f32[8192,512]{1,0:T(8,128)}) fusion(f32[512]{0:T(512)S(1)} %copy-done.13, bf16[512,512]{1,0:T(8,128)(2,1)S(1)} %copy-done, f32[8192,512]{1,0:T(8,128)} %fusion.28, f32[8192,512]{1,0:T(8,128)} %fusion.3, f32[512]{0:T(512)S(1)} %copy-done.27, bf16[8192,512]{1,0:T(8,128)(2,1)} %gather_fusion.1, ...), kind=kOutput, calls=%fused_computation.9 | convolution fusion | flops 8636063744 | bytes 59813888 | tf_op jit(solution)/shard_map/dot_general | solution.py:30
  161.6 9.2 %multiply_reduce_fusion = f32[8192]{0:T(1024)S(1)} fusion(f32[8192,512]{1,0:T(8,128)} %get-tuple-element.11, f32[8192]{0:T(1024)S(1)} %broadcast_multiply_fusion, f32[512]{0:T(512)S(1)} %copy-done.13), kind=kLoop, calls=%fused_computation.7 | loop fusion | flops 16769024 | bytes 16844800 | tf_op jit(solution)/shard_map/reduce_sum | solution.py:24
  170.9 1.5 copy-done.4
  172.4 10.6 %fusion = (bf16[8192,512]{1,0:T(8,128)(2,1)}, bf16[8192,512]{1,0:T(8,128)(2,1)}) fusion(pred[8192]{0:T(1024)(128)(4,1)S(1)} %broadcast_bitcast_fusion, bf16[1,1,64,128,512]{4,3,2,1,0:T(8,128)(2,1)} %param.28, f32[512]{0:T(512)S(1)} %copy-done.17, f32[8192]{0:T(1024)S(1)} %add_rsqrt_fusion, f32[8192]{0:T(1024)S(1)} %broadcast_multiply_fusion, ...), kind=kLoop, calls=%fused_computation.10 | loop fusion | flops 46137344 | bytes 42020864 | tf_op jit(solution)/shard_map/jit(_where)/select_n | solution.py:46
  183.0 473.5 %reduce-scatter.2.cloned.1.call-done = f32[8,512]{1,0:T(8,128)} async-done(((f32[1024,512]{1,0:T(8,128)}), f32[8,512]{1,0:T(8,128)}) %reduce-scatter.2.cloned.1.call-update) | async-done | bytes 16400 | tf_op jit(solution)/shard_map/reduce_scatter | solution.py:143
  656.5 1.2 fusion.75
  658.6 5.7 fusion.13
  664.3 12.0 %copy.31 = f32[8,8,128,512]{3,1,2,0:T(8,128)} copy(f32[8,8,128,512]{3,2,1,0:T(8,128)S(1)} %bitcast.100) | data formatting | bytes 33554432
  676.3 9.0 %convolution_convert_fusion = bf16[8,65536]{1,0:T(8,128)(2,1)S(1)} fusion(f32[64,65536]{1,0:T(8,128)} %bitcast.101, s32[64]{0:T(128)S(1)} %bitcast.120), kind=kOutput, calls=%fused_computation.4 | convolution fusion | flops 403177984 | bytes 17826048 | tf_op jit(solution)/shard_map/dot_general | solution.py:109
  685.4 1.4 convert_element_type.72
  686.9 4.9 add_reduce_fusion.1
  691.8 2.1 multiply_reduce_fusion.1
  693.9 30.8 %all-gather.2.cloned.1.call-done = bf16[1024,512]{1,0:T(8,128)(2,1)} async-done(((bf16[8,512]{1,0:T(8,128)(2,1)}), bf16[1024,512]{1,0:T(8,128)(2,1)}) %all-gather.2.cloned.1.call-update) | async-done | bytes 1048592 | tf_op jit(solution)/shard_map/all_gather | solution.py:160
  724.7 2.4 gather_fusion.2
  727.3 4.0 gather_fusion.3
  731.3 3.1 add_convert_fusion.1
  (92 shorter events, 8.9 us)
Async XLA Ops:
  7.2 132.2 %copy-start = (bf16[512,512]{1,0:T(8,128)(2,1)S(1)}, bf16[512,512]{1,0:T(8,128)(2,1)}, u32[]{:S(2)}) copy-start(bf16[512,512]{1,0:T(8,128)(2,1)} %param.41) | copy-start | bytes 1572868
  7.2 649.3 %reduce-scatter.2.cloned.1.call-start = ((), (), s32[]{:S(2)}) async-start(), calls=%async_computation.1 | async-start | bytes 2113536 | tf_op jit(solution)/shard_map/reduce_scatter | solution.py:143
  9.1 32.7 %collective-permute-start = (bf16[1,2,128,512]{3,2,1,0:T(8,128)(2,1)S(1)}, bf16[1,2,128,512]{3,2,1,0:T(8,128)(2,1)}, u32[]{:S(2)}, u32[]{:S(2)}) collective-permute-start(bf16[1,2,128,512]{3,2,1,0:T(8,128)(2,1)S(1)} %get-tuple-element.9), channel_id=1, source_target_pairs={{0,8},{8,16},{16,24},{24,32},{32,40},{40,48},{48,56},{56,64},{64,7... | collective-permute-start | bytes 786440 | tf_op jit(solution)/shard_map/ppermute | solution.py:16
  13.8 29.0 %collective-permute-start.1 = (bf16[1,2,128,512]{3,2,1,0:T(8,128)(2,1)}, bf16[1,2,128,512]{3,2,1,0:T(8,128)(2,1)S(1)}, u32[]{:S(2)}, u32[]{:S(2)}) collective-permute-start(bf16[1,2,128,512]{3,2,1,0:T(8,128)(2,1)} %get-tuple-element.8), channel_id=1, source_target_pairs={{8,0},{16,8},{24,16},{32,24},{40,32},{48,40},{56,48},{64,56},{72,6... | collective-permute-start | bytes 786440 | tf_op jit(solution)/shard_map/ppermute | solution.py:17
  17.0 10.4 %copy-start.6 = (bf16[128,512]{1,0:T(8,128)(2,1)}, bf16[128,512]{1,0:T(8,128)(2,1)S(1)}, u32[]{:S(2)}) copy-start(bf16[128,512]{1,0:T(8,128)(2,1)S(1)} %fusion.16) | copy-start | bytes 393220
  20.1 704.7 %all-gather.2.cloned.1.call-start = ((), (), s32[]{:S(2)}) async-start(), calls=%async_computation.2 | async-start | bytes 1056768 | tf_op jit(solution)/shard_map/all_gather | solution.py:160
  27.4 13.8 %copy-start.25 = (s32[1,1,128]{2,1,0:T(1,128)S(1)}, s32[1,1,128]{2,1,0:T(1,128)}, u32[]{:S(2)}) copy-start(s32[1,1,128]{2,1,0:T(1,128)} %param.37) | copy-start | bytes 1540
  27.4 15.3 %copy-start.2 = (bf16[4,2,128,512]{3,2,1,0:T(8,128)(2,1)S(1)}, bf16[4,2,128,512]{3,2,1,0:T(8,128)(2,1)}, u32[]{:S(2)}) copy-start(bf16[4,2,128,512]{3,2,1,0:T(8,128)(2,1)} %param.27) | copy-start | bytes 3145732
  44.2 45.1 %collective-permute-start.2 = (bf16[6,1,128,512]{3,2,1,0:T(8,128)(2,1)}, bf16[6,1,128,512]{3,2,1,0:T(8,128)(2,1)}, u32[]{:S(2)}, u32[]{:S(2)}) collective-permute-start(bf16[6,1,128,512]{3,2,1,0:T(8,128)(2,1)} %get-tuple-element.6), channel_id=1, source_target_pairs={{0,1},{1,2},{2,3},{3,4},{4,5},{5,6},{6,7},{8,9},{9,10},{10,11},{11... | collective-permute-start | bytes 2359304 | tf_op jit(solution)/shard_map/ppermute | solution.py:16
  48.6 40.7 %collective-permute-start.3 = (bf16[6,1,128,512]{3,2,1,0:T(8,128)(2,1)}, bf16[6,1,128,512]{3,2,1,0:T(8,128)(2,1)}, u32[]{:S(2)}, u32[]{:S(2)}) collective-permute-start(bf16[6,1,128,512]{3,2,1,0:T(8,128)(2,1)} %get-tuple-element.7), channel_id=1, source_target_pairs={{1,0},{2,1},{3,2},{4,3},{5,4},{6,5},{7,6},{9,8},{10,9},{11,10},{12... | collective-permute-start | bytes 2359304 | tf_op jit(solution)/shard_map/ppermute | solution.py:17
  51.3 33.7 %copy-start.11 = (bf16[8,512]{1,0:T(8,128)(2,1)S(1)}, bf16[8,512]{1,0:T(8,128)(2,1)}, u32[]{:S(2)}) copy-start(bf16[8,512]{1,0:T(8,128)(2,1)} %param.30) | copy-start | bytes 24580
  92.6 36.4 %copy-start.10 = (bf16[3,512,512]{2,1,0:T(8,128)(2,1)S(1)}, bf16[3,512,512]{2,1,0:T(8,128)(2,1)}, u32[]{:S(2)}) copy-start(bf16[3,512,512]{2,1,0:T(8,128)(2,1)} %param.39) | copy-start | bytes 4718596
  161.6 10.7 %copy-start.4 = (f32[8192,512]{1,0:T(8,128)S(1)}, f32[8192,512]{1,0:T(8,128)}, u32[]{:S(2)}) copy-start(f32[8192,512]{1,0:T(8,128)} %get-tuple-element.11) | copy-start | bytes 50331652
  161.6 10.7 %copy-start.17 = (f32[512]{0:T(512)S(1)}, f32[512]{0:T(512)}, u32[]{:S(2)}) copy-start(f32[512]{0:T(512)} %param.43) | copy-start | bytes 6148
  172.3 484.2 %copy-start.5 = (bf16[2,512,512]{2,1,0:T(8,128)(2,1)S(1)}, bf16[2,512,512]{2,1,0:T(8,128)(2,1)}, u32[]{:S(2)}) copy-start(bf16[2,512,512]{2,1,0:T(8,128)(2,1)} %param.49) | copy-start | bytes 3145732
  172.3 484.2 %copy-start.8 = (bf16[512,512]{1,0:T(8,128)(2,1)S(1)}, bf16[512,512]{1,0:T(8,128)(2,1)}, u32[]{:S(2)}) copy-start(bf16[512,512]{1,0:T(8,128)(2,1)} %param.51) | copy-start | bytes 1572868
  172.4 484.2 %copy-start.18 = (f32[512]{0:T(512)S(1)}, f32[512]{0:T(512)}, u32[]{:S(2)}) copy-start(f32[512]{0:T(512)} %param.52) | copy-start | bytes 6148
  172.4 484.2 %copy-start.19 = (f32[512]{0:T(512)S(1)}, f32[512]{0:T(512)}, u32[]{:S(2)}) copy-start(f32[512]{0:T(512)} %param.50) | copy-start | bytes 6148
  172.4 485.5 %copy-start.21 = (f32[512]{0:T(512)S(1)}, f32[512]{0:T(512)}, u32[]{:S(2)}) copy-start(f32[512]{0:T(512)} %param.53) | copy-start | bytes 6148
  172.4 486.2 %copy-start.9 = (s32[1,1,64,128]{3,2,1,0:T(8,128)S(1)}, s32[1,1,64,128]{3,2,1,0:T(8,128)}, u32[]{:S(2)}) copy-start(s32[1,1,64,128]{3,2,1,0:T(8,128)} %param.33) | copy-start | bytes 98308
  664.3 12.0 %copy-start.23 = (s32[1,1,64]{2,1,0:T(1,128)S(1)}, s32[1,1,64]{2,1,0:T(1,128)}, u32[]{:S(2)}) copy-start(s32[1,1,64]{2,1,0:T(1,128)} %param.32) | copy-start | bytes 772
  676.3 10.5 %copy-start.14 = (f32[512]{0:T(512)S(1)}, f32[512]{0:T(512)}, u32[]{:S(2)}) copy-start(f32[512]{0:T(512)} %param.47) | copy-start | bytes 6148
  676.3 10.5 %copy-start.26 = (bf16[512,512]{1,0:T(8,128)(2,1)S(1)}, bf16[512,512]{1,0:T(8,128)(2,1)}, u32[]{:S(2)}) copy-start(bf16[512,512]{1,0:T(8,128)(2,1)} %param.46) | copy-start | bytes 1572868
  676.3 10.5 %copy-start.28 = (f32[512]{0:T(512)S(1)}, f32[512]{0:T(512)}, u32[]{:S(2)}) copy-start(f32[512]{0:T(512)} %param.45) | copy-start | bytes 6148
  686.8 40.3 %copy-start.7 = (bf16[128,512]{1,0:T(8,128)(2,1)S(1)}, bf16[128,512]{1,0:T(8,128)(2,1)}, u32[]{:S(2)}) copy-start(bf16[128,512]{1,0:T(8,128)(2,1)} %copy-done.6) | copy-start | bytes 393220
  686.8 40.3 %copy-start.22 = (f32[1,1,128]{2,1,0:T(1,128)S(1)}, f32[1,1,128]{2,1,0:T(1,128)}, u32[]{:S(2)}) copy-start(f32[1,1,128]{2,1,0:T(1,128)} %param.38) | copy-start | bytes 1540
  686.8 40.3 %copy-start.24 = (pred[128]{0:T(512)(128)(4,1)S(1)}, pred[128]{0:T(512)(128)(4,1)}, u32[]{:S(2)}) copy-start(pred[128]{0:T(512)(128)(4,1)} %compare_and_fusion.3) | copy-start | bytes 388
  686.8 40.4 %copy-start.12 = (s32[1024]{0:T(1024)S(1)}, s32[1024]{0:T(1024)}, u32[]{:S(2)}) copy-start(s32[1024]{0:T(1024)} %broadcast_clamp_fusion.2) | copy-start | bytes 12292
  691.8 39.5 %copy-start.15 = (f32[4,2,128]{2,1,0:T(2,128)S(1)}, f32[4,2,128]{2,1,0:T(2,128)}, u32[]{:S(2)}) copy-start(f32[4,2,128]{2,1,0:T(2,128)} %param.36) | copy-start | bytes 12292
  691.8 39.5 %copy-start.16 = (pred[1024]{0:T(1024)(128)(4,1)S(1)}, pred[1024]{0:T(1024)(128)(4,1)}, u32[]{:S(2)}) copy-start(pred[1024]{0:T(1024)(128)(4,1)} %compare_and_fusion.2) | copy-start | bytes 3076
  691.8 39.5 %copy-start.20 = (f32[512]{0:T(512)S(1)}, f32[512]{0:T(512)}, u32[]{:S(2)}) copy-start(f32[512]{0:T(512)} %param.48) | copy-start | bytes 6148
  691.8 42.5 %copy-start.1 = (bf16[512,512]{1,0:T(8,128)(2,1)S(1)}, bf16[512,512]{1,0:T(8,128)(2,1)}, u32[]{:S(2)}) copy-start(bf16[512,512]{1,0:T(8,128)(2,1)} %param.41) | copy-start | bytes 1572868
  (3 other events, 27.8 us)
Sparse Core Ops, SparseCore 0:
  20.2 636.2 reduce-scatter.1
  660.3 64.4 all-gather.1
where the time goes:
time: 742 us; the launch traced here: 741 us
  waiting for transfers between devices  504 us (68%)
  local copies, waits for them, and re-layouts  95.7 us (13%)
  matrix products  76.4 us (10%)
  other arithmetic  37 us (5%)
  between operations  15.1 us (2%)
  starting transfers between devices  12.6 us (2%)
    reduce_scatter x1, waiting for transfers between devices, body(): lax.psum_scatter(jnp.dot(select, middle_wide, precision=lax.Precision.HIG...  473 us
    gather x1, local copies, waits for them, and re-layouts, edge_messages(): from_source = jnp.take(padded, sources.reshape(-1), axis=0)  36.4 us
    gather x1, local copies, waits for them, and re-layouts, edge_messages(): from_target = jnp.take(own_rows, targets.reshape(-1), axis=0)  33.7 us
    all_gather x1, waiting for transfers between devices, body(): everyone = lax.all_gather(coarse_result, ('gx', 'gy'), axis=0, tiled=True)  30.8 us
    dot_general x3, matrix products, two_layer(): jnp.dot(hidden, second_weight, preferred_element_type=jnp.float32)  28.3 us
  transfers between devices with their start and end apart: 6, of which 2 were waited for; matrix products, arithmetic and copies ran while one was open for 26% of the time, Pallas kernels for 0%

commit v1 on v0

--- a/solution.py
+++ b/solution.py
@@ -136,19 +136,33 @@
     mid_weights = middle_weight[0, 0]
     middle_wide = middle_mid.astype(jnp.float32)
     coarse_own = coarse_nodes.shape[0]
-    coarse_ids = lax.iota(jnp.int32, lax.axis_size(("gx", "gy")) * coarse_own)
-    select = (coarse_ids[:, None] == mid_parents[None, :]).astype(jnp.float32) * mid_weights[
-        None, :
-    ]
-    summed = lax.psum_scatter(
-        jnp.dot(
-            select, middle_wide, precision=lax.Precision.HIGHEST, preferred_element_type=jnp.float32
-        ),
-        ("gx", "gy"),
-        scatter_dimension=0,
-        tiled=True,
-    )
-    coarse_summed = summed.astype(jnp.bfloat16)
+    devices = lax.axis_size(("gx", "gy"))
+    owner = mid_parents // coarse_own
+    place = mid_parents % coarse_own
+    to_owner = lax.iota(jnp.int32, devices)[:, None] == owner[None, :]
+    weight_top = lax.reduce_precision(mid_weights, 8, 7)
+    weight_middle = lax.reduce_precision(mid_weights - weight_top, 8, 7)
+    weight_low = mid_weights - weight_top - weight_middle
+    notes = jnp.stack(
+        [weight_top, weight_middle, weight_low, place.astype(jnp.float32)], axis=1
+    ).astype(jnp.bfloat16)
+    notes = jnp.pad(notes, ((0, 0), (0, 124)))
+    rows_out = jnp.dot(
+        to_owner.astype(jnp.bfloat16),
+        jnp.concatenate([middle_mid, notes], axis=1),
+        preferred_element_type=jnp.float32,
+    ).astype(jnp.bfloat16)
+    rows_in = lax.all_to_all(rows_out, ("gx", "gy"), 0, 0, tiled=True)
+    notes_in = rows_in[:, latent : latent + 4].astype(jnp.float32)
+    weight_in = notes_in[:, 0] + notes_in[:, 1] + notes_in[:, 2]
+    place_in = notes_in[:, 3].astype(jnp.int32)
+    at_place = lax.iota(jnp.int32, coarse_own)[:, None] == place_in[None, :]
+    coarse_summed = jnp.dot(
+        at_place.astype(jnp.float32) * weight_in[None, :],
+        rows_in[:, :latent].astype(jnp.float32),
+        precision=lax.Precision.HIGHEST,
+        preferred_element_type=jnp.float32,
+    ).astype(jnp.bfloat16)
     coarse_pre = jnp.dot(coarse_nodes, coarse_in[0], preferred_element_type=jnp.float32)
     coarse_pre = coarse_pre + jnp.dot(
         coarse_summed, coarse_in[1], preferred_element_type=jnp.float32
@@ -157,8 +171,13 @@
         coarse_nodes.astype(jnp.float32)
         + two_layer(coarse_pre, coarse_bias, coarse_out, coarse_bias_two, coarse_gain)
     ).astype(jnp.bfloat16)
-    everyone = lax.all_gather(coarse_result, ("gx", "gy"), axis=0, tiled=True)
-    from_coarse = jnp.take(everyone, mid_parents, axis=0).astype(jnp.float32)
+    answers = jnp.dot(
+        at_place.T.astype(jnp.bfloat16), coarse_result, preferred_element_type=jnp.float32
+    ).astype(jnp.bfloat16)
+    from_owners = lax.all_to_all(answers, ("gx", "gy"), 0, 0, tiled=True)
+    from_coarse = jnp.dot(
+        to_owner.T.astype(jnp.bfloat16), from_owners, preferred_element_type=jnp.float32
+    )
     middle_result = (middle_wide + mid_weights[:, None] * from_coarse).astype(jnp.bfloat16)
     from_middle = jnp.take(middle_result, parents_local, axis=0).astype(jnp.float32)
     fine_result = (fine_mid + weights_local[:, None] * from_middle).astype(jnp.bfloat16)

time: 742 us -> 259 us (0.35)
  waiting for transfers between devices: 504 us -> 9.05 us
  starting transfers between devices: 12.6 us -> 32.6 us
  between operations: 15.1 us -> 1.73 us
    reduce_scatter x1 -> x0, waiting for transfers between devices: 473 us -> none  [body(): lax.psum_scatter(jnp.dot(select, middle_wide, precision=lax.Precision.HIG...]
    all_gather x1 -> x0, waiting for transfers between devices: 30.8 us -> none  [body(): everyone = lax.all_gather(coarse_result, ('gx', 'gy'), axis=0, tiled=True)]
    all_to_all x0 -> x2, starting transfers between devices: none -> 21.7 us  [the longest x1 11.5 us: body(): rows_in = lax.all_to_all(rows_out, ('gx', 'gy'), 0, 0, tiled=True)]
    all_to_all x0 -> x2, waiting for transfers between devices: none -> 9.04 us  [the longest x1 9.04 us: body(): from_owners = lax.all_to_all(answers, ('gx', 'gy'), 0, 0, tiled=True)]
    unnamed x61 -> x64, local copies, waits for them, and re-layouts: 14.6 us -> 17.8 us
  transfers between devices with their start and end apart: 6 -> 6, of which waited for: 2 -> 1; matrix products, arithmetic and copies ran while one was open for 26% -> 29% of each run, Pallas kernels for 0% -> 0%
where the time goes in v1:
time: 259 us; the launch traced here: 258 us
  local copies, waits for them, and re-layouts  98.6 us (38%)
  matrix products  74.9 us (29%)
  other arithmetic  40.6 us (16%)
  starting transfers between devices  32.6 us (13%)
  waiting for transfers between devices  9.05 us (3%)
    gather x1, local copies, waits for them, and re-layouts, edge_messages(): from_source = jnp.take(padded, sources.reshape(-1), axis=0)  36.3 us
    gather x1, local copies, waits for them, and re-layouts, edge_messages(): from_target = jnp.take(own_rows, targets.reshape(-1), axis=0)  33.6 us
    dot_general x3, matrix products, two_layer(): jnp.dot(hidden, second_weight, preferred_element_type=jnp.float32)  28.6 us
    unnamed x64, local copies, waits for them, and re-layouts  17.8 us
    dot_general x1, matrix products, edge_messages(): jnp.dot(flat_edges, first_w[0], preferred_element_type=jnp.float32)  13.7 us
    all_to_all x1, starting transfers between devices, body(): rows_in = lax.all_to_all(rows_out, ('gx', 'gy'), 0, 0, tiled=True)  11.5 us
    reduce_sum x3, other arithmetic, layer_norm(): spread = jnp.mean(centred * centred, axis=-1, keepdims=True)  11.4 us
    select_n x1, other arithmetic, edge_messages(): jnp.where(keep_rows, (flat_edges.astype(jnp.float32) + message.astype(jnp...  10.5 us
  transfers between devices with their start and end apart: 6, of which 1 were waited for; matrix products, arithmetic and copies ran while one was open for 29% of the time, Pallas kernels for 0%

profile of v1, /device:TPU:1, one launch (start us, length us, event | category | flops | bytes accessed | tf_op | source)
XLA Modules:
  0.0 257.6 jit_solution(880520035812007373)
XLA Ops:
  2.9 1.9 fusion.18
  7.7 11.5 %all-to-all-start = ((bf16[128,2,320]{2,1,0:T(2,128)(2,1)}), bf16[128,2,320]{2,1,0:T(2,128)(2,1)S(1)}, u32[]{:S(2)}, u32[]{:S(2)}) async-start(bf16[128,2,320]{2,1,0:T(2,128)(2,1)} %reshape.384), calls=%async_computation | async-start | bytes 393216 | tf_op jit(solution)/shard_map/all_to_all | solution.py:155
  19.2 1.9 fusion.92
  21.1 4.0 %collective-permute-start = (bf16[1,2,128,512]{3,2,1,0:T(8,128)(2,1)}, bf16[1,2,128,512]{3,2,1,0:T(8,128)(2,1)}, u32[]{:S(2)}, u32[]{:S(2)}) collective-permute-start(bf16[1,2,128,512]{3,2,1,0:T(8,128)(2,1)} %get-tuple-element.9), channel_id=1, source_target_pairs={{0,8},{8,16},{16,24},{24,32},{32,40},{40,48},{48,56},{56,64},{64,7... | collective-permute-start | bytes 786440 | tf_op jit(solution)/shard_map/ppermute | solution.py:16
  25.0 1.3 collective-permute-start.1
  27.0 1.4 compare_and_fusion.1
  30.5 1.4 compare_and_fusion
  32.8 33.6 %gather_fusion.1 = bf16[8192,512]{1,0:T(8,128)(2,1)} fusion(bf16[1024,512]{1,0:T(8,128)(2,1)S(1)} %bitcast.118, s32[8192]{0:T(1024)S(1)} %broadcast_clamp_fusion), kind=kCustom, calls=%fused_computation.1 | custom fusion | bytes 16809984 | tf_op jit(solution)/shard_map/jit(_take)/gather | solution.py:39
  67.2 3.1 %fusion.34 = f32[1024,512]{1,0:T(8,128)} fusion(bf16[1024,512]{1,0:T(8,128)(2,1)S(1)} %bitcast.119, bf16[2,512,512]{2,1,0:T(8,128)(2,1)} %param.44), kind=kOutput, calls=%fused_computation.51 | convolution fusion | flops 536870912 | bytes 3670016 | tf_op jit(solution)/shard_map/dot_general | solution.py:116
  70.5 13.7 %fusion.32 = f32[8192,512]{1,0:T(8,128)} fusion(bf16[8192,512]{1,0:T(8,128)(2,1)} %bitcast.125, bf16[3,512,512]{2,1,0:T(8,128)(2,1)} %param.39), kind=kOutput, calls=%fused_computation.49 | convolution fusion | flops 4294967296 | bytes 25690112 | tf_op jit(solution)/shard_map/dot_general | solution.py:40
  85.7 1.5 fusion.97
  88.5 1.3 fusion.91
  89.8 3.8 %collective-permute-start.2 = (bf16[6,1,128,512]{3,2,1,0:T(8,128)(2,1)}, bf16[6,1,128,512]{3,2,1,0:T(8,128)(2,1)}, u32[]{:S(2)}, u32[]{:S(2)}) collective-permute-start(bf16[6,1,128,512]{3,2,1,0:T(8,128)(2,1)} %get-tuple-element.6), channel_id=1, source_target_pairs={{0,1},{1,2},{2,3},{3,4},{4,5},{5,6},{6,7},{8,9},{9,10},{10,11},{11... | collective-permute-start | bytes 2359304 | tf_op jit(solution)/shard_map/ppermute | solution.py:16
  93.6 1.9 collective-permute-start.3
  99.1 10.2 %all-to-all-start.1 = ((bf16[128,2,256]{2,1,0:T(2,128)(2,1)}), bf16[128,2,256]{2,1,0:T(2,128)(2,1)S(1)}, u32[]{:S(2)}, u32[]{:S(2)}) async-start(bf16[128,2,256]{2,1,0:T(2,128)(2,1)} %reshape.386), calls=%async_computation.1 | async-start | bytes 262144 | tf_op jit(solution)/shard_map/all_to_all | solution.py:177
  110.0 9.0 %all-to-all-done.1 = bf16[128,2,256]{2,1,0:T(2,128)(2,1)S(1)} async-done(((bf16[128,2,256]{2,1,0:T(2,128)(2,1)}), bf16[128,2,256]{2,1,0:T(2,128)(2,1)S(1)}, u32[]{:S(2)}, u32[]{:S(2)}) %all-to-all-start.1) | async-done | bytes 131104 | tf_op jit(solution)/shard_map/all_to_all | solution.py:177
  119.2 1.1 fusion.17
  120.3 5.5 %gather_fusion.2 = bf16[1024,512]{1,0:T(8,128)(2,1)} fusion(bf16[128,512]{1,0:T(8,128)(2,1)S(1)} %fusion.17, s32[1024]{0:T(1024)} %broadcast_clamp_fusion.2), kind=kCustom, calls=%fused_computation.2 | custom fusion | bytes 2101248 | tf_op jit(solution)/shard_map/jit(_take)/gather | solution.py:182
  125.8 3.4 %pad_maximum_fusion = bf16[6,4,128,512]{3,2,1,0:T(8,128)(2,1)} fusion(bf16[6,1,128,512]{3,2,1,0:T(8,128)(2,1)} %collective-permute-done.3, bf16[6,2,128,512]{3,2,1,0:T(8,128)(2,1)S(1)} %constant_dynamic-update-slice_fusion, bf16[6,1,128,512]{3,2,1,0:T(8,128)(2,1)} %collective-permute-done.2), kind=kLoop, calls=%fused_computation.21 | loop fusion | flops 3145728 | bytes 6291456 | tf_op jit(solution)/shard_map/concatenate | solution.py:18
  129.2 36.3 %gather_fusion = bf16[8192,512]{1,0:T(8,128)(2,1)} fusion(bf16[3072,512]{1,0:T(8,128)(2,1)} %bitcast.120, s32[8192]{0:T(1024)S(1)} %copy-done.9), kind=kCustom, calls=%fused_computation | custom fusion | bytes 16809984 | tf_op jit(solution)/shard_map/jit(_take)/gather | solution.py:38
  165.5 10.4 %fusion.3 = f32[8192,512]{1,0:T(8,128)} fusion(bf16[8192,512]{1,0:T(8,128)(2,1)} %gather_fusion, pred[8192]{0:T(1024)(128)(4,1)S(1)} %copy-done.15, bf16[3,512,512]{2,1,0:T(8,128)(2,1)S(1)} %copy-done.8), kind=kOutput, calls=%fused_computation.12 | convolution fusion | flops 4299161600 | bytes 25698304 | tf_op jit(solution)/shard_map/dot_general | solution.py:41
  175.9 22.1 %add_reduce_fusion = (f32[8192]{0:T(1024)S(1)}, f32[8192,512]{1,0:T(8,128)}) fusion(f32[512]{0:T(512)S(1)} %copy-done.13, bf16[512,512]{1,0:T(8,128)(2,1)S(1)} %copy-done, f32[8192,512]{1,0:T(8,128)} %fusion.32, f32[8192,512]{1,0:T(8,128)} %fusion.3, f32[512]{0:T(512)S(1)} %copy-done.26, bf16[8192,512]{1,0:T(8,128)(2,1)} %gather_fusion.1, ...), kind=kOutput, calls=%fused_computation.8 | convolution fusion | flops 8636063744 | bytes 59813888 | tf_op jit(solution)/shard_map/dot_general | solution.py:30
  198.1 9.2 %multiply_reduce_fusion = f32[8192]{0:T(1024)S(1)} fusion(f32[8192,512]{1,0:T(8,128)} %get-tuple-element.14, f32[8192]{0:T(1024)S(1)} %broadcast_multiply_fusion, f32[512]{0:T(512)S(1)} %copy-done.13), kind=kLoop, calls=%fused_computation.6 | loop fusion | flops 16769024 | bytes 16844800 | tf_op jit(solution)/shard_map/reduce_sum | solution.py:24
  207.3 1.4 copy-done.4
  208.7 10.5 %fusion = (bf16[8192,512]{1,0:T(8,128)(2,1)}, bf16[8192,512]{1,0:T(8,128)(2,1)}) fusion(pred[8192]{0:T(1024)(128)(4,1)S(1)} %broadcast_bitcast_fusion, bf16[1,1,64,128,512]{4,3,2,1,0:T(8,128)(2,1)} %param.28, f32[512]{0:T(512)S(1)} %copy-done.21, f32[8192]{0:T(1024)S(1)} %add_rsqrt_fusion, f32[8192]{0:T(1024)S(1)} %broadcast_multiply_fusion, ...), kind=kLoop, calls=%fused_computation.9 | loop fusion | flops 46137344 | bytes 42020864 | tf_op jit(solution)/shard_map/jit(_where)/select_n | solution.py:46
  219.2 5.7 %fusion.13 = f32[64,128,512]{2,1,0:T(8,128)S(1)} fusion(bf16[64,128,512]{2,1,0:T(8,128)(2,1)} %bitcast.124, s32[64,128]{1,0:T(8,128)S(1)} %bitcast.131), kind=kOutput, calls=%fused_computation.20 | convolution fusion | flops 1074790400 | bytes 25198592 | tf_op jit(solution)/shard_map/uot,utx->uox/dot_general | solution.py:103
  225.0 11.9 %copy.49 = f32[8,8,128,512]{3,1,2,0:T(8,128)} copy(f32[8,8,128,512]{3,2,1,0:T(8,128)S(1)} %bitcast.122) | data formatting | bytes 33554432
  236.9 9.0 %convolution_convert_fusion = bf16[8,65536]{1,0:T(8,128)(2,1)S(1)} fusion(f32[64,65536]{1,0:T(8,128)} %bitcast.123, s32[64]{0:T(128)S(1)} %bitcast.143), kind=kOutput, calls=%fused_computation.3 | convolution fusion | flops 403177984 | bytes 17826048 | tf_op jit(solution)/shard_map/dot_general | solution.py:109
  246.0 1.4 convert_element_type.105
  247.5 4.9 %add_reduce_fusion.1 = (f32[1024]{0:T(1024)S(1)}, f32[1024,512]{1,0:T(8,128)}) fusion(f32[512]{0:T(512)S(1)} %copy-done.14, bf16[512,512]{1,0:T(8,128)(2,1)S(1)} %copy-done.25, f32[1024,512]{1,0:T(8,128)} %fusion.34, bf16[1024,512]{1,0:T(8,128)(2,1)} %convert_element_type.105, f32[512]{0:T(512)S(1)} %copy-done.27, bf16[2,512,512]{2,1,0:T(8,128)(2,1)} %param.44), kind=kOutput, calls=%fused_computation.26 | convolution fusion | flops 1078459392 | bytes 6299648 | tf_op jit(solution)/shard_map/dot_general | solution.py:30
  252.4 2.0 multiply_reduce_fusion.1
  254.5 3.1 %add_convert_fusion.1 = bf16[1024,512]{1,0:T(8,128)(2,1)} fusion(f32[1024,512]{1,0:T(8,128)} %get-tuple-element.18, bf16[1024,512]{1,0:T(8,128)(2,1)S(1)} %copy-done.5, f32[1024]{0:T(1024)S(1)} %bitcast.141, f32[512]{0:T(512)S(1)} %copy-done.22, f32[1024]{0:T(1024)S(1)} %add_rsqrt_fusion.1, f32[1024]{0:T(1024)S(1)} %broadcast_multiply_fusion.1, ...), kind=kLoop, calls=%fused_computation.22 | loop fusion | flops 5767168 | bytes 5260288 | tf_op jit(solution)/shard_map/convert_element_type | solution.py:183
  (102 shorter events, 16.3 us)
Async XLA Ops:
  0.6 175.3 %copy-start = (bf16[512,512]{1,0:T(8,128)(2,1)S(1)}, bf16[512,512]{1,0:T(8,128)(2,1)}, u32[]{:S(2)}) copy-start(bf16[512,512]{1,0:T(8,128)(2,1)} %param.41) | copy-start | bytes 1572868
  0.6 32.2 %copy-start.2 = (bf16[4,2,128,512]{3,2,1,0:T(8,128)(2,1)S(1)}, bf16[4,2,128,512]{3,2,1,0:T(8,128)(2,1)}, u32[]{:S(2)}) copy-start(bf16[4,2,128,512]{3,2,1,0:T(8,128)(2,1)} %param.27) | copy-start | bytes 3145732
  2.1 3.5 %copy-start.24 = (s32[128]{0:T(128)}, s32[128]{0:T(128)S(1)}, u32[]{:S(2)}) copy-start(s32[128]{0:T(128)S(1)} %and_select_fusion.1) | copy-start | bytes 1540
  7.7 77.1 %all-to-all-start = ((bf16[128,2,320]{2,1,0:T(2,128)(2,1)}), bf16[128,2,320]{2,1,0:T(2,128)(2,1)S(1)}, u32[]{:S(2)}, u32[]{:S(2)}) async-start(bf16[128,2,320]{2,1,0:T(2,128)(2,1)} %reshape.384), calls=%async_computation | async-start | bytes 393216 | tf_op jit(solution)/shard_map/all_to_all | solution.py:155
  21.1 66.3 %collective-permute-start = (bf16[1,2,128,512]{3,2,1,0:T(8,128)(2,1)}, bf16[1,2,128,512]{3,2,1,0:T(8,128)(2,1)}, u32[]{:S(2)}, u32[]{:S(2)}) collective-permute-start(bf16[1,2,128,512]{3,2,1,0:T(8,128)(2,1)} %get-tuple-element.9), channel_id=1, source_target_pairs={{0,8},{8,16},{16,24},{24,32},{32,40},{40,48},{48,56},{56,64},{64,7... | collective-permute-start | bytes 786440 | tf_op jit(solution)/shard_map/ppermute | solution.py:16
  25.0 63.4 %collective-permute-start.1 = (bf16[1,2,128,512]{3,2,1,0:T(8,128)(2,1)}, bf16[1,2,128,512]{3,2,1,0:T(8,128)(2,1)S(1)}, u32[]{:S(2)}, u32[]{:S(2)}) collective-permute-start(bf16[1,2,128,512]{3,2,1,0:T(8,128)(2,1)} %get-tuple-element.8), channel_id=1, source_target_pairs={{8,0},{16,8},{24,16},{32,24},{40,32},{48,40},{56,48},{64,56},{72,6... | collective-permute-start | bytes 786440 | tf_op jit(solution)/shard_map/ppermute | solution.py:17
  32.8 37.5 %copy-start.6 = (bf16[2,512,512]{2,1,0:T(8,128)(2,1)S(1)}, bf16[2,512,512]{2,1,0:T(8,128)(2,1)}, u32[]{:S(2)}) copy-start(bf16[2,512,512]{2,1,0:T(8,128)(2,1)} %param.49) | copy-start | bytes 3145732
  32.8 37.5 %copy-start.11 = (bf16[8,512]{1,0:T(8,128)(2,1)S(1)}, bf16[8,512]{1,0:T(8,128)(2,1)}, u32[]{:S(2)}) copy-start(bf16[8,512]{1,0:T(8,128)(2,1)} %param.30) | copy-start | bytes 24580
  70.5 15.2 %copy-start.19 = (f32[512]{0:T(512)S(1)}, f32[512]{0:T(512)}, u32[]{:S(2)}) copy-start(f32[512]{0:T(512)} %param.52) | copy-start | bytes 6148
  70.5 15.2 %copy-start.20 = (f32[512]{0:T(512)S(1)}, f32[512]{0:T(512)}, u32[]{:S(2)}) copy-start(f32[512]{0:T(512)} %param.50) | copy-start | bytes 6148
  85.3 2.1 copy-start.17
  89.8 36.0 %collective-permute-start.2 = (bf16[6,1,128,512]{3,2,1,0:T(8,128)(2,1)}, bf16[6,1,128,512]{3,2,1,0:T(8,128)(2,1)}, u32[]{:S(2)}, u32[]{:S(2)}) collective-permute-start(bf16[6,1,128,512]{3,2,1,0:T(8,128)(2,1)} %get-tuple-element.6), channel_id=1, source_target_pairs={{0,1},{1,2},{2,3},{3,4},{4,5},{5,6},{6,7},{8,9},{9,10},{10,11},{11... | collective-permute-start | bytes 2359304 | tf_op jit(solution)/shard_map/ppermute | solution.py:16
  93.6 32.2 %collective-permute-start.3 = (bf16[6,1,128,512]{3,2,1,0:T(8,128)(2,1)}, bf16[6,1,128,512]{3,2,1,0:T(8,128)(2,1)}, u32[]{:S(2)}, u32[]{:S(2)}) collective-permute-start(bf16[6,1,128,512]{3,2,1,0:T(8,128)(2,1)} %get-tuple-element.7), channel_id=1, source_target_pairs={{1,0},{2,1},{3,2},{4,3},{5,4},{6,5},{7,6},{9,8},{10,9},{11,10},{12... | collective-permute-start | bytes 2359304 | tf_op jit(solution)/shard_map/ppermute | solution.py:17
  99.1 19.9 %all-to-all-start.1 = ((bf16[128,2,256]{2,1,0:T(2,128)(2,1)}), bf16[128,2,256]{2,1,0:T(2,128)(2,1)S(1)}, u32[]{:S(2)}, u32[]{:S(2)}) async-start(bf16[128,2,256]{2,1,0:T(2,128)(2,1)} %reshape.386), calls=%async_computation.1 | async-start | bytes 262144 | tf_op jit(solution)/shard_map/all_to_all | solution.py:177
  120.3 45.2 %copy-start.3 = (bf16[128,512]{1,0:T(8,128)(2,1)}, bf16[128,512]{1,0:T(8,128)(2,1)S(1)}, u32[]{:S(2)}) copy-start(bf16[128,512]{1,0:T(8,128)(2,1)S(1)} %fusion.17) | copy-start | bytes 393220
  120.3 8.8 %copy-start.9 = (s32[8192]{0:T(1024)S(1)}, s32[8192]{0:T(1024)}, u32[]{:S(2)}) copy-start(s32[8192]{0:T(1024)} %broadcast_clamp_fusion.1) | copy-start | bytes 98308
  129.2 36.3 %copy-start.8 = (bf16[3,512,512]{2,1,0:T(8,128)(2,1)S(1)}, bf16[3,512,512]{2,1,0:T(8,128)(2,1)}, u32[]{:S(2)}) copy-start(bf16[3,512,512]{2,1,0:T(8,128)(2,1)} %param.39) | copy-start | bytes 4718596
  129.2 36.3 %copy-start.15 = (pred[8192]{0:T(1024)(128)(4,1)S(1)}, pred[8192]{0:T(1024)(128)(4,1)}, u32[]{:S(2)}) copy-start(pred[8192]{0:T(1024)(128)(4,1)} %compare_and_fusion.1) | copy-start | bytes 24580
  165.5 10.4 %copy-start.13 = (f32[512]{0:T(512)S(1)}, f32[512]{0:T(512)}, u32[]{:S(2)}) copy-start(f32[512]{0:T(512)} %param.42) | copy-start | bytes 6148
  165.5 10.4 %copy-start.16 = (pred[8192]{0:T(1024)(128)(4,1)S(1)}, pred[8192]{0:T(1024)(128)(4,1)}, u32[]{:S(2)}) copy-start(pred[8192]{0:T(1024)(128)(4,1)} %compare_and_fusion) | copy-start | bytes 24580
  165.5 10.4 %copy-start.26 = (f32[512]{0:T(512)S(1)}, f32[512]{0:T(512)}, u32[]{:S(2)}) copy-start(f32[512]{0:T(512)} %param.40) | copy-start | bytes 6148
  198.1 10.7 %copy-start.4 = (f32[8192,512]{1,0:T(8,128)S(1)}, f32[8192,512]{1,0:T(8,128)}, u32[]{:S(2)}) copy-start(f32[8192,512]{1,0:T(8,128)} %get-tuple-element.14) | copy-start | bytes 50331652
  198.1 10.7 %copy-start.21 = (f32[512]{0:T(512)S(1)}, f32[512]{0:T(512)}, u32[]{:S(2)}) copy-start(f32[512]{0:T(512)} %param.43) | copy-start | bytes 6148
  208.7 10.5 %copy-start.7 = (s32[1,1,64,128]{3,2,1,0:T(8,128)S(1)}, s32[1,1,64,128]{3,2,1,0:T(8,128)}, u32[]{:S(2)}) copy-start(s32[1,1,64,128]{3,2,1,0:T(8,128)} %param.33) | copy-start | bytes 98308
  224.9 12.0 %copy-start.23 = (s32[1,1,64]{2,1,0:T(1,128)S(1)}, s32[1,1,64]{2,1,0:T(1,128)}, u32[]{:S(2)}) copy-start(s32[1,1,64]{2,1,0:T(1,128)} %param.32) | copy-start | bytes 772
  236.9 10.5 %copy-start.14 = (f32[512]{0:T(512)S(1)}, f32[512]{0:T(512)}, u32[]{:S(2)}) copy-start(f32[512]{0:T(512)} %param.47) | copy-start | bytes 6148
  236.9 10.5 %copy-start.25 = (bf16[512,512]{1,0:T(8,128)(2,1)S(1)}, bf16[512,512]{1,0:T(8,128)(2,1)}, u32[]{:S(2)}) copy-start(bf16[512,512]{1,0:T(8,128)(2,1)} %param.46) | copy-start | bytes 1572868
  236.9 10.5 %copy-start.27 = (f32[512]{0:T(512)S(1)}, f32[512]{0:T(512)}, u32[]{:S(2)}) copy-start(f32[512]{0:T(512)} %param.45) | copy-start | bytes 6148
  246.0 11.6 %copy-start.1 = (bf16[512,512]{1,0:T(8,128)(2,1)S(1)}, bf16[512,512]{1,0:T(8,128)(2,1)}, u32[]{:S(2)}) copy-start(bf16[512,512]{1,0:T(8,128)(2,1)} %param.41) | copy-start | bytes 1572868
  247.4 7.0 %copy-start.5 = (bf16[1024,512]{1,0:T(8,128)(2,1)S(1)}, bf16[1024,512]{1,0:T(8,128)(2,1)}, u32[]{:S(2)}) copy-start(bf16[1024,512]{1,0:T(8,128)(2,1)} %gather_fusion.2) | copy-start | bytes 3145732
  247.4 7.0 %copy-start.18 = (f32[4,2,128]{2,1,0:T(2,128)S(1)}, f32[4,2,128]{2,1,0:T(2,128)}, u32[]{:S(2)}) copy-start(f32[4,2,128]{2,1,0:T(2,128)} %param.36) | copy-start | bytes 12292
  247.4 7.0 %copy-start.22 = (f32[512]{0:T(512)S(1)}, f32[512]{0:T(512)}, u32[]{:S(2)}) copy-start(f32[512]{0:T(512)} %param.48) | copy-start | bytes 6148
  (2 other events, 1.3 us)

commit v2 on v0

v2 whole, which is shorter than its diff:
```python
import functools
import jax
import jax.numpy as jnp
from jax import lax
from jax.experimental import pallas as pl
from jax.experimental.pallas import tpu as pltpu
from jax.sharding import PartitionSpec as P

epsilon = 1e-05
SUB = 4
BOTH = ("gx", "gy")


def silu(values):
    half = 0.5 * values
    return half * jnp.tanh(half) + half


def layer_norm(values, gain):
    centred = values - jnp.mean(values, axis=-1, keepdims=True)
    spread = jnp.mean(centred * centred, axis=-1, keepdims=True)
    return centred * lax.rsqrt(spread + epsilon) * gain


def matmul(a, b):
    return jnp.dot(a, b, preferred_element_type=jnp.float32)


def matmul_t(a, b):
    return lax.dot_general(a, b, (((0,), (0,)), ((), ())), preferred_element_type=jnp.float32)


WHOLE = 14


def bring(whole, held, semaphores):
    copies = [pltpu.make_async_copy(a, b, semaphores.at[n]) for n, (a, b) in enumerate(zip(whole, held))]
    for copy in copies:
        copy.start()
    for copy in copies:
        copy.wait()


def edge_kernel(
    edges, *rest
):
    whole, (result, aggregate, table, targets, sums, picked_a, picked_b), held, semaphores = (
        rest[:WHOLE], rest[WHOLE : WHOLE + 7], rest[WHOLE + 7 : -1], rest[-1]
    )
    (sources, target_blocks, live, target_nodes, own, up, down, left, right, first, bias, second, bias_two, gain) = held
    step = pl.program_id(0)
    steps = pl.num_programs(0)
    picked = (picked_a, picked_b)
    latent = own.shape[-1]
    lanes = 128
    parts = latent // lanes
    blk = 128
    chunks = 2 * steps

    def project(piece, places):
        rows = matmul(piece, first[1]) + bias[...]
        for n, place in enumerate(places):
            for j in range(parts):
                table[pl.ds(place * blk * parts + j, blk, stride=parts), :] = rows[
                    n * blk : (n + 1) * blk, j * lanes : (j + 1) * lanes
                ]

    def gather(chunk, b, into):
        block = chunk * SUB + b
        for e in range(blk):
            at = pl.multiple_of(sources[block, e] * parts, parts)
            into[pl.ds((b * blk + e) * parts, parts), :] = table[pl.ds(at, parts), :]

    @pl.when(step == 0)
    def _():
        bring(whole, held, semaphores)
        rows_x, rows_y = own.shape[0], own.shape[1]
        wide = rows_y + 2
        own_rows = own[...].reshape(-1, latent)
        project(own_rows, [(x + 1) * wide + y + 1 for x in range(rows_x) for y in range(rows_y)])
        project(up[...].reshape(-1, latent), [y + 1 for y in range(rows_y)])
        project(down[...].reshape(-1, latent), [(rows_x + 1) * wide + y + 1 for y in range(rows_y)])
        project(left[...].reshape(-1, latent), [x * wide for x in range(rows_x + 2)])
        project(right[...].reshape(-1, latent), [x * wide + wide - 1 for x in range(rows_x + 2)])
        targets[...] = matmul(own_rows, first[2]).astype(jnp.bfloat16).reshape(targets.shape)
        sums[...] = jnp.zeros_like(sums)
        for b in range(SUB):
            gather(0, b, picked_a)

    number = lax.broadcasted_iota(jnp.int32, (blk, blk), 0)

    def compute(half, b_next):
        chunk = 2 * step + half
        ref = picked[half]
        base = half * SUB
        states = edges[base : base + SUB].reshape(SUB * blk, latent)
        pre = matmul(states, first[0])
        hidden = []
        spots = []
        for b in range(SUB):
            b_next(b)
            block = chunk * SUB + b
            to = target_blocks[0, block]
            spot = (target_nodes[pl.ds(block, 1), :] == number).astype(jnp.bfloat16)
            spots.append((to, spot))
            from_target = matmul_t(spot, targets[to])
            from_source = jnp.concatenate(
                [ref[pl.ds(b * blk * parts + j, blk, stride=parts), :] for j in range(parts)], axis=1
            )
            hidden.append(
                silu(pre[b * blk : (b + 1) * blk] + from_target + from_source).astype(jnp.bfloat16)
            )
        out = matmul(jnp.concatenate(hidden, axis=0), second[...]) + bias_two[...]
        for b in range(SUB):
            rows = out[b * blk : (b + 1) * blk]
            block = chunk * SUB + b
            alive = jnp.where(block < live[0, 0], 1.0, 0.0)
            centred = rows - jnp.mean(rows, axis=-1, keepdims=True)
            spread = jnp.mean(centred * centred, axis=-1, keepdims=True)
            message = (centred * (lax.rsqrt(spread + epsilon) * alive) * gain[...]).astype(jnp.bfloat16)
            result[base + b] = edges[base + b] + message
            to, spot = spots[b]
            sums[to] += matmul(spot, message)

    compute(0, lambda b: gather(2 * step + 1, b, picked_b))
    compute(1, lambda b: gather(jnp.minimum(2 * step + 2, chunks - 1), b, picked_a))

    @pl.when(step == steps - 1)
    def _():
        aggregate[...] = sums[...].astype(aggregate.dtype)


def edge_call(edges, *whole):
    count, blk, latent = edges.shape
    per = 2 * SUB
    steps = count // per
    rows_x, rows_y = whole[4].shape[:2]
    own_blocks = rows_x * rows_y
    window = (rows_x + 2) * (rows_y + 2)
    table = window * blk * latent // 128
    picked = SUB * blk * latent // 128
    return pl.pallas_call(
        edge_kernel,
        grid=(steps,),
        in_specs=[pl.BlockSpec((per, blk, latent), lambda i: (i, 0, 0))]
        + [pl.BlockSpec(memory_space=pltpu.HBM)] * len(whole),
        out_specs=[
            pl.BlockSpec((per, blk, latent), lambda i: (i, 0, 0)),
            pl.BlockSpec((own_blocks, blk, latent), lambda i: (0, 0, 0)),
        ],
        scratch_shapes=[
            pltpu.VMEM((table, 128), jnp.float32),
            pltpu.VMEM((own_blocks, blk, latent), jnp.bfloat16),
            pltpu.VMEM((own_blocks, blk, latent), jnp.float32),
            pltpu.VMEM((picked, 128), jnp.float32),
            pltpu.VMEM((picked, 128), jnp.float32),
        ]
        + [pltpu.SMEM(a.shape, a.dtype) for a in whole[:3]]
        + [pltpu.VMEM(a.shape, a.dtype) for a in whole[3:]]
        + [pltpu.SemaphoreType.DMA((len(whole),))],
        out_shape=[
            jax.ShapeDtypeStruct(edges.shape, edges.dtype),
            jax.ShapeDtypeStruct((own_blocks, blk, latent), jnp.bfloat16),
        ],
        compiler_params=pltpu.CompilerParams(
            vmem_limit_bytes=48 * 2**20, dimension_semantics=("arbitrary",)
        ),
        cost_estimate=pl.CostEstimate(
            flops=20 * 10**9, bytes_accessed=100 * 10**6, transcendentals=5 * 10**6
        ),
        name="edges",
    )(edges, *whole)


def column(row):
    count = row.shape[-1]
    diagonal = lax.broadcasted_iota(jnp.int32, (count, count), 0) == lax.broadcasted_iota(
        jnp.int32, (count, count), 1
    )
    return jnp.sum(jnp.where(diagonal, row, jnp.zeros_like(row)), axis=1, keepdims=True)


def middle_kernel(own, parents, weights, middle, mid_parents, mid_weights, middle_mid, rows_out, *, coarse_own):
    blocks, blk, latent = own.shape
    count = middle.shape[0]
    number = lax.broadcasted_iota(jnp.int32, (count, blk), 0)
    tops = []
    rests = []
    wide = parents.shape[1]
    for b in range(blocks):
        x, y = b // wide, b % wide
        share = jnp.where(parents[x, y : y + 1, :] == number, weights[x, y : y + 1, :], 0.0)
        top = share.astype(jnp.bfloat16)
        tops.append(top)
        rests.append((share - top.astype(jnp.float32)).astype(jnp.bfloat16))
    rows = own[...].reshape(blocks * blk, latent)
    total = matmul(jnp.concatenate(tops, axis=1), rows) + matmul(jnp.concatenate(rests, axis=1), rows)
    mid = (middle[...].astype(jnp.float32) + total).astype(jnp.bfloat16)
    middle_mid[...] = mid
    owner = mid_parents[...] // coarse_own
    place = mid_parents[...] - owner * coarse_own
    devices = rows_out.shape[0]
    mine = owner == lax.broadcasted_iota(jnp.int32, (devices, count), 0)
    rows_out[:, :latent] = matmul(mine.astype(jnp.bfloat16), mid).astype(jnp.bfloat16)
    weight = jnp.sum(jnp.where(mine, mid_weights[...], 0.0), axis=1, keepdims=True)
    spot = jnp.sum(jnp.where(mine, place.astype(jnp.float32), 0.0), axis=1, keepdims=True)
    top = weight.astype(jnp.bfloat16).astype(jnp.float32)
    second = (weight - top).astype(jnp.bfloat16).astype(jnp.float32)
    lane = lax.broadcasted_iota(jnp.int32, (devices, rows_out.shape[1] - latent), 1)
    notes = jnp.where(lane == 0, top, jnp.where(lane == 1, second, jnp.where(lane == 2, weight - top - second, spot)))
    rows_out[:, latent:] = notes.astype(jnp.bfloat16)


def coarse_kernel(rows_in, coarse, first, bias, second, bias_two, gain, result, answers):
    own_count, latent = coarse.shape
    devices = rows_in.shape[0]
    notes = rows_in[:, latent:].astype(jnp.float32)
    lane = lax.broadcasted_iota(jnp.int32, (devices, 128), 1)
    at_place = notes[:, 3:4] == lane.astype(jnp.float32)
    rows = rows_in[:, :latent]
    total = jnp.zeros((128, latent), jnp.float32)
    for n in range(3):
        total += matmul_t(jnp.where(at_place, notes[:, n : n + 1], 0.0).astype(jnp.bfloat16), rows)
    summed = total[:own_count].astype(jnp.bfloat16)
    pre = matmul(coarse[...], first[0]) + matmul(summed, first[1]) + bias[...]
    hidden = silu(pre).astype(jnp.bfloat16)
    out = matmul(hidden, second[...]) + bias_two[...]
    new = coarse[...].astype(jnp.float32) + layer_norm(out, gain[...])
    result[...] = new.astype(jnp.bfloat16)
    padded = jnp.concatenate([new, jnp.zeros((128 - own_count, latent), jnp.float32)], axis=0)
    answers[...] = matmul(at_place.astype(jnp.bfloat16), padded.astype(jnp.bfloat16)).astype(jnp.bfloat16)


def final_kernel(
    own, aggregate, first, bias, second, bias_two, gain,
    middle_mid, from_owners, mid_parents, mid_weights, parents, weights, fine_result, middle_result, *, coarse_own,
):
    blocks, blk, latent = own.shape
    count = middle_mid.shape[0]
    rows = own[...].reshape(blocks * blk, latent)
    pre = matmul(rows, first[0]) + matmul(aggregate[...].reshape(blocks * blk, latent), first[1]) + bias[...]
    out = matmul(silu(pre).astype(jnp.bfloat16), second[...]) + bias_two[...]
    fine_mid = rows.astype(jnp.float32) + layer_norm(out, gain[...])
    devices = from_owners.shape[0]
    mine = mid_parents[...] // coarse_own == lax.broadcasted_iota(jnp.int32, (devices, count), 0)
    from_coarse = matmul_t(mine.astype(jnp.bfloat16), from_owners[...])
    new_middle = (middle_mid[...].astype(jnp.float32) + column(mid_weights[...]) * from_coarse).astype(jnp.bfloat16)
    middle_result[...] = new_middle
    number = lax.broadcasted_iota(jnp.int32, (count, blk), 0)
    wide = parents.shape[1]
    for b in range(blocks):
        x, y = b // wide, b % wide
        from_middle = matmul_t((parents[x, y : y + 1, :] == number).astype(jnp.bfloat16), new_middle)
        fine_result[b] = (
            fine_mid[b * blk : (b + 1) * blk] + column(weights[x, y : y + 1, :]) * from_middle
        ).astype(jnp.bfloat16)


def call(kernel, name, out_shape, *args, **static):
    count = len(args)
    total = count + len(out_shape)

    def run(*refs):
        held = refs[total : total + count]
        bring(refs[:count], held, refs[-1])
        kernel(*held, *refs[count:total], **static)

    return pl.pallas_call(
        run,
        out_shape=out_shape,
        in_specs=[pl.BlockSpec(memory_space=pltpu.HBM)] * count,
        out_specs=[pl.BlockSpec(memory_space=pltpu.VMEM)] * len(out_shape),
        scratch_shapes=[pltpu.VMEM(a.shape, a.dtype) for a in args] + [pltpu.SemaphoreType.DMA((count,))],
        cost_estimate=pl.CostEstimate(flops=10**9, bytes_accessed=9 * 10**6, transcendentals=10**5),
        compiler_params=pltpu.CompilerParams(vmem_limit_bytes=48 * 2**20),
        name=name,
    )(*args)


def exchanged(array, axis, dim):
    count, length = (lax.axis_size(axis), array.shape[dim])
    up = [(i, (i + 1) % count) for i in range(count - 1)]
    down = [(j, i) for i, j in up]
    last = lax.slice_in_dim(array, length - 1, length, axis=dim)
    first = lax.slice_in_dim(array, 0, 1, axis=dim)
    return lax.ppermute(last, axis, up), lax.ppermute(first, axis, down)


def body(
    fine_nodes, edge_states, middle_nodes, coarse_nodes, edge_sources, target_blocks, target_nodes,
    live_blocks, fine_parent, fine_weight, middle_parent, middle_weight,
    edge_in, edge_bias, edge_out, edge_bias_two, edge_gain,
    node_in, node_bias, node_out, node_bias_two, node_gain,
    coarse_in, coarse_bias, coarse_out, coarse_bias_two, coarse_gain,
):
    rows_x, rows_y, blk, latent = fine_nodes.shape
    blocks = rows_x * rows_y
    coarse_own = coarse_nodes.shape[0]
    devices = lax.axis_size(BOTH)
    row = lambda a: a.reshape(1, -1)
    own = fine_nodes.reshape(blocks, blk, latent)
    mid_parents = row(middle_parent)
    mid_weights = row(middle_weight)
    middle = middle_nodes.reshape(-1, latent)
    like = jax.ShapeDtypeStruct

    up, down = exchanged(fine_nodes, "gx", 0)
    middle_mid, rows_out = call(
        middle_kernel, "middle", [like(middle.shape, jnp.bfloat16), like((devices, latent + 128), jnp.bfloat16)],
        own, fine_parent, fine_weight, middle, mid_parents, mid_weights, coarse_own=coarse_own,
    )
    tall = lambda y: jnp.concatenate([up[:, y : y + 1], fine_nodes[:, y : y + 1], down[:, y : y + 1]], axis=0)
    count = lax.axis_size("gy")
    right_pairs = [(i, i + 1) for i in range(count - 1)]
    left = lax.ppermute(tall(rows_y - 1), "gy", right_pairs)
    right = lax.ppermute(tall(0), "gy", [(j, i) for i, j in right_pairs])
    rows_in = lax.all_to_all(rows_out, BOTH, 0, 0, tiled=True)
    edge_result, aggregate = edge_call(
        edge_states[0, 0], edge_sources[0, 0], target_blocks[0], live_blocks, target_nodes[0, 0],
        fine_nodes, up, down, left, right,
        edge_in, row(edge_bias), edge_out, row(edge_bias_two), row(edge_gain),
    )
    coarse_result, answers = call(
        coarse_kernel, "coarse", [like(coarse_nodes.shape, jnp.bfloat16), like((devices, latent), jnp.bfloat16)],
        rows_in, coarse_nodes, coarse_in, row(coarse_bias), coarse_out, row(coarse_bias_two), row(coarse_gain),
    )
    from_owners = lax.all_to_all(answers, BOTH, 0, 0, tiled=True)
    fine_result, middle_result = call(
        final_kernel, "final", [like(own.shape, jnp.bfloat16), like(middle.shape, jnp.bfloat16)],
        own, aggregate, node_in, row(node_bias), node_out, row(node_bias_two), row(node_gain),
        middle_mid, from_owners, mid_parents, mid_weights, fine_parent, fine_weight, coarse_own=coarse_own,
    )
    return (
        fine_result.reshape(fine_nodes.shape),
        edge_result.reshape(edge_states.shape),
        middle_result.reshape(middle_nodes.shape),
        coarse_result,
    )


def solution(mesh):
    placed = (
        P("gx", "gy", None, None),
        P("gx", "gy", None, None, None),
        P("gx", "gy", None, None),
        P(("gx", "gy"), None),
        P("gx", "gy", None, None),
        P("gx", "gy", None),
        P("gx", "gy", None, None),
        P("gx", "gy"),
        P("gx", "gy", None),
        P("gx", "gy", None),
        P("gx", "gy", None),
        P("gx", "gy", None),
        P(),
        P(),
        P(),
        P(),
        P(),
        P(),
        P(),
        P(),
        P(),
        P(),
        P(),
        P(),
        P(),
        P(),
        P(),
    )
    return jax.shard_map(
        body,
        mesh=mesh,
        in_specs=placed,
        out_specs=(
            P("gx", "gy", None, None),
            P("gx", "gy", None, None, None),
            P("gx", "gy", None, None),
            P(("gx", "gy"), None),
        ),
        check_vma=False,
    )
```

time: 742 us -> 117 us (0.16)
  waiting for transfers between devices: 504 us -> 15.2 us
  local copies, waits for them, and re-layouts: 95.7 us -> 14.9 us
  matrix products: 76.4 us -> 0 us
  Pallas kernels: 0 us -> 41.4 us
  other arithmetic: 37 us -> 3.97 us
  blocking collectives: 0 us -> 21.6 us
  between operations: 15.1 us -> 1.91 us
    reduce_scatter x1 -> x0, waiting for transfers between devices: 473 us -> none  [body(): lax.psum_scatter(jnp.dot(select, middle_wide, precision=lax.Precision.HIG...]
    dot_general x11 -> x0, matrix products: 76.4 us -> none  [the longest x3 28.3 us: two_layer(): jnp.dot(hidden, second_weight, preferred_element_type=jnp.float32)]
    gather x4 -> x0, local copies, waits for them, and re-layouts: 76.3 us -> none  [the longest x1 36.4 us: edge_messages(): from_source = jnp.take(padded, sources.reshape(-1), axis=0)]
    pallas_call x0 -> x4, Pallas kernels: none -> 41.4 us  [the longest x1 34.2 us: edge_call(): pl.pallas_call(edge_kernel, grid=(steps,), in_specs=[pl.BlockSpec((per, b...]
    all_gather x1 -> x0, waiting for transfers between devices: 30.8 us -> none  [body(): everyone = lax.all_gather(coarse_result, ('gx', 'gy'), axis=0, tiled=True)]
    all_to_all x0 -> x1, blocking collectives: none -> 21.6 us  [body(): rows_in = lax.all_to_all(rows_out, BOTH, 0, 0, tiled=True)]
    select_n x5 -> x0, other arithmetic: 12.9 us -> none  [the longest x1 10.6 us: edge_messages(): jnp.where(keep_rows, (flat_edges.astype(jnp.float32) + message.astype(jnp...]
    reduce_sum x3 -> x0, other arithmetic: 11.5 us -> none  [layer_norm(): spread = jnp.mean(centred * centred, axis=-1, keepdims=True)]
  transfers between devices with their start and end apart: 6 -> 5, of which waited for: 2 -> 3; matrix products, arithmetic and copies ran while one was open for 26% -> 9% of each run, Pallas kernels for 0% -> 2%
where the time goes in v2:
time: 117 us; the launch traced here: 116 us
  Pallas kernels  41.4 us (35%)
  blocking collectives  21.6 us (18%)
  starting transfers between devices  17.1 us (15%)
  waiting for transfers between devices  15.2 us (13%)
  local copies, waits for them, and re-layouts  14.9 us (13%)
  other arithmetic  3.97 us (3%)
  between operations  1.91 us (2%)
    pallas_call x1, Pallas kernels, edge_call(): pl.pallas_call(edge_kernel, grid=(steps,), in_specs=[pl.BlockSpec((per, b...  34.2 us
    all_to_all x1, blocking collectives, body(): rows_in = lax.all_to_all(rows_out, BOTH, 0, 0, tiled=True)  21.6 us
    unnamed x64, local copies, waits for them, and re-layouts  11.8 us
    all_to_all x1, waiting for transfers between devices, body(): from_owners = lax.all_to_all(answers, BOTH, 0, 0, tiled=True)  9.1 us
    pallas_call x3, Pallas kernels, call(): pl.pallas_call(run, out_shape=out_shape, in_specs=[pl.BlockSpec(memory_sp...  7.22 us
    ppermute x2, waiting for transfers between devices, exchanged(): return (lax.ppermute(last, axis, up), lax.ppermute(first, axis, down))  6.11 us
    ppermute x2, starting transfers between devices, exchanged(): return (lax.ppermute(last, axis, up), lax.ppermute(first, axis, down))  5.47 us
    all_to_all x1, starting transfers between devices, body(): from_owners = lax.all_to_all(answers, BOTH, 0, 0, tiled=True)  4.47 us
  transfers between devices with their start and end apart: 5, of which 3 were waited for; matrix products, arithmetic and copies ran while one was open for 9% of the time, Pallas kernels for 2%

profile of v2, /device:TPU:1, one launch (start us, length us, event | category | flops | bytes accessed | tf_op | source)
XLA Modules:
  0.0 116.1 jit_solution(17379778155946321237)
XLA Ops:
  0.7 1.2 %fusion.1 = (bf16[1,2,128,512]{3,2,1,0:T(8,128)(2,1)S(1)}, bf16[1,2,128,512]{3,2,1,0:T(8,128)(2,1)S(1)}) fusion(bf16[4,2,128,512]{3,2,1,0:T(8,128)(2,1)} %rest_4_.1), kind=kLoop, calls=%fused_computation.5 | loop fusion | bytes 1048576 | tf_op jit(solution)/shard_map/slice | solution.py:285
  1.9 4.0 %collective-permute-start = (bf16[1,2,128,512]{3,2,1,0:T(8,128)(2,1)S(1)}, bf16[1,2,128,512]{3,2,1,0:T(8,128)(2,1)S(1)}, u32[]{:S(2)}, u32[]{:S(2)}) collective-permute-start(bf16[1,2,128,512]{3,2,1,0:T(8,128)(2,1)S(1)} %get-tuple-element.23), channel_id=1, source_target_pairs={{0,8},{8,16},{16,24},{24,32},{32,40},{40,48},{48,56},{56,64},{64,7... | collective-permute-start | bytes 786440 | tf_op jit(solution)/shard_map/ppermute | solution.py:286
  6.0 1.4 %collective-permute-start.1 = (bf16[1,2,128,512]{3,2,1,0:T(8,128)(2,1)S(1)}, bf16[1,2,128,512]{3,2,1,0:T(8,128)(2,1)S(1)}, u32[]{:S(2)}, u32[]{:S(2)}) collective-permute-start(bf16[1,2,128,512]{3,2,1,0:T(8,128)(2,1)S(1)} %get-tuple-element.22), channel_id=1, source_target_pairs={{8,0},{16,8},{24,16},{32,24},{40,32},{48,40},{56,48},{64,56},{72,6... | collective-permute-start | bytes 786440 | tf_op jit(solution)/shard_map/ppermute | solution.py:286
  7.5 1.3 %fusion = (bf16[4,1,128,512]{3,2,1,0:T(8,128)(2,1)S(1)}, bf16[4,1,128,512]{3,2,1,0:T(8,128)(2,1)S(1)}) fusion(bf16[4,2,128,512]{3,2,1,0:T(8,128)(2,1)} %rest_4_.1), kind=kLoop, calls=%fused_computation.4 | loop fusion | bytes 2097152 | tf_op jit(solution)/shard_map/slice | solution.py:312
  8.8 2.1 %collective-permute-done.rest_5_ = bf16[1,2,128,512]{3,2,1,0:T(8,128)(2,1)S(1)} collective-permute-done((bf16[1,2,128,512]{3,2,1,0:T(8,128)(2,1)S(1)}, bf16[1,2,128,512]{3,2,1,0:T(8,128)(2,1)S(1)}, u32[]{:S(2)}, u32[]{:S(2)}) %collective-permute-start) | collective-permute-done | bytes 262176 | tf_op jit(solution)/shard_map/ppermute | solution.py:286
  10.9 4.0 %collective-permute-done.1.rest_6_ = bf16[1,2,128,512]{3,2,1,0:T(8,128)(2,1)S(1)} collective-permute-done((bf16[1,2,128,512]{3,2,1,0:T(8,128)(2,1)S(1)}, bf16[1,2,128,512]{3,2,1,0:T(8,128)(2,1)S(1)}, u32[]{:S(2)}, u32[]{:S(2)}) %collective-permute-start.1) | collective-permute-done | bytes 262176 | tf_op jit(solution)/shard_map/ppermute | solution.py:286
  14.9 1.0 pad_maximum_fusion.1
  15.9 3.8 %collective-permute-start.3 = (bf16[6,1,128,512]{3,2,1,0:T(8,128)(2,1)}, bf16[6,1,128,512]{3,2,1,0:T(8,128)(2,1)}, u32[]{:S(2)}, u32[]{:S(2)}) collective-permute-start(bf16[6,1,128,512]{3,2,1,0:T(8,128)(2,1)} %pad_maximum_fusion.1), channel_id=1, source_target_pairs={{1,0},{2,1},{3,2},{4,3},{5,4},{6,5},{7,6},{9,8},{10,9},{11,10},{12... | collective-permute-start | bytes 2359304 | tf_op jit(solution)/shard_map/ppermute | solution.py:316
  19.7 1.0 pad_maximum_fusion
  20.6 3.4 %collective-permute-start.2 = (bf16[6,1,128,512]{3,2,1,0:T(8,128)(2,1)}, bf16[6,1,128,512]{3,2,1,0:T(8,128)(2,1)}, u32[]{:S(2)}, u32[]{:S(2)}) collective-permute-start(bf16[6,1,128,512]{3,2,1,0:T(8,128)(2,1)} %pad_maximum_fusion), channel_id=1, source_target_pairs={{0,1},{1,2},{2,3},{3,4},{4,5},{5,6},{6,7},{8,9},{9,10},{10,11},{11... | collective-permute-start | bytes 2359304 | tf_op jit(solution)/shard_map/ppermute | solution.py:315
  24.1 1.2 %copy-done = bf16[4,2,128,512]{3,2,1,0:T(8,128)(2,1)S(1)} copy-done((bf16[4,2,128,512]{3,2,1,0:T(8,128)(2,1)S(1)}, bf16[4,2,128,512]{3,2,1,0:T(8,128)(2,1)}, u32[]{:S(2)}) %copy-start) | copy-done | bytes 1048600
  25.3 0.7 copy-done.4
  26.0 0.7 copy-done.6
  26.7 0.7 copy-done.11
  27.3 0.7 copy-done.13
  28.0 0.9 copy-done.18
  28.9 0.9 middle.1
  29.8 0.5 broadcast
  30.4 1.3 %reduce = bf16[128,640]{1,0:T(8,128)(2,1)} reduce(bf16[128,1,640]{2,0,1:T(8,128)(2,1)S(1)} %bitcast.31, bf16[]{:T(256)} %broadcast), dimensions={1}, to_apply=%copy.33.reduce_sub_computation | reduce | bytes 327682 | tf_op jit(solution)/shard_map/all_to_all | solution.py:317
  31.7 1.8 %reshape.76 = bf16[128,2,320]{2,1,0:T(2,128)(2,1)} reshape(bf16[128,640]{1,0:T(8,128)(2,1)} %reduce) | data formatting | bytes 327680
  33.5 21.6 %all_to_all.22 = bf16[128,2,320]{2,1,0:T(2,128)(2,1)} all-to-all(bf16[128,2,320]{2,1,0:T(2,128)(2,1)} %reshape.76), channel_id=1, replica_groups=mesh['gx'=16,'gy'=8] {'gx','gy'}, dimensions={0} | all-to-all | bytes 327680 | tf_op jit(solution)/shard_map/all_to_all | solution.py:317
  55.1 2.3 %reshape.77 = bf16[128,1,640]{2,1,0:T(2,128)(2,1)} reshape(bf16[128,2,320]{2,1,0:T(2,128)(2,1)} %all_to_all.22) | data formatting | bytes 327680
  57.3 1.0 copy.39
  58.4 1.9 %coarse.1 = (bf16[8,512]{1,0:T(8,128)(2,1)}, bf16[128,512]{1,0:T(8,128)(2,1)S(1)}) custom-call(bf16[128,640]{1,0:T(8,128)(2,1)S(1)} %bitcast.32, bf16[8,512]{1,0:T(8,128)(2,1)S(1)} %copy-done.21, bf16[2,512,512]{2,1,0:T(8,128)(2,1)S(1)} %copy-done.15, f32[1,512]{1,0:T(1,128)S(1)} %bitcast.44, bf16[512,512]{1,0:T(8,128)(2,1)S(1)} %copy-done.16, ...), custom_call_target="tpu_custom_call" | custom-call | flops 1000000000 | bytes 9000000 | tf_op jit(solution)/shard_map/coarse/pallas_call | solution.py:268
  60.2 0.7 reduce.1
  60.9 0.7 reshape.78
  61.6 4.5 %all-to-all-start.1 = ((bf16[128,2,256]{2,1,0:T(2,128)(2,1)}), bf16[128,2,256]{2,1,0:T(2,128)(2,1)S(1)}, u32[]{:S(2)}, u32[]{:S(2)}) async-start(bf16[128,2,256]{2,1,0:T(2,128)(2,1)} %reshape.78), calls=%async_computation.1 | async-start | bytes 262144 | tf_op jit(solution)/shard_map/all_to_all | solution.py:327
  66.8 9.1 %all-to-all-done.1 = bf16[128,2,256]{2,1,0:T(2,128)(2,1)S(1)} async-done(((bf16[128,2,256]{2,1,0:T(2,128)(2,1)}), bf16[128,2,256]{2,1,0:T(2,128)(2,1)S(1)}, u32[]{:S(2)}, u32[]{:S(2)}) %all-to-all-start.1) | async-done | bytes 131104 | tf_op jit(solution)/shard_map/all_to_all | solution.py:327
  75.9 0.1 reshape.79
  76.1 1.0 copy-done.17
  77.2 34.2 %edges.1 = (bf16[64,128,512]{2,1,0:T(8,128)(2,1)}, bf16[8,128,512]{2,1,0:T(8,128)(2,1)S(1)}) custom-call(bf16[64,128,512]{2,1,0:T(8,128)(2,1)} %bitcast.51, s32[64,128]{1,0:T(8,128)S(1)} %bitcast.42, s32[1,64]{1,0:T(1,128)S(1)} %bitcast.50, s32[1,1]{1,0:T(1,128)S(6)} %copy.43.rest_2_, s32[64,128]{1,0:T(8,128)S(1)} %bitcast.43, ...), custom_call_target="tpu_custom_call" | custom-call | flops 20000000000 | bytes 100000000 | tf_op jit(solution)/shard_map/edges/pallas_call | solution.py:142
  111.5 4.4 %final.1 = (bf16[8,128,512]{2,1,0:T(8,128)(2,1)}, bf16[128,512]{1,0:T(8,128)(2,1)}) custom-call(bf16[8,128,512]{2,1,0:T(8,128)(2,1)S(1)} %bitcast.29, bf16[8,128,512]{2,1,0:T(8,128)(2,1)S(1)} %get-tuple-element.12.refs_1_, bf16[2,512,512]{2,1,0:T(8,128)(2,1)S(1)} %copy-done.2, f32[1,512]{1,0:T(1,128)S(1)} %bitcast.34, bf16[512,512]{1,0:T(8,128)(2,1)S(1)} %copy-done.3, ...), custom_call_target="tpu_custom_call" | custom-call | flops 1000000000 | bytes 9000000 | tf_op jit(solution)/shard_map/final/pallas_call | solution.py:268
  (56 shorter events, 0.2 us)
Async XLA Ops:
  0.6 57.7 %copy-start.22 = (f32[512]{0:T(512)S(1)}, f32[512]{0:T(512)}, u32[]{:S(2)}) copy-start(f32[512]{0:T(512)} %param.50) | copy-start | bytes 6148
  0.6 57.7 %copy-start.23 = (f32[512]{0:T(512)S(1)}, f32[512]{0:T(512)}, u32[]{:S(2)}) copy-start(f32[512]{0:T(512)} %param.52) | copy-start | bytes 6148
  0.7 57.7 %copy-start.24 = (f32[512]{0:T(512)S(1)}, f32[512]{0:T(512)}, u32[]{:S(2)}) copy-start(f32[512]{0:T(512)} %param.53) | copy-start | bytes 6148
  0.7 57.7 %copy-start.21 = (bf16[8,512]{1,0:T(8,128)(2,1)S(1)}, bf16[8,512]{1,0:T(8,128)(2,1)}, u32[]{:S(2)}) copy-start(bf16[8,512]{1,0:T(8,128)(2,1)} %refs_1_.3) | copy-start | bytes 24580
  0.7 57.7 %copy-start.15 = (bf16[2,512,512]{2,1,0:T(8,128)(2,1)S(1)}, bf16[2,512,512]{2,1,0:T(8,128)(2,1)}, u32[]{:S(2)}) copy-start(bf16[2,512,512]{2,1,0:T(8,128)(2,1)} %refs_2_.4) | copy-start | bytes 3145732
  0.7 57.7 %copy-start.16 = (bf16[512,512]{1,0:T(8,128)(2,1)S(1)}, bf16[512,512]{1,0:T(8,128)(2,1)}, u32[]{:S(2)}) copy-start(bf16[512,512]{1,0:T(8,128)(2,1)} %refs_4_.2) | copy-start | bytes 1572868
  1.9 9.0 %collective-permute-start = (bf16[1,2,128,512]{3,2,1,0:T(8,128)(2,1)S(1)}, bf16[1,2,128,512]{3,2,1,0:T(8,128)(2,1)S(1)}, u32[]{:S(2)}, u32[]{:S(2)}) collective-permute-start(bf16[1,2,128,512]{3,2,1,0:T(8,128)(2,1)S(1)} %get-tuple-element.23), channel_id=1, source_target_pairs={{0,8},{8,16},{16,24},{24,32},{32,40},{40,48},{48,56},{56,64},{64,7... | collective-permute-start | bytes 786440 | tf_op jit(solution)/shard_map/ppermute | solution.py:286
  5.9 70.1 %copy-start.1 = (bf16[4,2,128,512]{3,2,1,0:T(8,128)(2,1)S(1)}, bf16[4,2,128,512]{3,2,1,0:T(8,128)(2,1)}, u32[]{:S(2)}) copy-start(bf16[4,2,128,512]{3,2,1,0:T(8,128)(2,1)} %rest_4_.1) | copy-start | bytes 3145732
  5.9 70.1 %copy-start.19 = (s32[1,1,64,128]{3,2,1,0:T(8,128)S(1)}, s32[1,1,64,128]{3,2,1,0:T(8,128)}, u32[]{:S(2)}) copy-start(s32[1,1,64,128]{3,2,1,0:T(8,128)} %param.31) | copy-start | bytes 98308
  6.0 70.1 %copy-start.20 = (s32[1,1,64,128]{3,2,1,0:T(8,128)S(1)}, s32[1,1,64,128]{3,2,1,0:T(8,128)}, u32[]{:S(2)}) copy-start(s32[1,1,64,128]{3,2,1,0:T(8,128)} %param.33) | copy-start | bytes 98308
  6.0 70.1 %copy-start.25 = (f32[512]{0:T(512)S(1)}, f32[512]{0:T(512)}, u32[]{:S(2)}) copy-start(f32[512]{0:T(512)} %param.40) | copy-start | bytes 6148
  6.0 70.1 %copy-start.26 = (f32[512]{0:T(512)S(1)}, f32[512]{0:T(512)}, u32[]{:S(2)}) copy-start(f32[512]{0:T(512)} %param.42) | copy-start | bytes 6148
  6.0 70.1 %copy-start.27 = (f32[512]{0:T(512)S(1)}, f32[512]{0:T(512)}, u32[]{:S(2)}) copy-start(f32[512]{0:T(512)} %param.43) | copy-start | bytes 6148
  6.0 70.1 %copy-start.28 = (s32[1,1,64]{2,1,0:T(1,128)S(1)}, s32[1,1,64]{2,1,0:T(1,128)}, u32[]{:S(2)}) copy-start(s32[1,1,64]{2,1,0:T(1,128)} %param.32) | copy-start | bytes 772
  6.0 8.9 %collective-permute-start.1 = (bf16[1,2,128,512]{3,2,1,0:T(8,128)(2,1)S(1)}, bf16[1,2,128,512]{3,2,1,0:T(8,128)(2,1)S(1)}, u32[]{:S(2)}, u32[]{:S(2)}) collective-permute-start(bf16[1,2,128,512]{3,2,1,0:T(8,128)(2,1)S(1)} %get-tuple-element.22), channel_id=1, source_target_pairs={{8,0},{16,8},{24,16},{32,24},{40,32},{48,40},{56,48},{64,56},{72,6... | collective-permute-start | bytes 786440 | tf_op jit(solution)/shard_map/ppermute | solution.py:286
  15.9 60.1 %collective-permute-start.3 = (bf16[6,1,128,512]{3,2,1,0:T(8,128)(2,1)}, bf16[6,1,128,512]{3,2,1,0:T(8,128)(2,1)}, u32[]{:S(2)}, u32[]{:S(2)}) collective-permute-start(bf16[6,1,128,512]{3,2,1,0:T(8,128)(2,1)} %pad_maximum_fusion.1), channel_id=1, source_target_pairs={{1,0},{2,1},{3,2},{4,3},{5,4},{6,5},{7,6},{9,8},{10,9},{11,10},{12... | collective-permute-start | bytes 2359304 | tf_op jit(solution)/shard_map/ppermute | solution.py:316
  20.6 55.4 %collective-permute-start.2 = (bf16[6,1,128,512]{3,2,1,0:T(8,128)(2,1)}, bf16[6,1,128,512]{3,2,1,0:T(8,128)(2,1)}, u32[]{:S(2)}, u32[]{:S(2)}) collective-permute-start(bf16[6,1,128,512]{3,2,1,0:T(8,128)(2,1)} %pad_maximum_fusion), channel_id=1, source_target_pairs={{0,1},{1,2},{2,3},{3,4},{4,5},{5,6},{6,7},{8,9},{9,10},{10,11},{11... | collective-permute-start | bytes 2359304 | tf_op jit(solution)/shard_map/ppermute | solution.py:315
  24.1 1.2 %copy-start = (bf16[4,2,128,512]{3,2,1,0:T(8,128)(2,1)S(1)}, bf16[4,2,128,512]{3,2,1,0:T(8,128)(2,1)}, u32[]{:S(2)}) copy-start(bf16[4,2,128,512]{3,2,1,0:T(8,128)(2,1)} %rest_4_.1) | copy-start | bytes 3145732
  25.3 0.7 copy-start.4
  26.0 0.7 copy-start.6
  28.0 0.9 copy-start.18
  61.6 14.2 %all-to-all-start.1 = ((bf16[128,2,256]{2,1,0:T(2,128)(2,1)}), bf16[128,2,256]{2,1,0:T(2,128)(2,1)S(1)}, u32[]{:S(2)}, u32[]{:S(2)}) async-start(bf16[128,2,256]{2,1,0:T(2,128)(2,1)} %reshape.78), calls=%async_computation.1 | async-start | bytes 262144 | tf_op jit(solution)/shard_map/all_to_all | solution.py:327
  76.1 1.0 copy-start.17
  77.1 34.3 %copy-start.2 = (bf16[2,512,512]{2,1,0:T(8,128)(2,1)S(1)}, bf16[2,512,512]{2,1,0:T(8,128)(2,1)}, u32[]{:S(2)}) copy-start(bf16[2,512,512]{2,1,0:T(8,128)(2,1)} %refs_2_.5) | copy-start | bytes 3145732
  77.1 34.3 %copy-start.3 = (bf16[512,512]{1,0:T(8,128)(2,1)S(1)}, bf16[512,512]{1,0:T(8,128)(2,1)}, u32[]{:S(2)}) copy-start(bf16[512,512]{1,0:T(8,128)(2,1)} %refs_4_.3) | copy-start | bytes 1572868
  77.1 34.3 %copy-start.5 = (s32[4,2,128]{2,1,0:T(2,128)S(1)}, s32[4,2,128]{2,1,0:T(2,128)}, u32[]{:S(2)}) copy-start(s32[4,2,128]{2,1,0:T(2,128)} %refs_11_.1) | copy-start | bytes 12292
  77.1 34.3 %copy-start.7 = (f32[4,2,128]{2,1,0:T(2,128)S(1)}, f32[4,2,128]{2,1,0:T(2,128)}, u32[]{:S(2)}) copy-start(f32[4,2,128]{2,1,0:T(2,128)} %refs_12_.1) | copy-start | bytes 12292
  77.1 34.3 %copy-start.8 = (f32[512]{0:T(512)S(1)}, f32[512]{0:T(512)}, u32[]{:S(2)}) copy-start(f32[512]{0:T(512)} %param.45) | copy-start | bytes 6148
  77.1 34.3 %copy-start.9 = (f32[512]{0:T(512)S(1)}, f32[512]{0:T(512)}, u32[]{:S(2)}) copy-start(f32[512]{0:T(512)} %param.47) | copy-start | bytes 6148
  77.2 34.3 %copy-start.10 = (f32[512]{0:T(512)S(1)}, f32[512]{0:T(512)}, u32[]{:S(2)}) copy-start(f32[512]{0:T(512)} %param.48) | copy-start | bytes 6148
  77.2 34.3 %copy-start.12 = (s32[1,1,128]{2,1,0:T(1,128)S(1)}, s32[1,1,128]{2,1,0:T(1,128)}, u32[]{:S(2)}) copy-start(s32[1,1,128]{2,1,0:T(1,128)} %param.37) | copy-start | bytes 1540
  77.2 34.3 %copy-start.14 = (f32[1,1,128]{2,1,0:T(1,128)S(1)}, f32[1,1,128]{2,1,0:T(1,128)}, u32[]{:S(2)}) copy-start(f32[1,1,128]{2,1,0:T(1,128)} %param.38) | copy-start | bytes 1540
  (2 other events, 1.3 us)

commit v3 on v2

--- a/solution.py
+++ b/solution.py
@@ -31,6 +31,10 @@
 
 
 WHOLE = 14
+
+
+def pinned(a):
+    return pltpu.with_memory_space_constraint(a, pltpu.HBM)
 
 
 def bring(whole, held, semaphores):
@@ -201,26 +205,32 @@
     place = mid_parents[...] - owner * coarse_own
     devices = rows_out.shape[0]
     mine = owner == lax.broadcasted_iota(jnp.int32, (devices, count), 0)
-    rows_out[:, :latent] = matmul(mine.astype(jnp.bfloat16), mid).astype(jnp.bfloat16)
+    rows_mine = matmul(mine.astype(jnp.bfloat16), mid)
     weight = jnp.sum(jnp.where(mine, mid_weights[...], 0.0), axis=1, keepdims=True)
     spot = jnp.sum(jnp.where(mine, place.astype(jnp.float32), 0.0), axis=1, keepdims=True)
-    top = weight.astype(jnp.bfloat16).astype(jnp.float32)
-    second = (weight - top).astype(jnp.bfloat16).astype(jnp.float32)
-    lane = lax.broadcasted_iota(jnp.int32, (devices, rows_out.shape[1] - latent), 1)
-    notes = jnp.where(lane == 0, top, jnp.where(lane == 1, second, jnp.where(lane == 2, weight - top - second, spot)))
-    rows_out[:, latent:] = notes.astype(jnp.bfloat16)
+    lane = lax.broadcasted_iota(jnp.int32, (devices, 128), 1)
+    parts = latent // 128
+    for j in range(parts):
+        rows_out[:, j, :] = rows_mine[:, j * 128 : (j + 1) * 128]
+    rows_out[:, parts, :] = jnp.where(lane == 0, weight, spot)
+    for j in range(parts + 1, rows_out.shape[1]):
+        rows_out[:, j, :] = jnp.zeros((devices, 128), jnp.float32)
 
 
 def coarse_kernel(rows_in, coarse, first, bias, second, bias_two, gain, result, answers):
     own_count, latent = coarse.shape
     devices = rows_in.shape[0]
-    notes = rows_in[:, latent:].astype(jnp.float32)
+    parts = latent // 128
+    weight = rows_in[:, parts, :][:, 0:1]
+    spot = rows_in[:, parts, :][:, 1:2]
     lane = lax.broadcasted_iota(jnp.int32, (devices, 128), 1)
-    at_place = notes[:, 3:4] == lane.astype(jnp.float32)
-    rows = rows_in[:, :latent]
+    at_place = spot == lane.astype(jnp.float32)
+    rows = jnp.concatenate([rows_in[:, j, :] for j in range(parts)], axis=1).astype(jnp.bfloat16)
     total = jnp.zeros((128, latent), jnp.float32)
-    for n in range(3):
-        total += matmul_t(jnp.where(at_place, notes[:, n : n + 1], 0.0).astype(jnp.bfloat16), rows)
+    for _ in range(3):
+        top = weight.astype(jnp.bfloat16).astype(jnp.float32)
+        total += matmul_t(jnp.where(at_place, top, 0.0).astype(jnp.bfloat16), rows)
+        weight = weight - top
     summed = total[:own_count].astype(jnp.bfloat16)
     pre = matmul(coarse[...], first[0]) + matmul(summed, first[1]) + bias[...]
     hidden = silu(pre).astype(jnp.bfloat16)
@@ -228,7 +238,9 @@
     new = coarse[...].astype(jnp.float32) + layer_norm(out, gain[...])
     result[...] = new.astype(jnp.bfloat16)
     padded = jnp.concatenate([new, jnp.zeros((128 - own_count, latent), jnp.float32)], axis=0)
-    answers[...] = matmul(at_place.astype(jnp.bfloat16), padded.astype(jnp.bfloat16)).astype(jnp.bfloat16)
+    answer = matmul(at_place.astype(jnp.bfloat16), padded.astype(jnp.bfloat16))
+    for j in range(parts):
+        answers[:, j, :] = answer[:, j * 128 : (j + 1) * 128]
 
 
 def final_kernel(
@@ -243,7 +255,8 @@
     fine_mid = rows.astype(jnp.float32) + layer_norm(out, gain[...])
     devices = from_owners.shape[0]
     mine = mid_parents[...] // coarse_own == lax.broadcasted_iota(jnp.int32, (devices, count), 0)
-    from_coarse = matmul_t(mine.astype(jnp.bfloat16), from_owners[...])
+    answer = jnp.concatenate([from_owners[:, j, :] for j in range(latent // 128)], axis=1)
+    from_coarse = matmul_t(mine.astype(jnp.bfloat16), answer.astype(jnp.bfloat16))
     new_middle = (middle_mid[...].astype(jnp.float32) + column(mid_weights[...]) * from_coarse).astype(jnp.bfloat16)
     middle_result[...] = new_middle
     number = lax.broadcasted_iota(jnp.int32, (count, blk), 0)
@@ -306,29 +319,34 @@
 
     up, down = exchanged(fine_nodes, "gx", 0)
     middle_mid, rows_out = call(
-        middle_kernel, "middle", [like(middle.shape, jnp.bfloat16), like((devices, latent + 128), jnp.bfloat16)],
-        own, fine_parent, fine_weight, middle, mid_parents, mid_weights, coarse_own=coarse_own,
-    )
+        middle_kernel, "middle", [like(middle.shape, jnp.bfloat16), like((devices, 8, 128), jnp.float32)],
+        *map(pinned, (own, fine_parent, fine_weight, middle, mid_parents, mid_weights)), coarse_own=coarse_own,
+    )
+    up, down, middle_mid = lax.optimization_barrier((up, down, middle_mid))
     tall = lambda y: jnp.concatenate([up[:, y : y + 1], fine_nodes[:, y : y + 1], down[:, y : y + 1]], axis=0)
     count = lax.axis_size("gy")
     right_pairs = [(i, i + 1) for i in range(count - 1)]
     left = lax.ppermute(tall(rows_y - 1), "gy", right_pairs)
     right = lax.ppermute(tall(0), "gy", [(j, i) for i, j in right_pairs])
     rows_in = lax.all_to_all(rows_out, BOTH, 0, 0, tiled=True)
+    coarse_result, answers = call(
+        coarse_kernel, "coarse", [like(coarse_nodes.shape, jnp.bfloat16), like((devices, latent // 128, 128), jnp.float32)],
+        rows_in,
+        *map(pinned, (coarse_nodes, coarse_in, row(coarse_bias), coarse_out, row(coarse_bias_two), row(coarse_gain))),
+    )
+    live, answers = lax.optimization_barrier((live_blocks, answers))
     edge_result, aggregate = edge_call(
-        edge_states[0, 0], edge_sources[0, 0], target_blocks[0], live_blocks, target_nodes[0, 0],
-        fine_nodes, up, down, left, right,
-        edge_in, row(edge_bias), edge_out, row(edge_bias_two), row(edge_gain),
-    )
-    coarse_result, answers = call(
-        coarse_kernel, "coarse", [like(coarse_nodes.shape, jnp.bfloat16), like((devices, latent), jnp.bfloat16)],
-        rows_in, coarse_nodes, coarse_in, row(coarse_bias), coarse_out, row(coarse_bias_two), row(coarse_gain),
+        edge_states[0, 0], pinned(edge_sources[0, 0]), pinned(target_blocks[0]), live, pinned(target_nodes[0, 0]),
+        pinned(fine_nodes), up, down, left, right,
+        *map(pinned, (edge_in, row(edge_bias), edge_out, row(edge_bias_two), row(edge_gain))),
     )
     from_owners = lax.all_to_all(answers, BOTH, 0, 0, tiled=True)
     fine_result, middle_result = call(
         final_kernel, "final", [like(own.shape, jnp.bfloat16), like(middle.shape, jnp.bfloat16)],
-        own, aggregate, node_in, row(node_bias), node_out, row(node_bias_two), row(node_gain),
-        middle_mid, from_owners, mid_parents, mid_weights, fine_parent, fine_weight, coarse_own=coarse_own,
+        pinned(own), aggregate,
+        *map(pinned, (node_in, row(node_bias), node_out, row(node_bias_two), row(node_gain))),
+        middle_mid, from_owners,
+        *map(pinned, (mid_parents, mid_weights, fine_parent, fine_weight)), coarse_own=coarse_own,
     )
     return (
         fine_result.reshape(fine_nodes.shape),

time: 117 us -> 96.7 us (0.83)
  blocking collectives: 21.6 us -> 0 us
  starting transfers between devices: 17.1 us -> 31.2 us
  local copies, waits for them, and re-layouts: 14.9 us -> 2.41 us
  Pallas kernels: 41.4 us -> 46.1 us
  other arithmetic: 3.97 us -> 1.95 us
  waiting for transfers between devices: 15.2 us -> 13.3 us
    all_to_all x1 -> x0, blocking collectives: 21.6 us -> none  [body(): rows_in = lax.all_to_all(rows_out, BOTH, 0, 0, tiled=True)]
    all_to_all x0 -> x1, starting transfers between devices: none -> 13.2 us  [body(): rows_in = lax.all_to_all(rows_out, BOTH, 0, 0, tiled=True)]
    all_to_all x0 -> x1, waiting for transfers between devices: none -> 13 us  [body(): rows_in = lax.all_to_all(rows_out, BOTH, 0, 0, tiled=True)]
    unnamed x64 -> x0, local copies, waits for them, and re-layouts: 11.8 us -> none
    all_to_all x1, waiting for transfers between devices: 9.1 us -> 0.01 us  [body(): from_owners = lax.all_to_all(answers, BOTH, 0, 0, tiled=True)]
    ppermute x2, waiting for transfers between devices: 6.11 us -> 0.27 us  [exchanged(): return (lax.ppermute(last, axis, up), lax.ppermute(first, axis, down))]
    pallas_call x3, Pallas kernels: 7.22 us -> 12.3 us  [call(): pl.pallas_call(run, out_shape=out_shape, in_specs=[pl.BlockSpec(memory_sp...]
    ppermute x1, starting transfers between devices: 3.43 us -> 5.53 us  [body(): left = lax.ppermute(tall(rows_y - 1), 'gy', right_pairs)]
  transfers between devices with their start and end apart: 5 -> 6, of which waited for: 3 -> 2; matrix products, arithmetic and copies ran while one was open for 9% -> 2% of each run, Pallas kernels for 2% -> 42%
where the time goes in v3:
time: 96.7 us; the launch traced here: 96.3 us
  Pallas kernels  46.1 us (48%)
  starting transfers between devices  31.2 us (32%)
  waiting for transfers between devices  13.3 us (14%)
  local copies, waits for them, and re-layouts  2.41 us (2%)
  other arithmetic  1.95 us (2%)
  between operations  1.4 us (1%)
    pallas_call x1, Pallas kernels, edge_call(): pl.pallas_call(edge_kernel, grid=(steps,), in_specs=[pl.BlockSpec((per, b...  33.7 us
    all_to_all x1, starting transfers between devices, body(): rows_in = lax.all_to_all(rows_out, BOTH, 0, 0, tiled=True)  13.2 us
    all_to_all x1, waiting for transfers between devices, body(): rows_in = lax.all_to_all(rows_out, BOTH, 0, 0, tiled=True)  13 us
    pallas_call x3, Pallas kernels, call(): pl.pallas_call(run, out_shape=out_shape, in_specs=[pl.BlockSpec(memory_sp...  12.3 us
    ppermute x2, starting transfers between devices, exchanged(): return (lax.ppermute(last, axis, up), lax.ppermute(first, axis, down))  5.97 us
    ppermute x1, starting transfers between devices, body(): left = lax.ppermute(tall(rows_y - 1), 'gy', right_pairs)  5.53 us
    all_to_all x1, starting transfers between devices, body(): from_owners = lax.all_to_all(answers, BOTH, 0, 0, tiled=True)  4.61 us
    concatenate x2, other arithmetic, body(): jnp.concatenate([up[:, y:y + 1], fine_nodes[:, y:y + 1], down[:, y:y + 1]...  1.95 us
  transfers between devices with their start and end apart: 6, of which 2 were waited for; matrix products, arithmetic and copies ran while one was open for 2% of the time, Pallas kernels for 42%

profile of v3, /device:TPU:1, one launch (start us, length us, event | category | flops | bytes accessed | tf_op | source)
XLA Modules:
  0.0 96.3 jit_solution(1091099707708733619)
XLA Ops:
  0.6 1.1 %fusion.1 = (bf16[1,2,128,512]{3,2,1,0:T(8,128)(2,1)S(1)}, bf16[1,2,128,512]{3,2,1,0:T(8,128)(2,1)S(1)}) fusion(bf16[4,2,128,512]{3,2,1,0:T(8,128)(2,1)} %rest_4_.1), kind=kLoop, calls=%fused_computation.3 | loop fusion | bytes 1048576 | tf_op jit(solution)/shard_map/slice | solution.py:298
  1.7 1.3 %collective-permute-start.1 = (bf16[1,2,128,512]{3,2,1,0:T(8,128)(2,1)S(1)}, bf16[1,2,128,512]{3,2,1,0:T(8,128)(2,1)S(1)}, u32[]{:S(2)}, u32[]{:S(2)}) collective-permute-start(bf16[1,2,128,512]{3,2,1,0:T(8,128)(2,1)S(1)} %get-tuple-element.32), channel_id=1, source_target_pairs={{8,0},{16,8},{24,16},{32,24},{40,32},{48,40},{56,48},{64,56},{72,6... | collective-permute-start | bytes 786440 | tf_op jit(solution)/shard_map/ppermute | solution.py:299
  3.0 4.7 %collective-permute-start = (bf16[1,2,128,512]{3,2,1,0:T(8,128)(2,1)S(1)}, bf16[1,2,128,512]{3,2,1,0:T(8,128)(2,1)S(1)}, u32[]{:S(2)}, u32[]{:S(2)}) collective-permute-start(bf16[1,2,128,512]{3,2,1,0:T(8,128)(2,1)S(1)} %get-tuple-element.33), channel_id=1, source_target_pairs={{0,8},{8,16},{16,24},{24,32},{32,40},{40,48},{48,56},{56,64},{64,7... | collective-permute-start | bytes 786440 | tf_op jit(solution)/shard_map/ppermute | solution.py:299
  7.7 2.9 %middle.1 = (bf16[128,512]{1,0:T(8,128)(2,1)S(1)}, f32[128,8,128]{2,1,0:T(8,128)}) custom-call(bf16[8,128,512]{2,1,0:T(8,128)(2,1)} %bitcast.20, s32[4,2,128]{2,1,0:T(2,128)} %refs_11_.1, f32[4,2,128]{2,1,0:T(2,128)} %refs_12_.1, bf16[128,512]{1,0:T(8,128)(2,1)} %bitcast.31, s32[1,128]{1,0:T(1,128)} %bitcast.25, f32[1,128]{1,0:T(1,128)} %bitcast.27), custom_call_target="tpu_custom_call" | custom-call | flops 1000000000 | bytes 9000000 | tf_op jit(solution)/shard_map/middle/pallas_call | solution.py:281
  10.6 1.3 %fusion = (bf16[4,1,128,512]{3,2,1,0:T(8,128)(2,1)S(1)}, bf16[4,1,128,512]{3,2,1,0:T(8,128)(2,1)S(1)}) fusion(bf16[4,2,128,512]{3,2,1,0:T(8,128)(2,1)} %rest_4_.1), kind=kLoop, calls=%fused_computation.2 | loop fusion | bytes 2097152 | tf_op jit(solution)/shard_map/slice | solution.py:326
  11.9 0.0 collective-permute-done.1.rest_6_
  12.0 0.3 collective-permute-done.rest_5_
  12.3 1.0 %pad_maximum_fusion = bf16[6,1,128,512]{3,2,1,0:T(8,128)(2,1)} fusion(bf16[1,1,128,512]{3,2,1,0:T(8,128)(2,1)S(1)} %get-tuple-element.38, bf16[4,1,128,512]{3,2,1,0:T(8,128)(2,1)S(1)} %get-tuple-element.31, bf16[1,1,128,512]{3,2,1,0:T(8,128)(2,1)S(1)} %get-tuple-element.35), kind=kLoop, calls=%fused_computation | loop fusion | flops 786432 | bytes 1572864 | tf_op jit(solution)/shard_map/concatenate | solution.py:326
  13.2 5.5 %collective-permute-start.2 = (bf16[6,1,128,512]{3,2,1,0:T(8,128)(2,1)}, bf16[6,1,128,512]{3,2,1,0:T(8,128)(2,1)S(1)}, u32[]{:S(2)}, u32[]{:S(2)}) collective-permute-start(bf16[6,1,128,512]{3,2,1,0:T(8,128)(2,1)} %pad_maximum_fusion), channel_id=1, source_target_pairs={{0,1},{1,2},{2,3},{3,4},{4,5},{5,6},{6,7},{8,9},{9,10},{10,11},{11... | collective-permute-start | bytes 2359304 | tf_op jit(solution)/shard_map/ppermute | solution.py:329
  18.8 1.0 %pad_maximum_fusion.1 = bf16[6,1,128,512]{3,2,1,0:T(8,128)(2,1)} fusion(bf16[1,1,128,512]{3,2,1,0:T(8,128)(2,1)S(1)} %get-tuple-element.39, bf16[4,1,128,512]{3,2,1,0:T(8,128)(2,1)S(1)} %get-tuple-element.30, bf16[1,1,128,512]{3,2,1,0:T(8,128)(2,1)S(1)} %get-tuple-element.34), kind=kLoop, calls=%fused_computation.1 | loop fusion | flops 786432 | bytes 1572864 | tf_op jit(solution)/shard_map/concatenate | solution.py:326
  19.7 1.9 %collective-permute-start.3 = (bf16[6,1,128,512]{3,2,1,0:T(8,128)(2,1)}, bf16[6,1,128,512]{3,2,1,0:T(8,128)(2,1)S(1)}, u32[]{:S(2)}, u32[]{:S(2)}) collective-permute-start(bf16[6,1,128,512]{3,2,1,0:T(8,128)(2,1)} %pad_maximum_fusion.1), channel_id=1, source_target_pairs={{1,0},{2,1},{3,2},{4,3},{5,4},{6,5},{7,6},{9,8},{10,9},{11,10},{12... | collective-permute-start | bytes 2359304 | tf_op jit(solution)/shard_map/ppermute | solution.py:330
  21.7 13.2 %all-to-all-start = ((f32[128,8,128]{2,1,0:T(8,128)}), f32[128,8,128]{2,1,0:T(8,128)S(1)}, u32[]{:S(2)}, u32[]{:S(2)}) async-start(f32[128,8,128]{2,1,0:T(8,128)} %get-tuple-element.17), calls=%async_computation | async-start | bytes 1048576 | tf_op jit(solution)/shard_map/all_to_all | solution.py:331
  35.5 13.0 %all-to-all-done.refs_0_ = f32[128,8,128]{2,1,0:T(8,128)S(1)} async-done(((f32[128,8,128]{2,1,0:T(8,128)}), f32[128,8,128]{2,1,0:T(8,128)S(1)}, u32[]{:S(2)}, u32[]{:S(2)}) %all-to-all-start) | async-done | bytes 524320 | tf_op jit(solution)/shard_map/all_to_all | solution.py:331
  48.5 3.8 %coarse.1 = (bf16[8,512]{1,0:T(8,128)(2,1)}, f32[128,4,128]{2,1,0:T(4,128)}) custom-call(f32[128,8,128]{2,1,0:T(8,128)S(1)} %all-to-all-done.refs_0_, bf16[8,512]{1,0:T(8,128)(2,1)} %refs_1_.3, bf16[2,512,512]{2,1,0:T(8,128)(2,1)} %refs_2_.4, f32[1,512]{1,0:T(1,128)} %bitcast.35, bf16[512,512]{1,0:T(8,128)(2,1)} %refs_4_.2, f32[1,512]{1,0:T(1,128)} %bitcast.36, ...), custom_call_target="tpu_custom_call" | custom-call | flops 1000000000 | bytes 9000000 | tf_op jit(solution)/shard_map/coarse/pallas_call | solution.py:281
  52.3 4.6 %all-to-all-start.1 = ((f32[128,4,128]{2,1,0:T(4,128)}), f32[128,4,128]{2,1,0:T(4,128)S(1)}, u32[]{:S(2)}, u32[]{:S(2)}) async-start(f32[128,4,128]{2,1,0:T(4,128)} %get-tuple-element.25), calls=%async_computation.1 | async-start | bytes 524288 | tf_op jit(solution)/shard_map/all_to_all | solution.py:343
  56.9 0.0 collective-permute-done.2.rest_7_
  56.9 0.0 collective-permute-done.3.rest_8_
  56.9 33.7 %edges.1 = (bf16[64,128,512]{2,1,0:T(8,128)(2,1)}, bf16[8,128,512]{2,1,0:T(8,128)(2,1)S(1)}) custom-call(bf16[64,128,512]{2,1,0:T(8,128)(2,1)} %bitcast.29, s32[64,128]{1,0:T(8,128)} %bitcast.33, s32[1,64]{1,0:T(1,128)} %bitcast.41, s32[1,1]{1,0:T(1,128)S(6)} %copy.31.rest_2_, s32[64,128]{1,0:T(8,128)} %bitcast.34, bf16[4,2,128,512]{3,2,1,0:T(8,128)(2,1)} %rest_4_.1, ...), custom_call_target="tpu_custom_call" | custom-call | flops 20000000000 | bytes 100000000 | tf_op jit(solution)/shard_map/edges/pallas_call | solution.py:146
  90.7 0.0 all-to-all-done.1.refs_8_
  90.7 5.6 %final.1 = (bf16[8,128,512]{2,1,0:T(8,128)(2,1)}, bf16[128,512]{1,0:T(8,128)(2,1)}) custom-call(bf16[8,128,512]{2,1,0:T(8,128)(2,1)} %bitcast.21, bf16[8,128,512]{2,1,0:T(8,128)(2,1)S(1)} %get-tuple-element.23.refs_1_, bf16[2,512,512]{2,1,0:T(8,128)(2,1)} %refs_2_.5, f32[1,512]{1,0:T(1,128)} %bitcast.22, bf16[512,512]{1,0:T(8,128)(2,1)} %refs_4_.3, ...), custom_call_target="tpu_custom_call" | custom-call | flops 1000000000 | bytes 9000000 | tf_op jit(solution)/shard_map/final/pallas_call | solution.py:281
  (1 shorter events, 0.0 us)
Async XLA Ops:
  1.7 10.2 %collective-permute-start.1 = (bf16[1,2,128,512]{3,2,1,0:T(8,128)(2,1)S(1)}, bf16[1,2,128,512]{3,2,1,0:T(8,128)(2,1)S(1)}, u32[]{:S(2)}, u32[]{:S(2)}) collective-permute-start(bf16[1,2,128,512]{3,2,1,0:T(8,128)(2,1)S(1)} %get-tuple-element.32), channel_id=1, source_target_pairs={{8,0},{16,8},{24,16},{32,24},{40,32},{48,40},{56,48},{64,56},{72,6... | collective-permute-start | bytes 786440 | tf_op jit(solution)/shard_map/ppermute | solution.py:299
  3.0 9.2 %collective-permute-start = (bf16[1,2,128,512]{3,2,1,0:T(8,128)(2,1)S(1)}, bf16[1,2,128,512]{3,2,1,0:T(8,128)(2,1)S(1)}, u32[]{:S(2)}, u32[]{:S(2)}) collective-permute-start(bf16[1,2,128,512]{3,2,1,0:T(8,128)(2,1)S(1)} %get-tuple-element.33), channel_id=1, source_target_pairs={{0,8},{8,16},{16,24},{24,32},{32,40},{40,48},{48,56},{56,64},{64,7... | collective-permute-start | bytes 786440 | tf_op jit(solution)/shard_map/ppermute | solution.py:299
  13.2 43.7 %collective-permute-start.2 = (bf16[6,1,128,512]{3,2,1,0:T(8,128)(2,1)}, bf16[6,1,128,512]{3,2,1,0:T(8,128)(2,1)S(1)}, u32[]{:S(2)}, u32[]{:S(2)}) collective-permute-start(bf16[6,1,128,512]{3,2,1,0:T(8,128)(2,1)} %pad_maximum_fusion), channel_id=1, source_target_pairs={{0,1},{1,2},{2,3},{3,4},{4,5},{5,6},{6,7},{8,9},{9,10},{10,11},{11... | collective-permute-start | bytes 2359304 | tf_op jit(solution)/shard_map/ppermute | solution.py:329
  19.7 37.2 %collective-permute-start.3 = (bf16[6,1,128,512]{3,2,1,0:T(8,128)(2,1)}, bf16[6,1,128,512]{3,2,1,0:T(8,128)(2,1)S(1)}, u32[]{:S(2)}, u32[]{:S(2)}) collective-permute-start(bf16[6,1,128,512]{3,2,1,0:T(8,128)(2,1)} %pad_maximum_fusion.1), channel_id=1, source_target_pairs={{1,0},{2,1},{3,2},{4,3},{5,4},{6,5},{7,6},{9,8},{10,9},{11,10},{12... | collective-permute-start | bytes 2359304 | tf_op jit(solution)/shard_map/ppermute | solution.py:330
  21.7 26.8 %all-to-all-start = ((f32[128,8,128]{2,1,0:T(8,128)}), f32[128,8,128]{2,1,0:T(8,128)S(1)}, u32[]{:S(2)}, u32[]{:S(2)}) async-start(f32[128,8,128]{2,1,0:T(8,128)} %get-tuple-element.17), calls=%async_computation | async-start | bytes 1048576 | tf_op jit(solution)/shard_map/all_to_all | solution.py:331
  52.3 38.4 %all-to-all-start.1 = ((f32[128,4,128]{2,1,0:T(4,128)}), f32[128,4,128]{2,1,0:T(4,128)S(1)}, u32[]{:S(2)}, u32[]{:S(2)}) async-start(f32[128,4,128]{2,1,0:T(4,128)} %get-tuple-element.25), calls=%async_computation.1 | async-start | bytes 524288 | tf_op jit(solution)/shard_map/all_to_all | solution.py:343

commit v4 on v3

--- a/solution.py
+++ b/solution.py
@@ -93,8 +93,7 @@
 
     number = lax.broadcasted_iota(jnp.int32, (blk, blk), 0)
 
-    def compute(half, b_next):
-        chunk = 2 * step + half
+    def begin(half, b_next):
         ref = picked[half]
         base = half * SUB
         states = edges[base : base + SUB].reshape(SUB * blk, latent)
@@ -103,7 +102,7 @@
         spots = []
         for b in range(SUB):
             b_next(b)
-            block = chunk * SUB + b
+            block = (2 * step + half) * SUB + b
             to = target_blocks[0, block]
             spot = (target_nodes[pl.ds(block, 1), :] == number).astype(jnp.bfloat16)
             spots.append((to, spot))
@@ -114,10 +113,13 @@
             hidden.append(
                 silu(pre[b * blk : (b + 1) * blk] + from_target + from_source).astype(jnp.bfloat16)
             )
-        out = matmul(jnp.concatenate(hidden, axis=0), second[...]) + bias_two[...]
+        return jnp.concatenate(hidden, axis=0), spots
+
+    def finish(half, out, spots):
+        base = half * SUB
         for b in range(SUB):
             rows = out[b * blk : (b + 1) * blk]
-            block = chunk * SUB + b
+            block = (2 * step + half) * SUB + b
             alive = jnp.where(block < live[0, 0], 1.0, 0.0)
             centred = rows - jnp.mean(rows, axis=-1, keepdims=True)
             spread = jnp.mean(centred * centred, axis=-1, keepdims=True)
@@ -126,8 +128,12 @@
             to, spot = spots[b]
             sums[to] += matmul(spot, message)
 
-    compute(0, lambda b: gather(2 * step + 1, b, picked_b))
-    compute(1, lambda b: gather(jnp.minimum(2 * step + 2, chunks - 1), b, picked_a))
+    hidden_a, spots_a = begin(0, lambda b: gather(2 * step + 1, b, picked_b))
+    out_a = matmul(hidden_a, second[...]) + bias_two[...]
+    hidden_b, spots_b = begin(1, lambda b: gather(jnp.minimum(2 * step + 2, chunks - 1), b, picked_a))
+    out_b = matmul(hidden_b, second[...]) + bias_two[...]
+    finish(0, out_a, spots_a)
+    finish(1, out_b, spots_b)
 
     @pl.when(step == steps - 1)
     def _():
@@ -243,16 +249,21 @@
         answers[:, j, :] = answer[:, j * 128 : (j + 1) * 128]
 
 
-def final_kernel(
-    own, aggregate, first, bias, second, bias_two, gain,
-    middle_mid, from_owners, mid_parents, mid_weights, parents, weights, fine_result, middle_result, *, coarse_own,
-):
+def node_kernel(own, aggregate, first, bias, second, bias_two, gain, fine_mid):
     blocks, blk, latent = own.shape
-    count = middle_mid.shape[0]
     rows = own[...].reshape(blocks * blk, latent)
     pre = matmul(rows, first[0]) + matmul(aggregate[...].reshape(blocks * blk, latent), first[1]) + bias[...]
     out = matmul(silu(pre).astype(jnp.bfloat16), second[...]) + bias_two[...]
-    fine_mid = rows.astype(jnp.float32) + layer_norm(out, gain[...])
+    new = rows.astype(jnp.float32) + layer_norm(out, gain[...])
+    fine_mid[...] = new.reshape(fine_mid.shape)
+
+
+def final_kernel(
+    fine_mid, middle_mid, from_owners, mid_parents, mid_weights, parents, weights,
+    fine_result, middle_result, *, coarse_own,
+):
+    blocks, blk, latent = fine_mid.shape
+    count = middle_mid.shape[0]
     devices = from_owners.shape[0]
     mine = mid_parents[...] // coarse_own == lax.broadcasted_iota(jnp.int32, (devices, count), 0)
     answer = jnp.concatenate([from_owners[:, j, :] for j in range(latent // 128)], axis=1)
@@ -265,7 +276,7 @@
         x, y = b // wide, b % wide
         from_middle = matmul_t((parents[x, y : y + 1, :] == number).astype(jnp.bfloat16), new_middle)
         fine_result[b] = (
-            fine_mid[b * blk : (b + 1) * blk] + column(weights[x, y : y + 1, :]) * from_middle
+            fine_mid[b] + column(weights[x, y : y + 1, :]) * from_middle
         ).astype(jnp.bfloat16)
 
 
@@ -329,23 +340,26 @@
     left = lax.ppermute(tall(rows_y - 1), "gy", right_pairs)
     right = lax.ppermute(tall(0), "gy", [(j, i) for i, j in right_pairs])
     rows_in = lax.all_to_all(rows_out, BOTH, 0, 0, tiled=True)
+    edge_result, aggregate = edge_call(
+        edge_states[0, 0], pinned(edge_sources[0, 0]), pinned(target_blocks[0]), live_blocks, pinned(target_nodes[0, 0]),
+        pinned(fine_nodes), up, down, pinned(left), pinned(right),
+        *map(pinned, (edge_in, row(edge_bias), edge_out, row(edge_bias_two), row(edge_gain))),
+    )
+    rows_in, aggregate = lax.optimization_barrier((rows_in, aggregate))
     coarse_result, answers = call(
         coarse_kernel, "coarse", [like(coarse_nodes.shape, jnp.bfloat16), like((devices, latent // 128, 128), jnp.float32)],
         rows_in,
         *map(pinned, (coarse_nodes, coarse_in, row(coarse_bias), coarse_out, row(coarse_bias_two), row(coarse_gain))),
     )
-    live, answers = lax.optimization_barrier((live_blocks, answers))
-    edge_result, aggregate = edge_call(
-        edge_states[0, 0], pinned(edge_sources[0, 0]), pinned(target_blocks[0]), live, pinned(target_nodes[0, 0]),
-        pinned(fine_nodes), up, down, left, right,
-        *map(pinned, (edge_in, row(edge_bias), edge_out, row(edge_bias_two), row(edge_gain))),
-    )
     from_owners = lax.all_to_all(answers, BOTH, 0, 0, tiled=True)
+    (fine_mid,) = call(
+        node_kernel, "nodes", [like(own.shape, jnp.float32)],
+        pinned(own), aggregate,
+        *map(pinned, (node_in, row(node_bias), node_out, row(node_bias_two), row(node_gain))),
+    )
     fine_result, middle_result = call(
         final_kernel, "final", [like(own.shape, jnp.bfloat16), like(middle.shape, jnp.bfloat16)],
-        pinned(own), aggregate,
-        *map(pinned, (node_in, row(node_bias), node_out, row(node_bias_two), row(node_gain))),
-        middle_mid, from_owners,
+        fine_mid, middle_mid, from_owners,
         *map(pinned, (mid_parents, mid_weights, fine_parent, fine_weight)), coarse_own=coarse_own,
     )
     return (

time: 96.7 us -> 102 us (1.055)
  starting transfers between devices: 31.2 us -> 42.4 us
  waiting for transfers between devices: 13.3 us -> 6.96 us
    all_to_all x1, waiting for transfers between devices: 13 us -> 0.01 us  [body(): rows_in = lax.all_to_all(rows_out, BOTH, 0, 0, tiled=True)]
    all_to_all x1, starting transfers between devices: 4.61 us -> 15.8 us  [body(): from_owners = lax.all_to_all(answers, BOTH, 0, 0, tiled=True)]
    all_to_all x1, waiting for transfers between devices: 0.01 us -> 6.71 us  [body(): from_owners = lax.all_to_all(answers, BOTH, 0, 0, tiled=True)]
    pallas_call x3 -> x4, Pallas kernels: 12.3 us -> 13.7 us  [call(): pl.pallas_call(run, out_shape=out_shape, in_specs=[pl.BlockSpec(memory_sp...]
  transfers between devices with their start and end apart: 6 -> 6, of which waited for: 2 -> 2; matrix products, arithmetic and copies ran while one was open for 2% -> 2% of each run, Pallas kernels for 42% -> 39%
where the time goes in v4:
time: 102 us
  Pallas kernels  46.5 us (46%)
  starting transfers between devices  42.4 us (42%)
  waiting for transfers between devices  6.96 us (7%)
  local copies, waits for them, and re-layouts  3.28 us (3%)
  between operations  1.42 us (1%)
  other arithmetic  1.07 us (1%)
    pallas_call x1, Pallas kernels, edge_call(): pl.pallas_call(edge_kernel, grid=(steps,), in_specs=[pl.BlockSpec((per, b...  32.8 us
    all_to_all x1, starting transfers between devices, body(): from_owners = lax.all_to_all(answers, BOTH, 0, 0, tiled=True)  15.8 us
    pallas_call x4, Pallas kernels, call(): pl.pallas_call(run, out_shape=out_shape, in_specs=[pl.BlockSpec(memory_sp...  13.7 us
    all_to_all x1, starting transfers between devices, body(): rows_in = lax.all_to_all(rows_out, BOTH, 0, 0, tiled=True)  13.2 us
    all_to_all x1, waiting for transfers between devices, body(): from_owners = lax.all_to_all(answers, BOTH, 0, 0, tiled=True)  6.71 us
    ppermute x2, starting transfers between devices, exchanged(): return (lax.ppermute(last, axis, up), lax.ppermute(first, axis, down))  5.97 us
    ppermute x1, starting transfers between devices, body(): left = lax.ppermute(tall(rows_y - 1), 'gy', right_pairs)  5.54 us
  transfers between devices with their start and end apart: 6, of which 2 were waited for; matrix products, arithmetic and copies ran while one was open for 2% of the time, Pallas kernels for 39%

profile of v4, /device:TPU:1, one launch (start us, length us, event | category | flops | bytes accessed | tf_op | source)
XLA Modules:
  0.0 101.6 jit_solution(9439762426427859122)
XLA Ops:
  0.6 1.1 %fusion.1 = (bf16[1,2,128,512]{3,2,1,0:T(8,128)(2,1)S(1)}, bf16[1,2,128,512]{3,2,1,0:T(8,128)(2,1)S(1)}) fusion(bf16[4,2,128,512]{3,2,1,0:T(8,128)(2,1)} %rest_4_.1), kind=kLoop, calls=%fused_computation.3 | loop fusion | bytes 1048576 | tf_op jit(solution)/shard_map/slice | solution.py:309
  1.7 1.3 %collective-permute-start.1 = (bf16[1,2,128,512]{3,2,1,0:T(8,128)(2,1)S(1)}, bf16[1,2,128,512]{3,2,1,0:T(8,128)(2,1)S(1)}, u32[]{:S(2)}, u32[]{:S(2)}) collective-permute-start(bf16[1,2,128,512]{3,2,1,0:T(8,128)(2,1)S(1)} %get-tuple-element.32), channel_id=1, source_target_pairs={{8,0},{16,8},{24,16},{32,24},{40,32},{48,40},{56,48},{64,56},{72,6... | collective-permute-start | bytes 786440 | tf_op jit(solution)/shard_map/ppermute | solution.py:310
  3.0 4.7 %collective-permute-start = (bf16[1,2,128,512]{3,2,1,0:T(8,128)(2,1)S(1)}, bf16[1,2,128,512]{3,2,1,0:T(8,128)(2,1)S(1)}, u32[]{:S(2)}, u32[]{:S(2)}) collective-permute-start(bf16[1,2,128,512]{3,2,1,0:T(8,128)(2,1)S(1)} %get-tuple-element.33), channel_id=1, source_target_pairs={{0,8},{8,16},{16,24},{24,32},{32,40},{40,48},{48,56},{56,64},{64,7... | collective-permute-start | bytes 786440 | tf_op jit(solution)/shard_map/ppermute | solution.py:310
  7.7 3.0 %middle.1 = (bf16[128,512]{1,0:T(8,128)(2,1)S(1)}, f32[128,8,128]{2,1,0:T(8,128)}) custom-call(bf16[8,128,512]{2,1,0:T(8,128)(2,1)} %bitcast.20, s32[4,2,128]{2,1,0:T(2,128)} %refs_5_.1, f32[4,2,128]{2,1,0:T(2,128)} %refs_6_.1, bf16[128,512]{1,0:T(8,128)(2,1)} %bitcast.26, s32[1,128]{1,0:T(1,128)} %bitcast.36, f32[1,128]{1,0:T(1,128)} %bitcast.38), custom_call_target="tpu_custom_call" | custom-call | flops 1000000000 | bytes 9000000 | tf_op jit(solution)/shard_map/middle/pallas_call | solution.py:292
  10.7 1.3 %fusion = (bf16[4,1,128,512]{3,2,1,0:T(8,128)(2,1)S(1)}, bf16[4,1,128,512]{3,2,1,0:T(8,128)(2,1)S(1)}) fusion(bf16[4,2,128,512]{3,2,1,0:T(8,128)(2,1)} %rest_4_.1), kind=kLoop, calls=%fused_computation.2 | loop fusion | bytes 2097152 | tf_op jit(solution)/shard_map/slice | solution.py:337
  12.0 0.0 collective-permute-done.1.rest_6_
  12.0 0.2 collective-permute-done.rest_5_
  12.3 0.1 pad_maximum_fusion
  12.4 5.5 %collective-permute-start.2 = (bf16[6,1,128,512]{3,2,1,0:T(8,128)(2,1)S(1)}, bf16[6,1,128,512]{3,2,1,0:T(8,128)(2,1)}, u32[]{:S(2)}, u32[]{:S(2)}) collective-permute-start(bf16[6,1,128,512]{3,2,1,0:T(8,128)(2,1)S(1)} %pad_maximum_fusion), channel_id=1, source_target_pairs={{0,1},{1,2},{2,3},{3,4},{4,5},{5,6},{6,7},{8,9},{9,10},{10,11},{11... | collective-permute-start | bytes 2359304 | tf_op jit(solution)/shard_map/ppermute | solution.py:340
  17.9 1.0 pad_maximum_fusion.1
  18.9 1.9 %collective-permute-start.3 = (bf16[6,1,128,512]{3,2,1,0:T(8,128)(2,1)}, bf16[6,1,128,512]{3,2,1,0:T(8,128)(2,1)S(1)}, u32[]{:S(2)}, u32[]{:S(2)}) collective-permute-start(bf16[6,1,128,512]{3,2,1,0:T(8,128)(2,1)} %pad_maximum_fusion.1), channel_id=1, source_target_pairs={{1,0},{2,1},{3,2},{4,3},{5,4},{6,5},{7,6},{9,8},{10,9},{11,10},{12... | collective-permute-start | bytes 2359304 | tf_op jit(solution)/shard_map/ppermute | solution.py:341
  20.8 13.2 %all-to-all-start = ((f32[128,8,128]{2,1,0:T(8,128)}), f32[128,8,128]{2,1,0:T(8,128)S(1)}, u32[]{:S(2)}, u32[]{:S(2)}) async-start(f32[128,8,128]{2,1,0:T(8,128)} %get-tuple-element.17), calls=%async_computation | async-start | bytes 1048576 | tf_op jit(solution)/shard_map/all_to_all | solution.py:342
  34.6 0.0 collective-permute-done.2.rest_7_
  34.6 0.0 collective-permute-done.3.rest_8_
  34.6 0.0 copy-start
  34.6 0.9 copy-done
  35.5 32.8 %edges.1 = (bf16[64,128,512]{2,1,0:T(8,128)(2,1)}, bf16[8,128,512]{2,1,0:T(8,128)(2,1)S(1)}) custom-call(bf16[64,128,512]{2,1,0:T(8,128)(2,1)} %bitcast.25, s32[64,128]{1,0:T(8,128)} %bitcast.27, s32[1,64]{1,0:T(1,128)} %bitcast.35, s32[1,1]{1,0:T(1,128)S(6)} %copy.31.rest_2_, s32[64,128]{1,0:T(8,128)} %bitcast.28, bf16[4,2,128,512]{3,2,1,0:T(8,128)(2,1)} %rest_4_.1, ...), custom_call_target="tpu_custom_call" | custom-call | flops 20000000000 | bytes 100000000 | tf_op jit(solution)/shard_map/edges/pallas_call | solution.py:152
  68.3 0.0 all-to-all-done.refs_0_
  68.3 3.8 %coarse.1 = (bf16[8,512]{1,0:T(8,128)(2,1)}, f32[128,4,128]{2,1,0:T(4,128)}) custom-call(f32[128,8,128]{2,1,0:T(8,128)S(1)} %all-to-all-done.refs_0_, bf16[8,512]{1,0:T(8,128)(2,1)} %refs_1_.3, bf16[2,512,512]{2,1,0:T(8,128)(2,1)} %refs_2_.5, f32[1,512]{1,0:T(1,128)} %bitcast.32, bf16[512,512]{1,0:T(8,128)(2,1)} %refs_4_.3, f32[1,512]{1,0:T(1,128)} %bitcast.33, ...), custom_call_target="tpu_custom_call" | custom-call | flops 1000000000 | bytes 9000000 | tf_op jit(solution)/shard_map/coarse/pallas_call | solution.py:292
  72.1 15.8 %all-to-all-start.1 = ((f32[128,4,128]{2,1,0:T(4,128)}), f32[128,4,128]{2,1,0:T(4,128)S(1)}, u32[]{:S(2)}, u32[]{:S(2)}) async-start(f32[128,4,128]{2,1,0:T(4,128)} %get-tuple-element.25), calls=%async_computation.1 | async-start | bytes 524288 | tf_op jit(solution)/shard_map/all_to_all | solution.py:354
  87.9 4.2 %nodes.1.refs_0_ = f32[8,128,512]{2,1,0:T(8,128)S(1)} custom-call(bf16[8,128,512]{2,1,0:T(8,128)(2,1)} %bitcast.21, bf16[8,128,512]{2,1,0:T(8,128)(2,1)S(1)} %get-tuple-element.22.refs_1_, bf16[2,512,512]{2,1,0:T(8,128)(2,1)} %refs_2_.4, f32[1,512]{1,0:T(1,128)} %bitcast.22, bf16[512,512]{1,0:T(8,128)(2,1)} %refs_4_.2, f32[1,512]{1,0:T(1,128)} %bitcast.23, ...), custom_call_target="tpu_custom_call" | custom-call | flops 1000000000 | bytes 9000000 | tf_op jit(solution)/shard_map/nodes/pallas_call | solution.py:292
  92.1 6.7 %all-to-all-done.1.refs_2_ = f32[128,4,128]{2,1,0:T(4,128)S(1)} async-done(((f32[128,4,128]{2,1,0:T(4,128)}), f32[128,4,128]{2,1,0:T(4,128)S(1)}, u32[]{:S(2)}, u32[]{:S(2)}) %all-to-all-start.1) | async-done | bytes 262176 | tf_op jit(solution)/shard_map/all_to_all | solution.py:354
  98.8 2.8 %final.1 = (bf16[8,128,512]{2,1,0:T(8,128)(2,1)}, bf16[128,512]{1,0:T(8,128)(2,1)}) custom-call(f32[8,128,512]{2,1,0:T(8,128)S(1)} %nodes.1.refs_0_, bf16[128,512]{1,0:T(8,128)(2,1)S(1)} %get-tuple-element.23.refs_1_, f32[128,4,128]{2,1,0:T(4,128)S(1)} %all-to-all-done.1.refs_2_, s32[1,128]{1,0:T(1,128)} %bitcast.37, f32[1,128]{1,0:T(1,128)} %bitcast.39, ...), custom_call_target="tpu_custom_call" | custom-call | flops 1000000000 | bytes 9000000 | tf_op jit(solution)/shard_map/final/pallas_call | solution.py:292
  (1 shorter events, 0.0 us)
Async XLA Ops:
  1.7 10.3 %collective-permute-start.1 = (bf16[1,2,128,512]{3,2,1,0:T(8,128)(2,1)S(1)}, bf16[1,2,128,512]{3,2,1,0:T(8,128)(2,1)S(1)}, u32[]{:S(2)}, u32[]{:S(2)}) collective-permute-start(bf16[1,2,128,512]{3,2,1,0:T(8,128)(2,1)S(1)} %get-tuple-element.32), channel_id=1, source_target_pairs={{8,0},{16,8},{24,16},{32,24},{40,32},{48,40},{56,48},{64,56},{72,6... | collective-permute-start | bytes 786440 | tf_op jit(solution)/shard_map/ppermute | solution.py:310
  3.0 9.2 %collective-permute-start = (bf16[1,2,128,512]{3,2,1,0:T(8,128)(2,1)S(1)}, bf16[1,2,128,512]{3,2,1,0:T(8,128)(2,1)S(1)}, u32[]{:S(2)}, u32[]{:S(2)}) collective-permute-start(bf16[1,2,128,512]{3,2,1,0:T(8,128)(2,1)S(1)} %get-tuple-element.33), channel_id=1, source_target_pairs={{0,8},{8,16},{16,24},{24,32},{32,40},{40,48},{48,56},{56,64},{64,7... | collective-permute-start | bytes 786440 | tf_op jit(solution)/shard_map/ppermute | solution.py:310
  12.4 22.3 %collective-permute-start.2 = (bf16[6,1,128,512]{3,2,1,0:T(8,128)(2,1)S(1)}, bf16[6,1,128,512]{3,2,1,0:T(8,128)(2,1)}, u32[]{:S(2)}, u32[]{:S(2)}) collective-permute-start(bf16[6,1,128,512]{3,2,1,0:T(8,128)(2,1)S(1)} %pad_maximum_fusion), channel_id=1, source_target_pairs={{0,1},{1,2},{2,3},{3,4},{4,5},{5,6},{6,7},{8,9},{9,10},{10,11},{11... | collective-permute-start | bytes 2359304 | tf_op jit(solution)/shard_map/ppermute | solution.py:340
  18.9 15.7 %collective-permute-start.3 = (bf16[6,1,128,512]{3,2,1,0:T(8,128)(2,1)}, bf16[6,1,128,512]{3,2,1,0:T(8,128)(2,1)S(1)}, u32[]{:S(2)}, u32[]{:S(2)}) collective-permute-start(bf16[6,1,128,512]{3,2,1,0:T(8,128)(2,1)} %pad_maximum_fusion.1), channel_id=1, source_target_pairs={{1,0},{2,1},{3,2},{4,3},{5,4},{6,5},{7,6},{9,8},{10,9},{11,10},{12... | collective-permute-start | bytes 2359304 | tf_op jit(solution)/shard_map/ppermute | solution.py:341
  20.8 47.5 %all-to-all-start = ((f32[128,8,128]{2,1,0:T(8,128)}), f32[128,8,128]{2,1,0:T(8,128)S(1)}, u32[]{:S(2)}, u32[]{:S(2)}) async-start(f32[128,8,128]{2,1,0:T(8,128)} %get-tuple-element.17), calls=%async_computation | async-start | bytes 1048576 | tf_op jit(solution)/shard_map/all_to_all | solution.py:342
  34.6 0.9 copy-start
  72.1 26.7 %all-to-all-start.1 = ((f32[128,4,128]{2,1,0:T(4,128)}), f32[128,4,128]{2,1,0:T(4,128)S(1)}, u32[]{:S(2)}, u32[]{:S(2)}) async-start(f32[128,4,128]{2,1,0:T(4,128)} %get-tuple-element.25), calls=%async_computation.1 | async-start | bytes 524288 | tf_op jit(solution)/shard_map/all_to_all | solution.py:354

commit v5 on v3

--- a/solution.py
+++ b/solution.py
@@ -46,20 +46,22 @@
 
 
 def edge_kernel(
-    edges, *rest
+    edges, *rest, start, carried
 ):
+    given = rest[WHOLE : WHOLE + 2] if carried else ()
+    rest = rest[:WHOLE] + rest[WHOLE + len(given) :]
     whole, (result, aggregate, table, targets, sums, picked_a, picked_b), held, semaphores = (
         rest[:WHOLE], rest[WHOLE : WHOLE + 7], rest[WHOLE + 7 : -1], rest[-1]
     )
     (sources, target_blocks, live, target_nodes, own, up, down, left, right, first, bias, second, bias_two, gain) = held
-    step = pl.program_id(0)
+    step = pl.program_id(0) + start
     steps = pl.num_programs(0)
     picked = (picked_a, picked_b)
     latent = own.shape[-1]
     lanes = 128
     parts = latent // lanes
     blk = 128
-    chunks = 2 * steps
+    chunks = 2 * (start + steps)
 
     def project(piece, places):
         rows = matmul(piece, first[1]) + bias[...]
@@ -75,7 +77,7 @@
             at = pl.multiple_of(sources[block, e] * parts, parts)
             into[pl.ds((b * blk + e) * parts, parts), :] = table[pl.ds(at, parts), :]
 
-    @pl.when(step == 0)
+    @pl.when(step == start)
     def _():
         bring(whole, held, semaphores)
         rows_x, rows_y = own.shape[0], own.shape[1]
@@ -87,14 +89,16 @@
         project(left[...].reshape(-1, latent), [x * wide for x in range(rows_x + 2)])
         project(right[...].reshape(-1, latent), [x * wide + wide - 1 for x in range(rows_x + 2)])
         targets[...] = matmul(own_rows, first[2]).astype(jnp.bfloat16).reshape(targets.shape)
-        sums[...] = jnp.zeros_like(sums)
+        if carried:
+            pltpu.sync_copy(given[0], sums)
+        else:
+            sums[...] = jnp.zeros_like(sums)
         for b in range(SUB):
-            gather(0, b, picked_a)
+            gather(2 * start, b, picked_a)
 
     number = lax.broadcasted_iota(jnp.int32, (blk, blk), 0)
 
-    def compute(half, b_next):
-        chunk = 2 * step + half
+    def begin(half, b_next):
         ref = picked[half]
         base = half * SUB
         states = edges[base : base + SUB].reshape(SUB * blk, latent)
@@ -103,7 +107,7 @@
         spots = []
         for b in range(SUB):
             b_next(b)
-            block = chunk * SUB + b
+            block = (2 * step + half) * SUB + b
             to = target_blocks[0, block]
             spot = (target_nodes[pl.ds(block, 1), :] == number).astype(jnp.bfloat16)
             spots.append((to, spot))
@@ -114,10 +118,13 @@
             hidden.append(
                 silu(pre[b * blk : (b + 1) * blk] + from_target + from_source).astype(jnp.bfloat16)
             )
-        out = matmul(jnp.concatenate(hidden, axis=0), second[...]) + bias_two[...]
+        return jnp.concatenate(hidden, axis=0), spots
+
+    def finish(half, out, spots):
+        base = half * SUB
         for b in range(SUB):
             rows = out[b * blk : (b + 1) * blk]
-            block = chunk * SUB + b
+            block = (2 * step + half) * SUB + b
             alive = jnp.where(block < live[0, 0], 1.0, 0.0)
             centred = rows - jnp.mean(rows, axis=-1, keepdims=True)
             spread = jnp.mean(centred * centred, axis=-1, keepdims=True)
@@ -126,30 +133,33 @@
             to, spot = spots[b]
             sums[to] += matmul(spot, message)
 
-    compute(0, lambda b: gather(2 * step + 1, b, picked_b))
-    compute(1, lambda b: gather(jnp.minimum(2 * step + 2, chunks - 1), b, picked_a))
-
-    @pl.when(step == steps - 1)
+    hidden_a, spots_a = begin(0, lambda b: gather(2 * step + 1, b, picked_b))
+    out_a = matmul(hidden_a, second[...]) + bias_two[...]
+    hidden_b, spots_b = begin(1, lambda b: gather(jnp.minimum(2 * step + 2, chunks - 1), b, picked_a))
+    out_b = matmul(hidden_b, second[...]) + bias_two[...]
+    finish(0, out_a, spots_a)
+    finish(1, out_b, spots_b)
+
+    @pl.when(step == start + steps - 1)
     def _():
         aggregate[...] = sums[...].astype(aggregate.dtype)
 
 
-def edge_call(edges, *whole):
+def edge_call(edges, *whole, start, steps, given=()):
     count, blk, latent = edges.shape
     per = 2 * SUB
-    steps = count // per
     rows_x, rows_y = whole[4].shape[:2]
     own_blocks = rows_x * rows_y
     window = (rows_x + 2) * (rows_y + 2)
     table = window * blk * latent // 128
     picked = SUB * blk * latent // 128
     return pl.pallas_call(
-        edge_kernel,
+        functools.partial(edge_kernel, start=start, carried=bool(given)),
         grid=(steps,),
-        in_specs=[pl.BlockSpec((per, blk, latent), lambda i: (i, 0, 0))]
-        + [pl.BlockSpec(memory_space=pltpu.HBM)] * len(whole),
+        in_specs=[pl.BlockSpec((per, blk, latent), lambda i: (i + start, 0, 0))]
+        + [pl.BlockSpec(memory_space=pltpu.HBM)] * (len(whole) + len(given)),
         out_specs=[
-            pl.BlockSpec((per, blk, latent), lambda i: (i, 0, 0)),
+            pl.BlockSpec((per, blk, latent), lambda i: (i + start, 0, 0)),
             pl.BlockSpec((own_blocks, blk, latent), lambda i: (0, 0, 0)),
         ],
         scratch_shapes=[
@@ -164,16 +174,17 @@
         + [pltpu.SemaphoreType.DMA((len(whole),))],
         out_shape=[
             jax.ShapeDtypeStruct(edges.shape, edges.dtype),
-            jax.ShapeDtypeStruct((own_blocks, blk, latent), jnp.bfloat16),
+            jax.ShapeDtypeStruct((own_blocks, blk, latent), jnp.bfloat16 if given else jnp.float32),
         ],
+        input_output_aliases={len(whole) + 2: 0} if given else {},
         compiler_params=pltpu.CompilerParams(
             vmem_limit_bytes=48 * 2**20, dimension_semantics=("arbitrary",)
         ),
         cost_estimate=pl.CostEstimate(
-            flops=20 * 10**9, bytes_accessed=100 * 10**6, transcendentals=5 * 10**6
+            flops=steps * 3 * 10**9, bytes_accessed=steps * 14 * 10**6, transcendentals=steps * 10**6
         ),
         name="edges",
-    )(edges, *whole)
+    )(edges, *whole, *given)
 
 
 def column(row):
@@ -329,6 +340,16 @@
     left = lax.ppermute(tall(rows_y - 1), "gy", right_pairs)
     right = lax.ppermute(tall(0), "gy", [(j, i) for i, j in right_pairs])
     rows_in = lax.all_to_all(rows_out, BOTH, 0, 0, tiled=True)
+    edge_whole = (
+        pinned(target_nodes[0, 0]), pinned(fine_nodes), up, down, pinned(left), pinned(right),
+        *map(pinned, (edge_in, row(edge_bias), edge_out, row(edge_bias_two), row(edge_gain))),
+    )
+    places = (pinned(edge_sources[0, 0]), pinned(target_blocks[0]))
+    all_steps = edge_states.shape[2] // (2 * SUB)
+    early = all_steps // 4
+    partial = edge_call(edge_states[0, 0], *places, live_blocks, *edge_whole, start=0, steps=early)
+    early_result, early_sums = partial
+    rows_in, early_sums = lax.optimization_barrier((rows_in, early_sums))
     coarse_result, answers = call(
         coarse_kernel, "coarse", [like(coarse_nodes.shape, jnp.bfloat16), like((devices, latent // 128, 128), jnp.float32)],
         rows_in,
@@ -336,9 +357,7 @@
     )
     live, answers = lax.optimization_barrier((live_blocks, answers))
     edge_result, aggregate = edge_call(
-        edge_states[0, 0], pinned(edge_sources[0, 0]), pinned(target_blocks[0]), live, pinned(target_nodes[0, 0]),
-        pinned(fine_nodes), up, down, left, right,
-        *map(pinned, (edge_in, row(edge_bias), edge_out, row(edge_bias_two), row(edge_gain))),
+        edge_states[0, 0], *places, live, *edge_whole, start=early, steps=all_steps - early, given=(pinned(early_sums), early_result)
     )
     from_owners = lax.all_to_all(answers, BOTH, 0, 0, tiled=True)
     fine_result, middle_result = call(

time: 96.7 us -> 97.3 us (level)
  waiting for transfers between devices: 13.3 us -> 3.2 us
  Pallas kernels: 46.1 us -> 54 us
  local copies, waits for them, and re-layouts: 2.41 us -> 4.61 us
  starting transfers between devices: 31.2 us -> 33.2 us
  other arithmetic: 1.95 us -> 0.19 us
    all_to_all x1, waiting for transfers between devices: 13 us -> 0.01 us  [body(): rows_in = lax.all_to_all(rows_out, BOTH, 0, 0, tiled=True)]
    pallas_call x1 -> x2, Pallas kernels: 33.7 us -> 41.7 us  [edge_call(): pl.pallas_call(functools.partial(edge_kernel, start=start, carried=bool(g...]
    all_to_all x1, starting transfers between devices: 4.61 us -> 9.77 us  [body(): from_owners = lax.all_to_all(answers, BOTH, 0, 0, tiled=True)]
    ppermute x2, waiting for transfers between devices: 0.27 us -> 3.19 us  [exchanged(): return (lax.ppermute(last, axis, up), lax.ppermute(first, axis, down))]
    all_to_all x1, starting transfers between devices: 13.2 us -> 10.9 us  [body(): rows_in = lax.all_to_all(rows_out, BOTH, 0, 0, tiled=True)]
    unnamed x0 -> x4, local copies, waits for them, and re-layouts: none -> 2.2 us
    ppermute x1, starting transfers between devices: 5.53 us -> 3.44 us  [body(): left = lax.ppermute(tall(rows_y - 1), 'gy', right_pairs)]
    ppermute x1, starting transfers between devices: 1.91 us -> 3.77 us  [body(): right = lax.ppermute(tall(0), 'gy', [(j, i) for i, j in right_pairs])]
  transfers between devices with their start and end apart: 6 -> 6, of which waited for: 2 -> 1; matrix products, arithmetic and copies ran while one was open for 2% -> 1% of each run, Pallas kernels for 42% -> 46%
where the time goes in v5:
time: 97.3 us; the launch traced here: 96.8 us
  Pallas kernels  54 us (55%)
  starting transfers between devices  33.2 us (34%)
  local copies, waits for them, and re-layouts  4.61 us (5%)
  waiting for transfers between devices  3.2 us (3%)
  between operations  1.6 us (2%)
    pallas_call x2, Pallas kernels, edge_call(): pl.pallas_call(functools.partial(edge_kernel, start=start, carried=bool(g...  41.7 us
    pallas_call x3, Pallas kernels, call(): pl.pallas_call(run, out_shape=out_shape, in_specs=[pl.BlockSpec(memory_sp...  12.3 us
    all_to_all x1, starting transfers between devices, body(): rows_in = lax.all_to_all(rows_out, BOTH, 0, 0, tiled=True)  10.9 us
    all_to_all x1, starting transfers between devices, body(): from_owners = lax.all_to_all(answers, BOTH, 0, 0, tiled=True)  9.77 us
    ppermute x2, starting transfers between devices, exchanged(): return (lax.ppermute(last, axis, up), lax.ppermute(first, axis, down))  5.34 us
    ppermute x1, starting transfers between devices, body(): right = lax.ppermute(tall(0), 'gy', [(j, i) for i, j in right_pairs])  3.77 us
    ppermute x1, starting transfers between devices, body(): left = lax.ppermute(tall(rows_y - 1), 'gy', right_pairs)  3.44 us
    ppermute x2, waiting for transfers between devices, exchanged(): return (lax.ppermute(last, axis, up), lax.ppermute(first, axis, down))  3.19 us
  transfers between devices with their start and end apart: 6, of which 1 were waited for; matrix products, arithmetic and copies ran while one was open for 1% of the time, Pallas kernels for 46%

profile of v5, /device:TPU:1, one launch (start us, length us, event | category | flops | bytes accessed | tf_op | source)
XLA Modules:
  0.0 96.8 jit_solution(11791303398875938260)
XLA Ops:
  0.6 1.1 %fusion.1 = (bf16[1,2,128,512]{3,2,1,0:T(8,128)(2,1)S(1)}, bf16[1,2,128,512]{3,2,1,0:T(8,128)(2,1)S(1)}) fusion(bf16[4,2,128,512]{3,2,1,0:T(8,128)(2,1)} %rest_4_.3), kind=kLoop, calls=%fused_computation.3 | loop fusion | bytes 1048576 | tf_op jit(solution)/shard_map/slice | solution.py:309
  1.7 4.0 %collective-permute-start = (bf16[1,2,128,512]{3,2,1,0:T(8,128)(2,1)S(1)}, bf16[1,2,128,512]{3,2,1,0:T(8,128)(2,1)S(1)}, u32[]{:S(2)}, u32[]{:S(2)}) collective-permute-start(bf16[1,2,128,512]{3,2,1,0:T(8,128)(2,1)S(1)} %get-tuple-element.41), channel_id=1, source_target_pairs={{0,8},{8,16},{16,24},{24,32},{32,40},{40,48},{48,56},{56,64},{64,7... | collective-permute-start | bytes 786440 | tf_op jit(solution)/shard_map/ppermute | solution.py:310
  5.8 1.3 %collective-permute-start.1 = (bf16[1,2,128,512]{3,2,1,0:T(8,128)(2,1)S(1)}, bf16[1,2,128,512]{3,2,1,0:T(8,128)(2,1)S(1)}, u32[]{:S(2)}, u32[]{:S(2)}) collective-permute-start(bf16[1,2,128,512]{3,2,1,0:T(8,128)(2,1)S(1)} %get-tuple-element.40), channel_id=1, source_target_pairs={{8,0},{16,8},{24,16},{32,24},{40,32},{48,40},{56,48},{64,56},{72,6... | collective-permute-start | bytes 786440 | tf_op jit(solution)/shard_map/ppermute | solution.py:310
  7.1 2.9 %middle.1 = (bf16[128,512]{1,0:T(8,128)(2,1)S(1)}, f32[128,8,128]{2,1,0:T(8,128)}) custom-call(bf16[8,128,512]{2,1,0:T(8,128)(2,1)} %bitcast.20, s32[4,2,128]{2,1,0:T(2,128)} %refs_11_.1, f32[4,2,128]{2,1,0:T(2,128)} %refs_12_.1, bf16[128,512]{1,0:T(8,128)(2,1)} %bitcast.32, s32[1,128]{1,0:T(1,128)} %bitcast.25, f32[1,128]{1,0:T(1,128)} %bitcast.27), custom_call_target="tpu_custom_call" | custom-call | flops 1000000000 | bytes 9000000 | tf_op jit(solution)/shard_map/middle/pallas_call | solution.py:292
  10.0 1.3 %fusion = (bf16[4,1,128,512]{3,2,1,0:T(8,128)(2,1)S(1)}, bf16[4,1,128,512]{3,2,1,0:T(8,128)(2,1)S(1)}) fusion(bf16[4,2,128,512]{3,2,1,0:T(8,128)(2,1)} %rest_4_.3), kind=kLoop, calls=%fused_computation.2 | loop fusion | bytes 2097152 | tf_op jit(solution)/shard_map/slice | solution.py:337
  11.3 0.0 collective-permute-done.rest_5_
  11.3 3.2 %collective-permute-done.1.rest_6_ = bf16[1,2,128,512]{3,2,1,0:T(8,128)(2,1)S(1)} collective-permute-done((bf16[1,2,128,512]{3,2,1,0:T(8,128)(2,1)S(1)}, bf16[1,2,128,512]{3,2,1,0:T(8,128)(2,1)S(1)}, u32[]{:S(2)}, u32[]{:S(2)}) %collective-permute-start.1) | collective-permute-done | bytes 262176 | tf_op jit(solution)/shard_map/ppermute | solution.py:310
  14.5 0.1 pad_maximum_fusion.1
  14.6 3.8 %collective-permute-start.3 = (bf16[6,1,128,512]{3,2,1,0:T(8,128)(2,1)S(1)}, bf16[6,1,128,512]{3,2,1,0:T(8,128)(2,1)S(1)}, u32[]{:S(2)}, u32[]{:S(2)}) collective-permute-start(bf16[6,1,128,512]{3,2,1,0:T(8,128)(2,1)S(1)} %pad_maximum_fusion.1), channel_id=1, source_target_pairs={{1,0},{2,1},{3,2},{4,3},{5,4},{6,5},{7,6},{9,8},{10,9},{11,10},{12... | collective-permute-start | bytes 2359304 | tf_op jit(solution)/shard_map/ppermute | solution.py:341
  18.4 0.1 pad_maximum_fusion
  18.5 3.4 %collective-permute-start.2 = (bf16[6,1,128,512]{3,2,1,0:T(8,128)(2,1)S(1)}, bf16[6,1,128,512]{3,2,1,0:T(8,128)(2,1)}, u32[]{:S(2)}, u32[]{:S(2)}) collective-permute-start(bf16[6,1,128,512]{3,2,1,0:T(8,128)(2,1)S(1)} %pad_maximum_fusion), channel_id=1, source_target_pairs={{0,1},{1,2},{2,3},{3,4},{4,5},{5,6},{6,7},{8,9},{9,10},{10,11},{11... | collective-permute-start | bytes 2359304 | tf_op jit(solution)/shard_map/ppermute | solution.py:340
  22.0 10.9 %all-to-all-start = ((f32[128,8,128]{2,1,0:T(8,128)}), f32[128,8,128]{2,1,0:T(8,128)S(1)}, u32[]{:S(2)}, u32[]{:S(2)}) async-start(f32[128,8,128]{2,1,0:T(8,128)} %get-tuple-element.21), calls=%async_computation | async-start | bytes 1048576 | tf_op jit(solution)/shard_map/all_to_all | solution.py:342
  33.5 0.0 collective-permute-done.3.rest_8_
  33.5 0.0 copy-start.1
  33.5 0.0 collective-permute-done.2.rest_7_
  33.5 0.9 copy-done.1
  34.4 13.8 %edges.2 = (bf16[64,128,512]{2,1,0:T(8,128)(2,1)}, f32[8,128,512]{2,1,0:T(8,128)S(1)}) custom-call(bf16[64,128,512]{2,1,0:T(8,128)(2,1)} %bitcast.29, s32[64,128]{1,0:T(8,128)} %bitcast.34, s32[1,64]{1,0:T(1,128)} %bitcast.47, s32[1,1]{1,0:T(1,128)S(6)} %copy.33.rest_2_, s32[64,128]{1,0:T(8,128)} %bitcast.36, bf16[4,2,128,512]{3,2,1,0:T(8,128)(2,1)} %rest_4_.3, ...), custom_call_target="tpu_custom_call" | custom-call | flops 6000000000 | bytes 28000000 | tf_op jit(solution)/shard_map/edges/pallas_call | solution.py:156
  48.2 0.0 copy-start
  48.2 1.3 %copy-done = f32[8,128,512]{2,1,0:T(8,128)} copy-done((f32[8,128,512]{2,1,0:T(8,128)}, f32[8,128,512]{2,1,0:T(8,128)S(1)}, u32[]{:S(2)}) %copy-start) | copy-done | bytes 2097176
  49.5 0.0 all-to-all-done.refs_0_
  49.5 3.8 %coarse.1 = (bf16[8,512]{1,0:T(8,128)(2,1)}, f32[128,4,128]{2,1,0:T(4,128)}) custom-call(f32[128,8,128]{2,1,0:T(8,128)S(1)} %all-to-all-done.refs_0_, bf16[8,512]{1,0:T(8,128)(2,1)} %refs_1_.3, bf16[2,512,512]{2,1,0:T(8,128)(2,1)} %refs_2_.4, f32[1,512]{1,0:T(1,128)} %bitcast.38, bf16[512,512]{1,0:T(8,128)(2,1)} %refs_4_.2, f32[1,512]{1,0:T(1,128)} %bitcast.39, ...), custom_call_target="tpu_custom_call" | custom-call | flops 1000000000 | bytes 9000000 | tf_op jit(solution)/shard_map/coarse/pallas_call | solution.py:292
  53.3 9.8 %all-to-all-start.1 = ((f32[128,4,128]{2,1,0:T(4,128)}), f32[128,4,128]{2,1,0:T(4,128)S(1)}, u32[]{:S(2)}, u32[]{:S(2)}) async-start(f32[128,4,128]{2,1,0:T(4,128)} %get-tuple-element.33), calls=%async_computation.1 | async-start | bytes 524288 | tf_op jit(solution)/shard_map/all_to_all | solution.py:362
  63.1 27.9 %edges.3 = (bf16[64,128,512]{2,1,0:T(8,128)(2,1)}, bf16[8,128,512]{2,1,0:T(8,128)(2,1)S(1)}) custom-call(bf16[64,128,512]{2,1,0:T(8,128)(2,1)} %bitcast.30, s32[64,128]{1,0:T(8,128)} %bitcast.35, s32[1,64]{1,0:T(1,128)} %bitcast.48, s32[1,1]{1,0:T(1,128)S(6)} %copy.33.rest_2_, s32[64,128]{1,0:T(8,128)} %bitcast.37, ...), custom_call_target="tpu_custom_call", output_to_operand_aliasing={{0}: (16, {})} | custom-call | flops 17999998976 | bytes 84000000 | tf_op jit(solution)/shard_map/edges/pallas_call | solution.py:156
  91.0 0.0 all-to-all-done.1.refs_8_
  91.0 5.6 %final.1 = (bf16[8,128,512]{2,1,0:T(8,128)(2,1)}, bf16[128,512]{1,0:T(8,128)(2,1)}) custom-call(bf16[8,128,512]{2,1,0:T(8,128)(2,1)} %bitcast.21, bf16[8,128,512]{2,1,0:T(8,128)(2,1)S(1)} %get-tuple-element.31.refs_1_, bf16[2,512,512]{2,1,0:T(8,128)(2,1)} %refs_2_.5, f32[1,512]{1,0:T(1,128)} %bitcast.22, bf16[512,512]{1,0:T(8,128)(2,1)} %refs_4_.3, ...), custom_call_target="tpu_custom_call" | custom-call | flops 1000000000 | bytes 9000000 | tf_op jit(solution)/shard_map/final/pallas_call | solution.py:292
  (1 shorter events, 0.0 us)
Async XLA Ops:
  1.7 9.6 %collective-permute-start = (bf16[1,2,128,512]{3,2,1,0:T(8,128)(2,1)S(1)}, bf16[1,2,128,512]{3,2,1,0:T(8,128)(2,1)S(1)}, u32[]{:S(2)}, u32[]{:S(2)}) collective-permute-start(bf16[1,2,128,512]{3,2,1,0:T(8,128)(2,1)S(1)} %get-tuple-element.41), channel_id=1, source_target_pairs={{0,8},{8,16},{16,24},{24,32},{32,40},{40,48},{48,56},{56,64},{64,7... | collective-permute-start | bytes 786440 | tf_op jit(solution)/shard_map/ppermute | solution.py:310
  5.8 8.8 %collective-permute-start.1 = (bf16[1,2,128,512]{3,2,1,0:T(8,128)(2,1)S(1)}, bf16[1,2,128,512]{3,2,1,0:T(8,128)(2,1)S(1)}, u32[]{:S(2)}, u32[]{:S(2)}) collective-permute-start(bf16[1,2,128,512]{3,2,1,0:T(8,128)(2,1)S(1)} %get-tuple-element.40), channel_id=1, source_target_pairs={{8,0},{16,8},{24,16},{32,24},{40,32},{48,40},{56,48},{64,56},{72,6... | collective-permute-start | bytes 786440 | tf_op jit(solution)/shard_map/ppermute | solution.py:310
  14.6 18.9 %collective-permute-start.3 = (bf16[6,1,128,512]{3,2,1,0:T(8,128)(2,1)S(1)}, bf16[6,1,128,512]{3,2,1,0:T(8,128)(2,1)S(1)}, u32[]{:S(2)}, u32[]{:S(2)}) collective-permute-start(bf16[6,1,128,512]{3,2,1,0:T(8,128)(2,1)S(1)} %pad_maximum_fusion.1), channel_id=1, source_target_pairs={{1,0},{2,1},{3,2},{4,3},{5,4},{6,5},{7,6},{9,8},{10,9},{11,10},{12... | collective-permute-start | bytes 2359304 | tf_op jit(solution)/shard_map/ppermute | solution.py:341
  18.5 15.0 %collective-permute-start.2 = (bf16[6,1,128,512]{3,2,1,0:T(8,128)(2,1)S(1)}, bf16[6,1,128,512]{3,2,1,0:T(8,128)(2,1)}, u32[]{:S(2)}, u32[]{:S(2)}) collective-permute-start(bf16[6,1,128,512]{3,2,1,0:T(8,128)(2,1)S(1)} %pad_maximum_fusion), channel_id=1, source_target_pairs={{0,1},{1,2},{2,3},{3,4},{4,5},{5,6},{6,7},{8,9},{9,10},{10,11},{11... | collective-permute-start | bytes 2359304 | tf_op jit(solution)/shard_map/ppermute | solution.py:340
  22.0 27.5 %all-to-all-start = ((f32[128,8,128]{2,1,0:T(8,128)}), f32[128,8,128]{2,1,0:T(8,128)S(1)}, u32[]{:S(2)}, u32[]{:S(2)}) async-start(f32[128,8,128]{2,1,0:T(8,128)} %get-tuple-element.21), calls=%async_computation | async-start | bytes 1048576 | tf_op jit(solution)/shard_map/all_to_all | solution.py:342
  33.5 0.9 copy-start.1
  48.2 1.3 %copy-start = (f32[8,128,512]{2,1,0:T(8,128)}, f32[8,128,512]{2,1,0:T(8,128)S(1)}, u32[]{:S(2)}) copy-start(f32[8,128,512]{2,1,0:T(8,128)S(1)} %get-tuple-element.29.rest_14_) | copy-start | bytes 6291460
  53.3 37.7 %all-to-all-start.1 = ((f32[128,4,128]{2,1,0:T(4,128)}), f32[128,4,128]{2,1,0:T(4,128)S(1)}, u32[]{:S(2)}, u32[]{:S(2)}) async-start(f32[128,4,128]{2,1,0:T(4,128)} %get-tuple-element.33), calls=%async_computation.1 | async-start | bytes 524288 | tf_op jit(solution)/shard_map/all_to_all | solution.py:362

commit v6 on v3

--- a/solution.py
+++ b/solution.py
@@ -93,8 +93,7 @@
 
     number = lax.broadcasted_iota(jnp.int32, (blk, blk), 0)
 
-    def compute(half, b_next):
-        chunk = 2 * step + half
+    def begin(half, b_next):
         ref = picked[half]
         base = half * SUB
         states = edges[base : base + SUB].reshape(SUB * blk, latent)
@@ -103,7 +102,7 @@
         spots = []
         for b in range(SUB):
             b_next(b)
-            block = chunk * SUB + b
+            block = (2 * step + half) * SUB + b
             to = target_blocks[0, block]
             spot = (target_nodes[pl.ds(block, 1), :] == number).astype(jnp.bfloat16)
             spots.append((to, spot))
@@ -114,10 +113,13 @@
             hidden.append(
                 silu(pre[b * blk : (b + 1) * blk] + from_target + from_source).astype(jnp.bfloat16)
             )
-        out = matmul(jnp.concatenate(hidden, axis=0), second[...]) + bias_two[...]
+        return jnp.concatenate(hidden, axis=0), spots
+
+    def finish(half, out, spots):
+        base = half * SUB
         for b in range(SUB):
             rows = out[b * blk : (b + 1) * blk]
-            block = chunk * SUB + b
+            block = (2 * step + half) * SUB + b
             alive = jnp.where(block < live[0, 0], 1.0, 0.0)
             centred = rows - jnp.mean(rows, axis=-1, keepdims=True)
             spread = jnp.mean(centred * centred, axis=-1, keepdims=True)
@@ -126,8 +128,12 @@
             to, spot = spots[b]
             sums[to] += matmul(spot, message)
 
-    compute(0, lambda b: gather(2 * step + 1, b, picked_b))
-    compute(1, lambda b: gather(jnp.minimum(2 * step + 2, chunks - 1), b, picked_a))
+    hidden_a, spots_a = begin(0, lambda b: gather(2 * step + 1, b, picked_b))
+    out_a = matmul(hidden_a, second[...]) + bias_two[...]
+    hidden_b, spots_b = begin(1, lambda b: gather(jnp.minimum(2 * step + 2, chunks - 1), b, picked_a))
+    out_b = matmul(hidden_b, second[...]) + bias_two[...]
+    finish(0, out_a, spots_a)
+    finish(1, out_b, spots_b)
 
     @pl.when(step == steps - 1)
     def _():
@@ -322,13 +328,13 @@
         middle_kernel, "middle", [like(middle.shape, jnp.bfloat16), like((devices, 8, 128), jnp.float32)],
         *map(pinned, (own, fine_parent, fine_weight, middle, mid_parents, mid_weights)), coarse_own=coarse_own,
     )
-    up, down, middle_mid = lax.optimization_barrier((up, down, middle_mid))
+    rows_in = lax.all_to_all(rows_out, BOTH, 0, 0, tiled=True)
+    up, down, rows_in = lax.optimization_barrier((up, down, rows_in))
     tall = lambda y: jnp.concatenate([up[:, y : y + 1], fine_nodes[:, y : y + 1], down[:, y : y + 1]], axis=0)
     count = lax.axis_size("gy")
     right_pairs = [(i, i + 1) for i in range(count - 1)]
     left = lax.ppermute(tall(rows_y - 1), "gy", right_pairs)
     right = lax.ppermute(tall(0), "gy", [(j, i) for i, j in right_pairs])
-    rows_in = lax.all_to_all(rows_out, BOTH, 0, 0, tiled=True)
     coarse_result, answers = call(
         coarse_kernel, "coarse", [like(coarse_nodes.shape, jnp.bfloat16), like((devices, latent // 128, 128), jnp.float32)],
         rows_in,

time: 96.7 us -> 90.6 us (0.937)
  waiting for transfers between devices: 13.3 us -> 6.35 us
  starting transfers between devices: 31.2 us -> 33.5 us
  Pallas kernels: 46.1 us -> 44.6 us
    all_to_all x1, waiting for transfers between devices: 13 us -> 0.01 us  [body(): rows_in = lax.all_to_all(rows_out, BOTH, 0, 0, tiled=True)]
    all_to_all x1, starting transfers between devices: 4.61 us -> 10.9 us  [body(): from_owners = lax.all_to_all(answers, BOTH, 0, 0, tiled=True)]
    ppermute x2, waiting for transfers between devices: 0.27 us -> 6.34 us  [exchanged(): return (lax.ppermute(last, axis, up), lax.ppermute(first, axis, down))]
    all_to_all x1, starting transfers between devices: 13.2 us -> 11.5 us  [body(): rows_in = lax.all_to_all(rows_out, BOTH, 0, 0, tiled=True)]
    ppermute x1, starting transfers between devices: 5.53 us -> 3.88 us  [body(): left = lax.ppermute(tall(rows_y - 1), 'gy', right_pairs)]
    pallas_call x1, Pallas kernels: 33.7 us -> 32.3 us  [edge_call(): pl.pallas_call(edge_kernel, grid=(steps,), in_specs=[pl.BlockSpec((per, b...]
  transfers between devices with their start and end apart: 6 -> 6, of which waited for: 2 -> 1; matrix products, arithmetic and copies ran while one was open for 2% -> 4% of each run, Pallas kernels for 42% -> 40%
where the time goes in v6:
time: 90.6 us; the launch traced here: 90.2 us
  Pallas kernels  44.6 us (49%)
  starting transfers between devices  33.5 us (37%)
  waiting for transfers between devices  6.35 us (7%)
  local copies, waits for them, and re-layouts  2.41 us (3%)
  other arithmetic  1.95 us (2%)
  between operations  1.39 us (2%)
    pallas_call x1, Pallas kernels, edge_call(): pl.pallas_call(edge_kernel, grid=(steps,), in_specs=[pl.BlockSpec((per, b...  32.3 us
    pallas_call x3, Pallas kernels, call(): pl.pallas_call(run, out_shape=out_shape, in_specs=[pl.BlockSpec(memory_sp...  12.3 us
    all_to_all x1, starting transfers between devices, body(): rows_in = lax.all_to_all(rows_out, BOTH, 0, 0, tiled=True)  11.5 us
    all_to_all x1, starting transfers between devices, body(): from_owners = lax.all_to_all(answers, BOTH, 0, 0, tiled=True)  10.9 us
    ppermute x2, waiting for transfers between devices, exchanged(): return (lax.ppermute(last, axis, up), lax.ppermute(first, axis, down))  6.34 us
    ppermute x2, starting transfers between devices, exchanged(): return (lax.ppermute(last, axis, up), lax.ppermute(first, axis, down))  5.29 us
    ppermute x1, starting transfers between devices, body(): left = lax.ppermute(tall(rows_y - 1), 'gy', right_pairs)  3.88 us
    concatenate x2, other arithmetic, body(): jnp.concatenate([up[:, y:y + 1], fine_nodes[:, y:y + 1], down[:, y:y + 1]...  1.95 us
  transfers between devices with their start and end apart: 6, of which 1 were waited for; matrix products, arithmetic and copies ran while one was open for 4% of the time, Pallas kernels for 40%

profile of v6, /device:TPU:1, one launch (start us, length us, event | category | flops | bytes accessed | tf_op | source)
XLA Modules:
  0.0 90.2 jit_solution(15128409854613599082)
XLA Ops:
  0.6 2.9 %middle.1 = (bf16[128,512]{1,0:T(8,128)(2,1)S(1)}, f32[128,8,128]{2,1,0:T(8,128)}) custom-call(bf16[8,128,512]{2,1,0:T(8,128)(2,1)} %bitcast.20, s32[4,2,128]{2,1,0:T(2,128)} %refs_11_.1, f32[4,2,128]{2,1,0:T(2,128)} %refs_12_.1, bf16[128,512]{1,0:T(8,128)(2,1)} %bitcast.31, s32[1,128]{1,0:T(1,128)} %bitcast.25, f32[1,128]{1,0:T(1,128)} %bitcast.27), custom_call_target="tpu_custom_call" | custom-call | flops 1000000000 | bytes 9000000 | tf_op jit(solution)/shard_map/middle/pallas_call | solution.py:287
  3.6 11.5 %all-to-all-start = ((f32[128,8,128]{2,1,0:T(8,128)}), f32[128,8,128]{2,1,0:T(8,128)S(1)}, u32[]{:S(2)}, u32[]{:S(2)}) async-start(f32[128,8,128]{2,1,0:T(8,128)} %get-tuple-element.17), calls=%async_computation | async-start | bytes 1048576 | tf_op jit(solution)/shard_map/all_to_all | solution.py:331
  15.1 1.1 %fusion.1 = (bf16[1,2,128,512]{3,2,1,0:T(8,128)(2,1)S(1)}, bf16[1,2,128,512]{3,2,1,0:T(8,128)(2,1)S(1)}) fusion(bf16[4,2,128,512]{3,2,1,0:T(8,128)(2,1)} %rest_4_.1), kind=kLoop, calls=%fused_computation.3 | loop fusion | bytes 1048576 | tf_op jit(solution)/shard_map/slice | solution.py:304
  16.1 1.3 %collective-permute-start.1 = (bf16[1,2,128,512]{3,2,1,0:T(8,128)(2,1)S(1)}, bf16[1,2,128,512]{3,2,1,0:T(8,128)(2,1)S(1)}, u32[]{:S(2)}, u32[]{:S(2)}) collective-permute-start(bf16[1,2,128,512]{3,2,1,0:T(8,128)(2,1)S(1)} %get-tuple-element.32), channel_id=1, source_target_pairs={{8,0},{16,8},{24,16},{32,24},{40,32},{48,40},{56,48},{64,56},{72,6... | collective-permute-start | bytes 786440 | tf_op jit(solution)/shard_map/ppermute | solution.py:305
  17.4 4.0 %collective-permute-start = (bf16[1,2,128,512]{3,2,1,0:T(8,128)(2,1)S(1)}, bf16[1,2,128,512]{3,2,1,0:T(8,128)(2,1)S(1)}, u32[]{:S(2)}, u32[]{:S(2)}) collective-permute-start(bf16[1,2,128,512]{3,2,1,0:T(8,128)(2,1)S(1)} %get-tuple-element.33), channel_id=1, source_target_pairs={{0,8},{8,16},{16,24},{24,32},{32,40},{40,48},{48,56},{56,64},{64,7... | collective-permute-start | bytes 786440 | tf_op jit(solution)/shard_map/ppermute | solution.py:305
  21.5 1.3 %fusion = (bf16[4,1,128,512]{3,2,1,0:T(8,128)(2,1)S(1)}, bf16[4,1,128,512]{3,2,1,0:T(8,128)(2,1)S(1)}) fusion(bf16[4,2,128,512]{3,2,1,0:T(8,128)(2,1)} %rest_4_.1), kind=kLoop, calls=%fused_computation.2 | loop fusion | bytes 2097152 | tf_op jit(solution)/shard_map/slice | solution.py:333
  22.8 6.3 %collective-permute-done.1.rest_6_ = bf16[1,2,128,512]{3,2,1,0:T(8,128)(2,1)S(1)} collective-permute-done((bf16[1,2,128,512]{3,2,1,0:T(8,128)(2,1)S(1)}, bf16[1,2,128,512]{3,2,1,0:T(8,128)(2,1)S(1)}, u32[]{:S(2)}, u32[]{:S(2)}) %collective-permute-start.1) | collective-permute-done | bytes 262176 | tf_op jit(solution)/shard_map/ppermute | solution.py:305
  29.1 0.0 collective-permute-done.rest_5_
  29.1 0.0 all-to-all-done.refs_0_
  29.2 1.0 %pad_maximum_fusion = bf16[6,1,128,512]{3,2,1,0:T(8,128)(2,1)} fusion(bf16[1,1,128,512]{3,2,1,0:T(8,128)(2,1)S(1)} %get-tuple-element.38, bf16[4,1,128,512]{3,2,1,0:T(8,128)(2,1)S(1)} %get-tuple-element.31, bf16[1,1,128,512]{3,2,1,0:T(8,128)(2,1)S(1)} %get-tuple-element.35), kind=kLoop, calls=%fused_computation | loop fusion | flops 786432 | bytes 1572864 | tf_op jit(solution)/shard_map/concatenate | solution.py:333
  30.1 3.9 %collective-permute-start.2 = (bf16[6,1,128,512]{3,2,1,0:T(8,128)(2,1)}, bf16[6,1,128,512]{3,2,1,0:T(8,128)(2,1)S(1)}, u32[]{:S(2)}, u32[]{:S(2)}) collective-permute-start(bf16[6,1,128,512]{3,2,1,0:T(8,128)(2,1)} %pad_maximum_fusion), channel_id=1, source_target_pairs={{0,1},{1,2},{2,3},{3,4},{4,5},{5,6},{6,7},{8,9},{9,10},{10,11},{11... | collective-permute-start | bytes 2359304 | tf_op jit(solution)/shard_map/ppermute | solution.py:336
  34.0 1.0 %pad_maximum_fusion.1 = bf16[6,1,128,512]{3,2,1,0:T(8,128)(2,1)} fusion(bf16[1,1,128,512]{3,2,1,0:T(8,128)(2,1)S(1)} %get-tuple-element.39, bf16[4,1,128,512]{3,2,1,0:T(8,128)(2,1)S(1)} %get-tuple-element.30, bf16[1,1,128,512]{3,2,1,0:T(8,128)(2,1)S(1)} %get-tuple-element.34), kind=kLoop, calls=%fused_computation.1 | loop fusion | flops 786432 | bytes 1572864 | tf_op jit(solution)/shard_map/concatenate | solution.py:333
  35.0 1.9 %collective-permute-start.3 = (bf16[6,1,128,512]{3,2,1,0:T(8,128)(2,1)}, bf16[6,1,128,512]{3,2,1,0:T(8,128)(2,1)S(1)}, u32[]{:S(2)}, u32[]{:S(2)}) collective-permute-start(bf16[6,1,128,512]{3,2,1,0:T(8,128)(2,1)} %pad_maximum_fusion.1), channel_id=1, source_target_pairs={{1,0},{2,1},{3,2},{4,3},{5,4},{6,5},{7,6},{9,8},{10,9},{11,10},{12... | collective-permute-start | bytes 2359304 | tf_op jit(solution)/shard_map/ppermute | solution.py:337
  37.6 3.8 %coarse.1 = (bf16[8,512]{1,0:T(8,128)(2,1)}, f32[128,4,128]{2,1,0:T(4,128)}) custom-call(f32[128,8,128]{2,1,0:T(8,128)S(1)} %all-to-all-done.refs_0_, bf16[8,512]{1,0:T(8,128)(2,1)} %refs_1_.3, bf16[2,512,512]{2,1,0:T(8,128)(2,1)} %refs_2_.4, f32[1,512]{1,0:T(1,128)} %bitcast.35, bf16[512,512]{1,0:T(8,128)(2,1)} %refs_4_.2, f32[1,512]{1,0:T(1,128)} %bitcast.36, ...), custom_call_target="tpu_custom_call" | custom-call | flops 1000000000 | bytes 9000000 | tf_op jit(solution)/shard_map/coarse/pallas_call | solution.py:287
  41.3 10.9 %all-to-all-start.1 = ((f32[128,4,128]{2,1,0:T(4,128)}), f32[128,4,128]{2,1,0:T(4,128)S(1)}, u32[]{:S(2)}, u32[]{:S(2)}) async-start(f32[128,4,128]{2,1,0:T(4,128)} %get-tuple-element.25), calls=%async_computation.1 | async-start | bytes 524288 | tf_op jit(solution)/shard_map/all_to_all | solution.py:349
  52.2 0.0 collective-permute-done.2.rest_7_
  52.2 0.0 collective-permute-done.3.rest_8_
  52.2 32.3 %edges.1 = (bf16[64,128,512]{2,1,0:T(8,128)(2,1)}, bf16[8,128,512]{2,1,0:T(8,128)(2,1)S(1)}) custom-call(bf16[64,128,512]{2,1,0:T(8,128)(2,1)} %bitcast.29, s32[64,128]{1,0:T(8,128)} %bitcast.33, s32[1,64]{1,0:T(1,128)} %bitcast.41, s32[1,1]{1,0:T(1,128)S(6)} %copy.31.rest_2_, s32[64,128]{1,0:T(8,128)} %bitcast.34, bf16[4,2,128,512]{3,2,1,0:T(8,128)(2,1)} %rest_4_.1, ...), custom_call_target="tpu_custom_call" | custom-call | flops 20000000000 | bytes 100000000 | tf_op jit(solution)/shard_map/edges/pallas_call | solution.py:152
  84.5 0.0 all-to-all-done.1.refs_8_
  84.5 5.6 %final.1 = (bf16[8,128,512]{2,1,0:T(8,128)(2,1)}, bf16[128,512]{1,0:T(8,128)(2,1)}) custom-call(bf16[8,128,512]{2,1,0:T(8,128)(2,1)} %bitcast.21, bf16[8,128,512]{2,1,0:T(8,128)(2,1)S(1)} %get-tuple-element.23.refs_1_, bf16[2,512,512]{2,1,0:T(8,128)(2,1)} %refs_2_.5, f32[1,512]{1,0:T(1,128)} %bitcast.22, bf16[512,512]{1,0:T(8,128)(2,1)} %refs_4_.3, ...), custom_call_target="tpu_custom_call" | custom-call | flops 1000000000 | bytes 9000000 | tf_op jit(solution)/shard_map/final/pallas_call | solution.py:287
  (1 shorter events, 0.0 us)
Async XLA Ops:
  3.6 25.5 %all-to-all-start = ((f32[128,8,128]{2,1,0:T(8,128)}), f32[128,8,128]{2,1,0:T(8,128)S(1)}, u32[]{:S(2)}, u32[]{:S(2)}) async-start(f32[128,8,128]{2,1,0:T(8,128)} %get-tuple-element.17), calls=%async_computation | async-start | bytes 1048576 | tf_op jit(solution)/shard_map/all_to_all | solution.py:331
  16.1 13.0 %collective-permute-start.1 = (bf16[1,2,128,512]{3,2,1,0:T(8,128)(2,1)S(1)}, bf16[1,2,128,512]{3,2,1,0:T(8,128)(2,1)S(1)}, u32[]{:S(2)}, u32[]{:S(2)}) collective-permute-start(bf16[1,2,128,512]{3,2,1,0:T(8,128)(2,1)S(1)} %get-tuple-element.32), channel_id=1, source_target_pairs={{8,0},{16,8},{24,16},{32,24},{40,32},{48,40},{56,48},{64,56},{72,6... | collective-permute-start | bytes 786440 | tf_op jit(solution)/shard_map/ppermute | solution.py:305
  17.4 11.7 %collective-permute-start = (bf16[1,2,128,512]{3,2,1,0:T(8,128)(2,1)S(1)}, bf16[1,2,128,512]{3,2,1,0:T(8,128)(2,1)S(1)}, u32[]{:S(2)}, u32[]{:S(2)}) collective-permute-start(bf16[1,2,128,512]{3,2,1,0:T(8,128)(2,1)S(1)} %get-tuple-element.33), channel_id=1, source_target_pairs={{0,8},{8,16},{16,24},{24,32},{32,40},{40,48},{48,56},{56,64},{64,7... | collective-permute-start | bytes 786440 | tf_op jit(solution)/shard_map/ppermute | solution.py:305
  30.1 22.1 %collective-permute-start.2 = (bf16[6,1,128,512]{3,2,1,0:T(8,128)(2,1)}, bf16[6,1,128,512]{3,2,1,0:T(8,128)(2,1)S(1)}, u32[]{:S(2)}, u32[]{:S(2)}) collective-permute-start(bf16[6,1,128,512]{3,2,1,0:T(8,128)(2,1)} %pad_maximum_fusion), channel_id=1, source_target_pairs={{0,1},{1,2},{2,3},{3,4},{4,5},{5,6},{6,7},{8,9},{9,10},{10,11},{11... | collective-permute-start | bytes 2359304 | tf_op jit(solution)/shard_map/ppermute | solution.py:336
  35.0 17.2 %collective-permute-start.3 = (bf16[6,1,128,512]{3,2,1,0:T(8,128)(2,1)}, bf16[6,1,128,512]{3,2,1,0:T(8,128)(2,1)S(1)}, u32[]{:S(2)}, u32[]{:S(2)}) collective-permute-start(bf16[6,1,128,512]{3,2,1,0:T(8,128)(2,1)} %pad_maximum_fusion.1), channel_id=1, source_target_pairs={{1,0},{2,1},{3,2},{4,3},{5,4},{6,5},{7,6},{9,8},{10,9},{11,10},{12... | collective-permute-start | bytes 2359304 | tf_op jit(solution)/shard_map/ppermute | solution.py:337
  41.3 43.2 %all-to-all-start.1 = ((f32[128,4,128]{2,1,0:T(4,128)}), f32[128,4,128]{2,1,0:T(4,128)S(1)}, u32[]{:S(2)}, u32[]{:S(2)}) async-start(f32[128,4,128]{2,1,0:T(4,128)} %get-tuple-element.25), calls=%async_computation.1 | async-start | bytes 524288 | tf_op jit(solution)/shard_map/all_to_all | solution.py:349

commit v7 on v6

--- a/solution.py
+++ b/solution.py
@@ -77,17 +77,27 @@
 
     @pl.when(step == 0)
     def _():
-        bring(whole, held, semaphores)
+        copies = [pltpu.make_async_copy(a, b, semaphores.at[n]) for n, (a, b) in enumerate(zip(whole, held))]
+        soon, sides = (4, 9, 10), (5, 6, 7, 8)
+        later = tuple(n for n in range(len(copies)) if n not in soon + sides)
+        for n in soon + sides + later:
+            copies[n].start()
+        for n in soon:
+            copies[n].wait()
         rows_x, rows_y = own.shape[0], own.shape[1]
         wide = rows_y + 2
         own_rows = own[...].reshape(-1, latent)
         project(own_rows, [(x + 1) * wide + y + 1 for x in range(rows_x) for y in range(rows_y)])
+        targets[...] = matmul(own_rows, first[2]).astype(jnp.bfloat16).reshape(targets.shape)
+        sums[...] = jnp.zeros_like(sums)
+        for n in sides:
+            copies[n].wait()
         project(up[...].reshape(-1, latent), [y + 1 for y in range(rows_y)])
         project(down[...].reshape(-1, latent), [(rows_x + 1) * wide + y + 1 for y in range(rows_y)])
         project(left[...].reshape(-1, latent), [x * wide for x in range(rows_x + 2)])
         project(right[...].reshape(-1, latent), [x * wide + wide - 1 for x in range(rows_x + 2)])
-        targets[...] = matmul(own_rows, first[2]).astype(jnp.bfloat16).reshape(targets.shape)
-        sums[...] = jnp.zeros_like(sums)
+        for n in later:
+            copies[n].wait()
         for b in range(SUB):
             gather(0, b, picked_a)
 

time: 90.6 us -> 90.6 us (level)
  no operation moved by 1% of the time
where the time goes in v7:
time: 90.6 us; the launch traced here: 90.1 us
  Pallas kernels  44.6 us (49%)
  starting transfers between devices  33.5 us (37%)
  waiting for transfers between devices  6.35 us (7%)
  local copies, waits for them, and re-layouts  2.41 us (3%)
  other arithmetic  1.95 us (2%)
  between operations  1.39 us (2%)
    pallas_call x1, Pallas kernels, edge_call(): pl.pallas_call(edge_kernel, grid=(steps,), in_specs=[pl.BlockSpec((per, b...  32.2 us
    pallas_call x3, Pallas kernels, call(): pl.pallas_call(run, out_shape=out_shape, in_specs=[pl.BlockSpec(memory_sp...  12.3 us
    all_to_all x1, starting transfers between devices, body(): rows_in = lax.all_to_all(rows_out, BOTH, 0, 0, tiled=True)  11.5 us
    all_to_all x1, starting transfers between devices, body(): from_owners = lax.all_to_all(answers, BOTH, 0, 0, tiled=True)  10.9 us
    ppermute x2, waiting for transfers between devices, exchanged(): return (lax.ppermute(last, axis, up), lax.ppermute(first, axis, down))  6.34 us
    ppermute x2, starting transfers between devices, exchanged(): return (lax.ppermute(last, axis, up), lax.ppermute(first, axis, down))  5.29 us
    ppermute x1, starting transfers between devices, body(): left = lax.ppermute(tall(rows_y - 1), 'gy', right_pairs)  3.88 us
    concatenate x2, other arithmetic, body(): jnp.concatenate([up[:, y:y + 1], fine_nodes[:, y:y + 1], down[:, y:y + 1]...  1.95 us
  transfers between devices with their start and end apart: 6, of which 1 were waited for; matrix products, arithmetic and copies ran while one was open for 4% of the time, Pallas kernels for 40%

profile of v7, /device:TPU:1, one launch (start us, length us, event | category | flops | bytes accessed | tf_op | source)
XLA Modules:
  0.0 90.1 jit_solution(13365599717128917633)
XLA Ops:
  0.6 2.9 %middle.1 = (bf16[128,512]{1,0:T(8,128)(2,1)S(1)}, f32[128,8,128]{2,1,0:T(8,128)}) custom-call(bf16[8,128,512]{2,1,0:T(8,128)(2,1)} %bitcast.20, s32[4,2,128]{2,1,0:T(2,128)} %refs_11_.1, f32[4,2,128]{2,1,0:T(2,128)} %refs_12_.1, bf16[128,512]{1,0:T(8,128)(2,1)} %bitcast.31, s32[1,128]{1,0:T(1,128)} %bitcast.25, f32[1,128]{1,0:T(1,128)} %bitcast.27), custom_call_target="tpu_custom_call" | custom-call | flops 1000000000 | bytes 9000000 | tf_op jit(solution)/shard_map/middle/pallas_call | solution.py:297
  3.6 11.5 %all-to-all-start = ((f32[128,8,128]{2,1,0:T(8,128)}), f32[128,8,128]{2,1,0:T(8,128)S(1)}, u32[]{:S(2)}, u32[]{:S(2)}) async-start(f32[128,8,128]{2,1,0:T(8,128)} %get-tuple-element.17), calls=%async_computation | async-start | bytes 1048576 | tf_op jit(solution)/shard_map/all_to_all | solution.py:341
  15.1 1.1 %fusion.1 = (bf16[1,2,128,512]{3,2,1,0:T(8,128)(2,1)S(1)}, bf16[1,2,128,512]{3,2,1,0:T(8,128)(2,1)S(1)}) fusion(bf16[4,2,128,512]{3,2,1,0:T(8,128)(2,1)} %rest_4_.1), kind=kLoop, calls=%fused_computation.3 | loop fusion | bytes 1048576 | tf_op jit(solution)/shard_map/slice | solution.py:314
  16.1 1.3 %collective-permute-start.1 = (bf16[1,2,128,512]{3,2,1,0:T(8,128)(2,1)S(1)}, bf16[1,2,128,512]{3,2,1,0:T(8,128)(2,1)S(1)}, u32[]{:S(2)}, u32[]{:S(2)}) collective-permute-start(bf16[1,2,128,512]{3,2,1,0:T(8,128)(2,1)S(1)} %get-tuple-element.32), channel_id=1, source_target_pairs={{8,0},{16,8},{24,16},{32,24},{40,32},{48,40},{56,48},{64,56},{72,6... | collective-permute-start | bytes 786440 | tf_op jit(solution)/shard_map/ppermute | solution.py:315
  17.4 4.0 %collective-permute-start = (bf16[1,2,128,512]{3,2,1,0:T(8,128)(2,1)S(1)}, bf16[1,2,128,512]{3,2,1,0:T(8,128)(2,1)S(1)}, u32[]{:S(2)}, u32[]{:S(2)}) collective-permute-start(bf16[1,2,128,512]{3,2,1,0:T(8,128)(2,1)S(1)} %get-tuple-element.33), channel_id=1, source_target_pairs={{0,8},{8,16},{16,24},{24,32},{32,40},{40,48},{48,56},{56,64},{64,7... | collective-permute-start | bytes 786440 | tf_op jit(solution)/shard_map/ppermute | solution.py:315
  21.5 1.3 %fusion = (bf16[4,1,128,512]{3,2,1,0:T(8,128)(2,1)S(1)}, bf16[4,1,128,512]{3,2,1,0:T(8,128)(2,1)S(1)}) fusion(bf16[4,2,128,512]{3,2,1,0:T(8,128)(2,1)} %rest_4_.1), kind=kLoop, calls=%fused_computation.2 | loop fusion | bytes 2097152 | tf_op jit(solution)/shard_map/slice | solution.py:343
  22.8 6.3 %collective-permute-done.1.rest_6_ = bf16[1,2,128,512]{3,2,1,0:T(8,128)(2,1)S(1)} collective-permute-done((bf16[1,2,128,512]{3,2,1,0:T(8,128)(2,1)S(1)}, bf16[1,2,128,512]{3,2,1,0:T(8,128)(2,1)S(1)}, u32[]{:S(2)}, u32[]{:S(2)}) %collective-permute-start.1) | collective-permute-done | bytes 262176 | tf_op jit(solution)/shard_map/ppermute | solution.py:315
  29.1 0.0 collective-permute-done.rest_5_
  29.1 0.0 all-to-all-done.refs_0_
  29.2 1.0 %pad_maximum_fusion = bf16[6,1,128,512]{3,2,1,0:T(8,128)(2,1)} fusion(bf16[1,1,128,512]{3,2,1,0:T(8,128)(2,1)S(1)} %get-tuple-element.38, bf16[4,1,128,512]{3,2,1,0:T(8,128)(2,1)S(1)} %get-tuple-element.31, bf16[1,1,128,512]{3,2,1,0:T(8,128)(2,1)S(1)} %get-tuple-element.35), kind=kLoop, calls=%fused_computation | loop fusion | flops 786432 | bytes 1572864 | tf_op jit(solution)/shard_map/concatenate | solution.py:343
  30.1 3.9 %collective-permute-start.2 = (bf16[6,1,128,512]{3,2,1,0:T(8,128)(2,1)}, bf16[6,1,128,512]{3,2,1,0:T(8,128)(2,1)S(1)}, u32[]{:S(2)}, u32[]{:S(2)}) collective-permute-start(bf16[6,1,128,512]{3,2,1,0:T(8,128)(2,1)} %pad_maximum_fusion), channel_id=1, source_target_pairs={{0,1},{1,2},{2,3},{3,4},{4,5},{5,6},{6,7},{8,9},{9,10},{10,11},{11... | collective-permute-start | bytes 2359304 | tf_op jit(solution)/shard_map/ppermute | solution.py:346
  34.0 1.0 %pad_maximum_fusion.1 = bf16[6,1,128,512]{3,2,1,0:T(8,128)(2,1)} fusion(bf16[1,1,128,512]{3,2,1,0:T(8,128)(2,1)S(1)} %get-tuple-element.39, bf16[4,1,128,512]{3,2,1,0:T(8,128)(2,1)S(1)} %get-tuple-element.30, bf16[1,1,128,512]{3,2,1,0:T(8,128)(2,1)S(1)} %get-tuple-element.34), kind=kLoop, calls=%fused_computation.1 | loop fusion | flops 786432 | bytes 1572864 | tf_op jit(solution)/shard_map/concatenate | solution.py:343
  35.0 1.9 %collective-permute-start.3 = (bf16[6,1,128,512]{3,2,1,0:T(8,128)(2,1)}, bf16[6,1,128,512]{3,2,1,0:T(8,128)(2,1)S(1)}, u32[]{:S(2)}, u32[]{:S(2)}) collective-permute-start(bf16[6,1,128,512]{3,2,1,0:T(8,128)(2,1)} %pad_maximum_fusion.1), channel_id=1, source_target_pairs={{1,0},{2,1},{3,2},{4,3},{5,4},{6,5},{7,6},{9,8},{10,9},{11,10},{12... | collective-permute-start | bytes 2359304 | tf_op jit(solution)/shard_map/ppermute | solution.py:347
  37.6 3.8 %coarse.1 = (bf16[8,512]{1,0:T(8,128)(2,1)}, f32[128,4,128]{2,1,0:T(4,128)}) custom-call(f32[128,8,128]{2,1,0:T(8,128)S(1)} %all-to-all-done.refs_0_, bf16[8,512]{1,0:T(8,128)(2,1)} %refs_1_.3, bf16[2,512,512]{2,1,0:T(8,128)(2,1)} %refs_2_.4, f32[1,512]{1,0:T(1,128)} %bitcast.35, bf16[512,512]{1,0:T(8,128)(2,1)} %refs_4_.2, f32[1,512]{1,0:T(1,128)} %bitcast.36, ...), custom_call_target="tpu_custom_call" | custom-call | flops 1000000000 | bytes 9000000 | tf_op jit(solution)/shard_map/coarse/pallas_call | solution.py:297
  41.3 10.9 %all-to-all-start.1 = ((f32[128,4,128]{2,1,0:T(4,128)}), f32[128,4,128]{2,1,0:T(4,128)S(1)}, u32[]{:S(2)}, u32[]{:S(2)}) async-start(f32[128,4,128]{2,1,0:T(4,128)} %get-tuple-element.25), calls=%async_computation.1 | async-start | bytes 524288 | tf_op jit(solution)/shard_map/all_to_all | solution.py:359
  52.2 0.0 collective-permute-done.2.rest_7_
  52.2 0.0 collective-permute-done.3.rest_8_
  52.2 32.2 %edges.1 = (bf16[64,128,512]{2,1,0:T(8,128)(2,1)}, bf16[8,128,512]{2,1,0:T(8,128)(2,1)S(1)}) custom-call(bf16[64,128,512]{2,1,0:T(8,128)(2,1)} %bitcast.29, s32[64,128]{1,0:T(8,128)} %bitcast.33, s32[1,64]{1,0:T(1,128)} %bitcast.41, s32[1,1]{1,0:T(1,128)S(6)} %copy.31.rest_2_, s32[64,128]{1,0:T(8,128)} %bitcast.34, bf16[4,2,128,512]{3,2,1,0:T(8,128)(2,1)} %rest_4_.1, ...), custom_call_target="tpu_custom_call" | custom-call | flops 20000000000 | bytes 100000000 | tf_op jit(solution)/shard_map/edges/pallas_call | solution.py:162
  84.5 0.0 all-to-all-done.1.refs_8_
  84.5 5.6 %final.1 = (bf16[8,128,512]{2,1,0:T(8,128)(2,1)}, bf16[128,512]{1,0:T(8,128)(2,1)}) custom-call(bf16[8,128,512]{2,1,0:T(8,128)(2,1)} %bitcast.21, bf16[8,128,512]{2,1,0:T(8,128)(2,1)S(1)} %get-tuple-element.23.refs_1_, bf16[2,512,512]{2,1,0:T(8,128)(2,1)} %refs_2_.5, f32[1,512]{1,0:T(1,128)} %bitcast.22, bf16[512,512]{1,0:T(8,128)(2,1)} %refs_4_.3, ...), custom_call_target="tpu_custom_call" | custom-call | flops 1000000000 | bytes 9000000 | tf_op jit(solution)/shard_map/final/pallas_call | solution.py:297
  (1 shorter events, 0.0 us)
Async XLA Ops:
  3.6 25.5 %all-to-all-start = ((f32[128,8,128]{2,1,0:T(8,128)}), f32[128,8,128]{2,1,0:T(8,128)S(1)}, u32[]{:S(2)}, u32[]{:S(2)}) async-start(f32[128,8,128]{2,1,0:T(8,128)} %get-tuple-element.17), calls=%async_computation | async-start | bytes 1048576 | tf_op jit(solution)/shard_map/all_to_all | solution.py:341
  16.1 13.0 %collective-permute-start.1 = (bf16[1,2,128,512]{3,2,1,0:T(8,128)(2,1)S(1)}, bf16[1,2,128,512]{3,2,1,0:T(8,128)(2,1)S(1)}, u32[]{:S(2)}, u32[]{:S(2)}) collective-permute-start(bf16[1,2,128,512]{3,2,1,0:T(8,128)(2,1)S(1)} %get-tuple-element.32), channel_id=1, source_target_pairs={{8,0},{16,8},{24,16},{32,24},{40,32},{48,40},{56,48},{64,56},{72,6... | collective-permute-start | bytes 786440 | tf_op jit(solution)/shard_map/ppermute | solution.py:315
  17.4 11.7 %collective-permute-start = (bf16[1,2,128,512]{3,2,1,0:T(8,128)(2,1)S(1)}, bf16[1,2,128,512]{3,2,1,0:T(8,128)(2,1)S(1)}, u32[]{:S(2)}, u32[]{:S(2)}) collective-permute-start(bf16[1,2,128,512]{3,2,1,0:T(8,128)(2,1)S(1)} %get-tuple-element.33), channel_id=1, source_target_pairs={{0,8},{8,16},{16,24},{24,32},{32,40},{40,48},{48,56},{56,64},{64,7... | collective-permute-start | bytes 786440 | tf_op jit(solution)/shard_map/ppermute | solution.py:315
  30.1 22.1 %collective-permute-start.2 = (bf16[6,1,128,512]{3,2,1,0:T(8,128)(2,1)}, bf16[6,1,128,512]{3,2,1,0:T(8,128)(2,1)S(1)}, u32[]{:S(2)}, u32[]{:S(2)}) collective-permute-start(bf16[6,1,128,512]{3,2,1,0:T(8,128)(2,1)} %pad_maximum_fusion), channel_id=1, source_target_pairs={{0,1},{1,2},{2,3},{3,4},{4,5},{5,6},{6,7},{8,9},{9,10},{10,11},{11... | collective-permute-start | bytes 2359304 | tf_op jit(solution)/shard_map/ppermute | solution.py:346
  35.0 17.2 %collective-permute-start.3 = (bf16[6,1,128,512]{3,2,1,0:T(8,128)(2,1)}, bf16[6,1,128,512]{3,2,1,0:T(8,128)(2,1)S(1)}, u32[]{:S(2)}, u32[]{:S(2)}) collective-permute-start(bf16[6,1,128,512]{3,2,1,0:T(8,128)(2,1)} %pad_maximum_fusion.1), channel_id=1, source_target_pairs={{1,0},{2,1},{3,2},{4,3},{5,4},{6,5},{7,6},{9,8},{10,9},{11,10},{12... | collective-permute-start | bytes 2359304 | tf_op jit(solution)/shard_map/ppermute | solution.py:347
  41.3 43.1 %all-to-all-start.1 = ((f32[128,4,128]{2,1,0:T(4,128)}), f32[128,4,128]{2,1,0:T(4,128)S(1)}, u32[]{:S(2)}, u32[]{:S(2)}) async-start(f32[128,4,128]{2,1,0:T(4,128)} %get-tuple-element.25), calls=%async_computation.1 | async-start | bytes 524288 | tf_op jit(solution)/shard_map/all_to_all | solution.py:359
